TPU v7x, 32 devices: a whole 2x2x4 slice. The times are simulated.
32 devices in a mesh: groups: 2 (over x), sky: 16 (over z, y, core).
Axes of the slice: x: 2, y: 2, z: 4, core: 2. Of those that a mesh axis runs over, the one named last changes fastest.
Arguments:
- image: bfloat16 [32, 512, 128], P(('groups', 'sky')), parts along dimension 0, may hold values from -6 to 6
- row_taps: bfloat16 [40, 31], replicated, may hold values from -1 to 1
- col_taps: bfloat16 [40, 31], replicated, may hold values from -1 to 1
- mix_coeff: float32 [32, 3, 40], P(('groups', 'sky')), parts along dimension 0, may hold values from -1 to 1
- shift_frac: float32 [32, 2], P(('groups', 'sky')), parts along dimension 0, may hold values from 0.05 to 0.95
- ccd_visit: int32 [32], P(('groups', 'sky')), parts along dimension 0, may hold values from 0 to 3
- visit_weight: bfloat16 [8], P('groups'), parts along dimension 0, may hold values from 0.25 to 4
- tile_block: int32 [2048], P(('groups', 'sky')), parts along dimension 0, may hold values from 0 to 255, as said below
- tile_offset: int32 [2048], P(('groups', 'sky')), parts along dimension 0, may hold values from 0 to 7
Outputs:
- coadd: float32 [4096, 128], P(('groups', 'sky')), parts along dimension 0
- weight_map: float32 [4096], P(('groups', 'sky')), parts along dimension 0
There are 2 independent parts, one for each index of `groups`. A program takes and returns all parts, laid end to end along the dimension named above; an argument that names none is the same for every part. Nothing has to cross between parts.
Inputs may be any that keep to these rules, and one draw needn't show every extreme that they name: `tile_block`: the owner of sky block b is device b // 16 of the sky axis. The 64 tiles of one window go to exactly 16 distinct owners, 4 tiles to each; at least four owners receive 4 tiles from every window.
All inputs are finite; a program needn't handle non-finite values.
Results may differ from a plain program's by a relative error of at most 0.0041.
Values may be sent and summed in bfloat16 or wider, within the bound.
No kernel may reach another device: no remote copies, remote signals or barrier semaphores. Data moves between devices by JAX's collectives and lax.ppermute only.
A program may use at most 64 MiB of HBM per device.

v0:
```python
import jax
import jax.numpy as jnp
from jax import lax
from jax.sharding import PartitionSpec as P

TILE_R = 8
TILES_DEV = 64
BLK_DEV = 16


def shifted(value, axis, steps):
    count = lax.axis_size(axis)
    leading, last = (max(0, -steps), min(count, count - steps))
    return lax.ppermute(value, axis, [(source, source + steps) for source in range(leading, last)])


def lanczos_taps(fraction):
    positions = jnp.arange(-2, 4).astype(jnp.float32)
    offsets = positions[None, :] - fraction[:, None]
    angles = jnp.pi * offsets
    kernel = jnp.sin(angles) / angles * (jnp.sin(angles / 3.0) / (angles / 3.0))
    return kernel / jnp.sum(kernel, axis=1, keepdims=True)


def banded(taps_group, out_count):
    group_size, tap_count = taps_group.shape
    in_count = out_count + tap_count - 1
    zero_fill = jnp.zeros((group_size, in_count + 1 - tap_count), taps_group.dtype)
    row_pattern = jnp.concatenate([taps_group, zero_fill], axis=1)
    repeated = jnp.tile(row_pattern, (1, out_count))[:, : out_count * in_count]
    return repeated.reshape(group_size, out_count, in_count)


def match_window(window, row_taps, col_taps, coefficients):
    win_rows, win_cols = window.shape
    basis_count, tap_count = row_taps.shape
    half_taps = tap_count // 2
    row_block = min(128, win_rows)
    row_blocks = win_rows // row_block
    padded = jnp.pad(window, ((0, 0), (half_taps, half_taps)))
    col_slabs = jnp.stack([padded], axis=1)
    column_pos = (2.0 * jnp.arange(win_cols).astype(jnp.float32) + 1.0) / win_cols - 1.0
    row_pos = (2.0 * jnp.arange(win_rows).astype(jnp.float32) + 1.0) / win_rows - 1.0

    def add_group(group_index, running):
        first_basis = group_index * 2
        row_group = lax.dynamic_slice_in_dim(row_taps, first_basis, 2, 0)
        col_group = lax.dynamic_slice_in_dim(col_taps, first_basis, 2, 0)
        coef_group = lax.dynamic_slice_in_dim(coefficients, first_basis, 2, 1)
        across = jnp.einsum(
            "rbs,kcs->krbc", col_slabs, banded(row_group, 128), preferred_element_type=jnp.float32
        )
        smoothed = across.reshape(2, win_rows, win_cols).astype(jnp.bfloat16)
        rows_padded = jnp.pad(smoothed, ((0, 0), (half_taps, half_taps), (0, 0)))
        row_slabs = jnp.stack(
            [
                rows_padded[
                    :, block_index * row_block : block_index * row_block + row_block + 2 * half_taps
                ]
                for block_index in range(row_blocks)
            ],
            axis=1,
        )
        vertical = jnp.einsum(
            "krs,kbsc->kbrc",
            banded(col_group, row_block),
            row_slabs,
            preferred_element_type=jnp.float32,
        )
        vertical = vertical.reshape(2, win_rows, win_cols)
        weights = (
            coef_group[0][:, None, None]
            + coef_group[1][:, None, None] * column_pos[None, None, :]
            + coef_group[2][:, None, None] * row_pos[None, :, None]
        )
        return running + jnp.sum(weights * vertical, axis=0)

    return lax.fori_loop(
        0, basis_count // 2, add_group, jnp.zeros((win_rows, win_cols), jnp.float32)
    )


def warp_window(matched, fraction):
    win_rows, win_cols = matched.shape
    taps_across = lanczos_taps(fraction[1:2])[0]
    taps_down = lanczos_taps(fraction[0:1])[0]
    padded = jnp.pad(matched, ((0, 0), (2, 3)))
    spread = taps_across[0] * padded[:, 0:win_cols]
    for offset_index in range(1, 6):
        spread = (
            spread + taps_across[offset_index] * padded[:, offset_index : offset_index + win_cols]
        )
    padded = jnp.pad(spread, ((2, 3), (0, 0)))
    warped = taps_down[0] * padded[0:win_rows]
    for offset_index in range(1, 6):
        warped = warped + taps_down[offset_index] * padded[offset_index : offset_index + win_rows]
    return warped.astype(jnp.bfloat16)


def pack_slots(selector, tile_rows):
    return jnp.dot(
        selector.astype(jnp.bfloat16), tile_rows, preferred_element_type=jnp.float32
    ).astype(jnp.bfloat16)


def on_device(
    image,
    row_taps,
    col_taps,
    mix_coeff,
    shift_frac,
    ccd_visit,
    visit_weight,
    tile_block,
    tile_offset,
):
    win_cols = image.shape[2]
    matched = match_window(image[0], row_taps, col_taps, mix_coeff[0])
    warped = warp_window(matched, shift_frac[0])
    tile_count = TILES_DEV
    blocks_owned = BLK_DEV
    owned_rows = BLK_DEV * TILE_R
    sky_count = lax.axis_size("sky")
    capacity = max(2, tile_count // sky_count)
    slot_count = sky_count * capacity
    tile_rows = warped.reshape(tile_count, TILE_R * win_cols)
    tile_owner = tile_block // blocks_owned
    tile_local = tile_block - tile_owner * blocks_owned
    earlier = jnp.arange(tile_count)[None, :] < jnp.arange(tile_count)[:, None]
    tile_rank = jnp.sum((tile_owner[None, :] == tile_owner[:, None]) & earlier, axis=1)
    slot_ids = jnp.arange(slot_count)[:, None]
    visit_match = ccd_visit[:, None] == jnp.arange(visit_weight.shape[0])[None, :]
    own_weight = jnp.sum(
        jnp.where(visit_match, visit_weight[None, :], jnp.zeros((), jnp.bfloat16)), axis=1
    )
    main_select = slot_ids == (tile_owner * capacity + tile_rank)[None, :]
    send_main = pack_slots(main_select, tile_rows)
    filled = jnp.any(main_select, axis=1)
    starts = jnp.sum(
        jnp.where(main_select, (tile_local * TILE_R + tile_offset)[None, :], 0), axis=1
    )
    weights = jnp.where(filled, own_weight[0], jnp.zeros((), jnp.bfloat16))
    received, got_start, got_weight = (
        lax.all_to_all(send_main, "sky", split_axis=0, concat_axis=0, tiled=True),
        lax.all_to_all(starts, "sky", split_axis=0, concat_axis=0, tiled=True),
        lax.all_to_all(weights, "sky", split_axis=0, concat_axis=0, tiled=True),
    )
    slot_weight = got_weight.astype(jnp.float32)
    target = (got_start[:, None] + jnp.arange(TILE_R)[None, :]).reshape(-1)
    column_weight = jnp.repeat(got_weight, TILE_R)
    row_ids = jnp.arange(owned_rows + TILE_R)
    placement = jnp.where(
        row_ids[:, None] == target[None, :], column_weight[None, :], jnp.zeros((), jnp.bfloat16)
    )
    row_sums = jnp.dot(
        placement, received.reshape(-1, win_cols), preferred_element_type=jnp.float32
    )
    distance = row_ids[:, None] - got_start[None, :]
    covered = (distance >= 0) & (distance < TILE_R)
    totals = jnp.sum(jnp.where(covered, slot_weight[None, :], 0.0), axis=1)
    row_sums, totals = (row_sums, totals)
    carried_sums, carried_totals = shifted((row_sums[owned_rows:], totals[owned_rows:]), "sky", 1)
    sky_sum = jnp.concatenate(
        [row_sums[:TILE_R] + carried_sums, row_sums[TILE_R:owned_rows]], axis=0
    )
    weight_map = jnp.concatenate(
        [totals[:TILE_R] + carried_totals, totals[TILE_R:owned_rows]], axis=0
    )
    coadd = sky_sum / jnp.maximum(weight_map, 1.0)[:, None]
    return (coadd, weight_map)


def solution(mesh):
    return jax.shard_map(
        on_device,
        mesh=mesh,
        in_specs=(
            P(("groups", "sky"), None, None),
            P(),
            P(),
            P(("groups", "sky"), None, None),
            P(("groups", "sky"), None),
            P(("groups", "sky")),
            P("groups"),
            P(("groups", "sky")),
            P(("groups", "sky")),
        ),
        out_specs=(P(("groups", "sky"), None), P(("groups", "sky"))),
        check_vma=False,
    )
```

profile of v0, /device:TPU:10, one launch (start us, length us, event | category | flops | bytes accessed | tf_op | source)
XLA Modules:
  0.0 120.9 jit_solution(13972909325291598700)
XLA Ops:
  0.6 0.7 multiply_add_fusion.2
  4.2 0.7 select_n.56
  4.9 6.4 %all-to-all-start.1 = ((bf16[16,4,1]{1,2,0:T(2,128)(2,1)}), bf16[16,4,1]{1,2,0:T(2,128)(2,1)S(1)}, u32[]{:S(2)}, u32[]{:S(2)}) async-start(bf16[16,4,1]{1,2,0:T(2,128)(2,1)} %select_n.56), calls=%async_computation.1 | async-start | bytes 16384 | tf_op jit(solution)/shard_map/all_to_all | solution.py:146
  11.3 0.7 copy-done.3
  12.1 1.0 copy.44
  13.9 61.1 %while.16 = (s32[]{:T(128)}, f32[512,128]{1,0:T(8,128)S(1)}, f32[3,40]{1,0:T(4,128)S(1)}, bf16[40,31]{1,0:T(8,128)(2,1)S(1)}, bf16[512,1,158]{0,2,1:T(8,128)(2,1...) while((s32[]{:T(128)}, f32[512,128]{1,0:T(8,128)S(1)}, ...), condition=%wide.region_8.9_spmd.clone, body=%wide.region_6.8_spmd.clone.sunk | while | flops 83917440 | bytes 4484617 | solution.py:78
  75.6 1.3 %fusion.40 = f32[]{:T(128)} fusion(f32[]{:T(128)} %bitcast.4), kind=kLoop, calls=%fused_computation.90 | loop fusion | flops 53 | bytes 8 | tf_op jit(solution)/shard_map/reduce_sum | solution.py:22
  76.9 1.3 %fusion.41 = f32[1,6]{1,0:T(1,128)S(1)} fusion(f32[]{:T(128)} %fusion.40, f32[]{:T(128)} %bitcast.4), kind=kLoop, calls=%fused_computation.91 | loop fusion | flops 54 | bytes 32 | tf_op jit(solution)/shard_map/div | solution.py:22
  78.8 1.3 %fusion.42 = f32[]{:T(128)} fusion(f32[]{:T(128)} %bitcast.2), kind=kLoop, calls=%fused_computation.92 | loop fusion | flops 53 | bytes 8 | tf_op jit(solution)/shard_map/reduce_sum | solution.py:22
  80.1 1.3 %fusion.43 = f32[1,6]{1,0:T(1,128)S(1)} fusion(f32[]{:T(128)} %fusion.42, f32[]{:T(128)} %bitcast.2), kind=kLoop, calls=%fused_computation.94 | loop fusion | flops 54 | bytes 32 | tf_op jit(solution)/shard_map/div | solution.py:22
  81.3 0.7 fusion.45
  82.0 4.1 %fusion.18 = f32[512,128]{1,0:T(8,128)S(1)} fusion(f32[512,128]{1,0:T(8,128)S(1)} %get-tuple-element.200, f32[]{:T(128)} %bitcast.12, f32[]{:T(128)} %bitcast.11, f32[]{:T(128)} %bitcast.10, f32[]{:T(128)} %bitcast.9, f32[]{:T(128)} %bitcast.8, f32[]{:T(128)} %bitcast.5), kind=kLoop, calls=%fused_computation.41 | loop fusion | flops 720896 | bytes 524312 | tf_op jit(solution)/shard_map/add | solution.py:91
  86.1 3.9 %add_convert_fusion = bf16[512,128]{1,0:T(8,128)(2,1)S(1)} fusion(f32[512,128]{1,0:T(8,128)S(1)} %fusion.18, f32[]{:T(128)} %bitcast.17, f32[]{:T(128)} %bitcast.16, f32[]{:T(128)} %bitcast.15, f32[]{:T(128)} %bitcast.14, f32[]{:T(128)} %bitcast.13, f32[]{:T(128)} %bitcast.3), kind=kLoop, calls=%fused_computation.46 | loop fusion | flops 786432 | bytes 393240 | tf_op jit(solution)/shard_map/convert_element_type | solution.py:97
  90.2 0.7 all_to_all.18
  90.9 6.0 %all-to-all-start = ((s32[16,4,1]{1,2,0:T(1,128)}), s32[16,4,1]{1,2,0:T(1,128)S(1)}, u32[]{:S(2)}, u32[]{:S(2)}) async-start(s32[16,4,1]{1,2,0:T(1,128)} %bitcast), calls=%async_computation | async-start | bytes 16384 | tf_op jit(solution)/shard_map/all_to_all | solution.py:145
  97.1 0.7 all_to_all.22
  98.1 3.7 %all-to-all-done = s32[16,4,1]{1,2,0:T(1,128)S(1)} async-done(((s32[16,4,1]{1,2,0:T(1,128)}), s32[16,4,1]{1,2,0:T(1,128)S(1)}, u32[]{:S(2)}, u32[]{:S(2)}) %all-to-all-start) | async-done | bytes 288 | tf_op jit(solution)/shard_map/all_to_all | solution.py:145
  101.9 4.8 %all-to-all-start.2 = ((bf16[16,4,1024]{2,1,0:T(4,128)(2,1)}), bf16[16,4,1024]{2,1,0:T(4,128)(2,1)S(1)}, u32[]{:S(2)}, u32[]{:S(2)}) async-start(bf16[16,4,1024]{2,1,0:T(4,128)(2,1)} %all_to_all.22), calls=%async_computation.2 | async-start | bytes 262144 | tf_op jit(solution)/shard_map/all_to_all | solution.py:144
  107.2 0.7 reduce.15
  108.3 2.1 %collective-permute-start.1 = (f32[8]{0:T(128)S(1)}, f32[8]{0:T(128)S(1)}, u32[]{:S(2)}, u32[]{:S(2)}) collective-permute-start(f32[8]{0:T(128)S(1)} %slice.226), channel_id=1, source_target_pairs={{0,1},{1,2},{2,3},{3,4},{4,5},{5,6},{6,7},{7,8},{8,9},{9,10},{10,1... | collective-permute-start | bytes 104 | tf_op jit(solution)/shard_map/ppermute | solution.py:14
  110.4 3.7 %collective-permute-done.1 = f32[8]{0:T(128)S(1)} collective-permute-done((f32[8]{0:T(128)S(1)}, f32[8]{0:T(128)S(1)}, u32[]{:S(2)}, u32[]{:S(2)}) %collective-permute-start.1) | collective-permute-done | bytes 64 | tf_op jit(solution)/shard_map/ppermute | solution.py:14
  114.4 1.9 %collective-permute-start = (f32[8,128]{1,0:T(8,128)S(1)}, f32[8,128]{1,0:T(8,128)S(1)}, u32[]{:S(2)}, u32[]{:S(2)}) collective-permute-start(f32[8,128]{1,0:T(8,128)S(1)} %slice.242), channel_id=1, source_target_pairs={{0,1},{1,2},{2,3},{3,4},{4,5},{5,6},{6,7},{7,8},{8,9},{9,10},{10,1... | collective-permute-start | bytes 12296 | tf_op jit(solution)/shard_map/ppermute | solution.py:14
  116.9 3.3 %collective-permute-done = f32[8,128]{1,0:T(8,128)S(1)} collective-permute-done((f32[8,128]{1,0:T(8,128)S(1)}, f32[8,128]{1,0:T(8,128)S(1)}, u32[]{:S(2)}, u32[]{:S(2)}) %collective-permute-start) | collective-permute-done | bytes 4128 | tf_op jit(solution)/shard_map/ppermute | solution.py:14
  120.2 0.7 maximum_divide_fusion
  (485 shorter events, 65.0 us)
Async XLA Ops:
  2.3 0.7 copy-start.4
  4.9 7.1 %copy-start = (bf16[40,31]{0,1:T(8,128)(2,1)S(1)}, bf16[40,31]{0,1:T(8,128)(2,1)}, u32[]{:S(2)}) copy-start(bf16[40,31]{0,1:T(8,128)(2,1)} %param.12) | copy-start | bytes 7444
  4.9 86.0 %all-to-all-start.1 = ((bf16[16,4,1]{1,2,0:T(2,128)(2,1)}), bf16[16,4,1]{1,2,0:T(2,128)(2,1)S(1)}, u32[]{:S(2)}, u32[]{:S(2)}) async-start(bf16[16,4,1]{1,2,0:T(2,128)(2,1)} %select_n.56), calls=%async_computation.1 | async-start | bytes 16384 | tf_op jit(solution)/shard_map/all_to_all | solution.py:146
  11.3 0.7 copy-start.3
  13.1 0.7 copy-start.1
  13.9 61.1 %copy-start.2 = (f32[1,2]{1,0:T(1,128)S(1)}, f32[1,2]{1,0:T(1,128)}, u32[]{:S(2)}) copy-start(f32[1,2]{1,0:T(1,128)} %param.15) | copy-start | bytes 28
  90.9 10.9 %all-to-all-start = ((s32[16,4,1]{1,2,0:T(1,128)}), s32[16,4,1]{1,2,0:T(1,128)S(1)}, u32[]{:S(2)}, u32[]{:S(2)}) async-start(s32[16,4,1]{1,2,0:T(1,128)} %bitcast), calls=%async_computation | async-start | bytes 16384 | tf_op jit(solution)/shard_map/all_to_all | solution.py:145
  101.9 12.2 %all-to-all-start.2 = ((bf16[16,4,1024]{2,1,0:T(4,128)(2,1)}), bf16[16,4,1024]{2,1,0:T(4,128)(2,1)S(1)}, u32[]{:S(2)}, u32[]{:S(2)}) async-start(bf16[16,4,1024]{2,1,0:T(4,128)(2,1)} %all_to_all.22), calls=%async_computation.2 | async-start | bytes 262144 | tf_op jit(solution)/shard_map/all_to_all | solution.py:144
  108.3 5.8 %collective-permute-start.1 = (f32[8]{0:T(128)S(1)}, f32[8]{0:T(128)S(1)}, u32[]{:S(2)}, u32[]{:S(2)}) collective-permute-start(f32[8]{0:T(128)S(1)} %slice.226), channel_id=1, source_target_pairs={{0,1},{1,2},{2,3},{3,4},{4,5},{5,6},{6,7},{7,8},{8,9},{9,10},{10,1... | collective-permute-start | bytes 104 | tf_op jit(solution)/shard_map/ppermute | solution.py:14
  114.4 5.8 %collective-permute-start = (f32[8,128]{1,0:T(8,128)S(1)}, f32[8,128]{1,0:T(8,128)S(1)}, u32[]{:S(2)}, u32[]{:S(2)}) collective-permute-start(f32[8,128]{1,0:T(8,128)S(1)} %slice.242), channel_id=1, source_target_pairs={{0,1},{1,2},{2,3},{3,4},{4,5},{5,6},{6,7},{7,8},{8,9},{9,10},{10,1... | collective-permute-start | bytes 12296 | tf_op jit(solution)/shard_map/ppermute | solution.py:14
where the time goes:
time: 122 us; the launch traced here: 121 us
  local copies, waits for them, and re-layouts  51.9 us (43%)
  other arithmetic  22 us (18%)
  starting transfers between devices  21.3 us (17%)
  matrix products  10.8 us (9%)
  waiting for transfers between devices  10.7 us (9%)
  loops' own time  2.8 us (2%)
  between operations  1.48 us (1%)
    another operation x80, local copies, waits for them, and re-layouts, banded(): repeated = jnp.tile(row_pattern, (1, out_count))[:, :out_count * in_count]  16.1 us
    reshape x40, local copies, waits for them, and re-layouts, banded(): return repeated.reshape(group_size, out_count, in_count)  15.9 us
    ppermute x2, waiting for transfers between devices, shifted(): lax.ppermute(value, axis, [(source, source + steps) for source in range(l...  7 us
    all_to_all x1, starting transfers between devices, on_device(): lax.all_to_all(weights, 'sky', split_axis=0, concat_axis=0, tiled=True)  6.43 us
    dot_general x20, matrix products, add_group(): jnp.einsum('krs,kbsc->kbrc', banded(col_group, row_block), row_slabs, pre...  6.25 us
    all_to_all x1, starting transfers between devices, on_device(): lax.all_to_all(starts, 'sky', split_axis=0, concat_axis=0, tiled=True)  6.02 us
    all_to_all x1, starting transfers between devices, on_device(): lax.all_to_all(send_main, 'sky', split_axis=0, concat_axis=0, tiled=True)  4.84 us
    another operation x20, local copies, waits for them, and re-layouts, add_group(): jnp.stack([rows_padded[:, block_index * row_block:block_index * row_block...  4.57 us
  transfers between devices with their start and end apart: 5, of which 3 were waited for; matrix products, arithmetic and copies ran while one was open for 64% of the time, Pallas kernels for 0%

commit v1 on v0

v1 whole, which is shorter than its diff:
```python
import functools

import jax
import jax.numpy as jnp
from jax import lax
from jax.experimental import pallas as pl
from jax.experimental.pallas import tpu as pltpu
from jax.sharding import PartitionSpec as P

BLK_DEV = 16
SUB = 8
TAIL = 16
EMPTY = -64
TAPS_DOWN = 6


def iota(shape, axis):
    return lax.broadcasted_iota(jnp.int32, shape, axis)


def weight_of(visit_ref, weight_ref):
    values = weight_ref[...].astype(jnp.float32)
    chosen = jnp.where(iota(values.shape, 1) == visit_ref[0], values, 0.0)
    return jnp.sum(chosen, axis=1, keepdims=True)


def assign_slots(capacity, block_ref, offset_ref, slot_of, starts, counts):
    tiles = slot_of.shape[0]
    owners = counts.shape[0]

    @pl.loop(0, owners)
    def _(owner):
        counts[owner] = 0

    if owners * capacity > tiles:

        @pl.loop(0, owners * capacity)
        def _(slot):
            starts[slot] = EMPTY

    def assign(tile, carry):
        block = block_ref[tile]
        owner = lax.div(block, BLK_DEV)
        rank = counts[owner]
        counts[owner] = rank + 1
        slot = owner * capacity + rank
        slot_of[tile] = slot
        starts[slot] = (block - owner * BLK_DEV) * SUB + offset_ref[tile]
        return carry

    lax.fori_loop(0, tiles, assign, 0, unroll=8)


def lanczos_rows(frac_ref, cols):
    row = iota((2 * SUB, cols), 0)
    tap = jnp.where(row < SUB, row, row - SUB)
    fraction = jnp.where(row < SUB, frac_ref[0, 1], frac_ref[0, 0])
    angles = jnp.pi * ((tap - 2).astype(jnp.float32) - fraction)
    third = angles / 3.0
    kernel = jnp.sin(angles) / angles * (jnp.sin(third) / third)
    kernel = jnp.where(tap < TAPS_DOWN, kernel, 0.0)
    across, down = kernel[:SUB], kernel[SUB:]
    across = across / jnp.sum(across, axis=0, keepdims=True)
    down = down / jnp.sum(down, axis=0, keepdims=True)
    return across, down


def combined_taps(row_ref, col_ref, mix_ref, base):
    basis, taps = row_ref.shape
    cols = base.shape[2]
    half = taps // 2
    s, l = iota((taps, cols), 0), iota((taps, cols), 1)
    turned = ((s + l == half) | (s + l == half + cols)).astype(jnp.float32).astype(jnp.bfloat16)
    moved = (l == s + 1).astype(jnp.float32).astype(jnp.bfloat16)
    across = jnp.dot(row_ref[...], turned, preferred_element_type=jnp.float32).astype(jnp.bfloat16)
    down = jnp.dot(col_ref[...], moved, preferred_element_type=jnp.float32)
    same = iota((basis, basis), 0) == iota((basis, basis), 1)
    over = functools.partial(
        lax.dot_general,
        dimension_numbers=(((0,), (0,)), ((), ())),
        preferred_element_type=jnp.float32,
    )
    found = []
    for term in range(3):
        coefficient = jnp.sum(
            jnp.where(same, mix_ref[0, term : term + 1, :], 0.0), axis=1, keepdims=True
        )
        scaled = down * coefficient
        high = scaled.astype(jnp.bfloat16)
        low = (scaled - high.astype(jnp.float32)).astype(jnp.bfloat16)
        found.append((over(high, across) + over(low, across))[: base.shape[1]])
    lane = iota(found[0].shape, 1)
    lane = jnp.where(lane < cols // 2, lane, lane - cols).astype(jnp.float32)
    base[0] = found[0] + (2.0 / cols) * lane * found[1]
    base[1] = found[1]
    base[2] = found[2]


def build_bands(base, band, half):
    cols = base.shape[2]
    fold = band.shape[0]
    blocks = cols // SUB
    sub = iota((SUB, cols), 0)
    lane = iota((SUB, cols), 1)
    first_u = (2.0 * sub.astype(jnp.float32) + 1.0) / cols - 1.0

    def spin(term, row):
        taps = jnp.broadcast_to(base[term, pl.ds(row, 1), :], (SUB, cols))
        return pltpu.roll(taps, 0, 1, stride=1, stride_axis=0)

    def keep(block, value):
        if block * SUB >= half and (block + 1) * SUB - 1 + half < cols:
            return value
        return jnp.where(jnp.abs(lane - sub - block * SUB) <= half, value, 0.0)

    @pl.loop(0, fold)
    def _(r):
        for part in range(2):
            row = r + fold * part
            slope = spin(1, row)
            level = spin(0, row) + first_u * slope
            rise = spin(2, row)
            for pair in range(blocks // 2):
                two = []
                for block in (2 * pair, 2 * pair + 1):
                    value = level + (2.0 * SUB * block / cols) * slope
                    value = keep(block, pltpu.roll(value, SUB * block, 1) if block else value)
                    other = keep(block, pltpu.roll(rise, SUB * block, 1) if block else rise)
                    two.append(jnp.concatenate([value, other], axis=1))
                first = part * cols + pair * 2 * SUB
                band[r, first : first + 2 * SUB, :] = jnp.concatenate(two, axis=0).astype(
                    jnp.bfloat16
                )


def window_kernel(
    capacity,
    image_ref,
    row_ref,
    col_ref,
    mix_ref,
    weight_ref,
    frac_ref,
    visit_ref,
    block_ref,
    offset_ref,
    out_ref,
    padded,
    base,
    band,
    total,
    spread,
    slots,
    slot_of,
    starts,
    counts,
):
    rows, cols = image_ref.shape[1:]
    half = row_ref.shape[1] // 2
    fold = band.shape[0]
    tiles = slot_of.shape[0]
    owners = out_ref.shape[0]
    data_rows = capacity * SUB
    owned = BLK_DEV * SUB

    assign_slots(capacity, block_ref, offset_ref, slot_of, starts, counts)
    across, down = lanczos_rows(frac_ref, cols)
    weight = weight_of(visit_ref, weight_ref)

    padded[:fold] = jnp.zeros((fold, cols), jnp.float32)
    padded[fold : fold + rows] = image_ref[0].astype(jnp.float32)
    padded[fold + rows :] = jnp.zeros((fold, cols), jnp.float32)
    combined_taps(row_ref, col_ref, mix_ref, base)
    build_bands(base, band, half)

    total[...] = jnp.zeros(total.shape, jnp.float32)

    @pl.loop(0, fold)
    def _(r):
        moved = padded[pl.ds(r, rows + fold), :].astype(jnp.bfloat16)
        pair = jnp.concatenate([moved[:rows], moved[fold:]], axis=1)
        total[...] += jnp.dot(pair, band[r], preferred_element_type=jnp.float32)

    lane = iota((1, cols), 1)
    taps_across = [
        jnp.where((lane + m - 2 >= 0) & (lane + m - 2 < cols), across[m : m + 1], 0.0)
        for m in range(TAPS_DOWN)
    ]
    spread[:SUB] = jnp.zeros((SUB, cols), jnp.float32)
    spread[SUB + rows :] = jnp.zeros((SUB, cols), jnp.float32)
    chunk = 64

    @pl.loop(0, rows // chunk)
    def _(index):
        first = pl.multiple_of(index * chunk, chunk)
        position = (2 * (iota((chunk, cols), 0) + first) + 1).astype(jnp.float32) / rows - 1.0
        both = total[pl.ds(first, chunk), :]
        matched = both[:, :cols] + position * both[:, cols:]
        result = taps_across[2] * matched
        for m in range(TAPS_DOWN):
            if m != 2:
                result = result + taps_across[m] * pltpu.roll(matched, (2 - m) % cols, 1)
        spread[pl.ds(first + SUB, chunk), :] = result

    if owners * capacity > tiles:
        slots[...] = jnp.zeros(slots.shape, jnp.float32)

    def warp(tile, carry):
        first = tile * SUB + SUB - 2
        result = down[0:1] * spread[pl.ds(first, SUB), :]
        for m in range(1, TAPS_DOWN):
            result = result + down[m : m + 1] * spread[pl.ds(first + m, SUB), :]
        slots[pl.ds(pl.multiple_of(slot_of[tile] * SUB, SUB), SUB), :] = result
        return carry

    lax.fori_loop(0, tiles, warp, 0, unroll=8)

    sub = iota((SUB, cols), 0)
    wide = iota((SUB, cols), 1)
    cap_bits = capacity.bit_length() - 1
    lane_row = wide & (SUB - 1)
    lane_slot = (wide >> 3) & (capacity - 1)
    spill_slot = wide & (capacity - 1)
    spill_row = wide >> cap_bits
    tile_weight = jnp.broadcast_to(weight, (SUB, cols))

    def message(owner, carry):
        previous = jnp.maximum(owner - 1, 0)
        first = owner * data_rows
        out_ref[owner, :data_rows, :] = slots[
            pl.ds(pl.multiple_of(first, data_rows), data_rows), :
        ].astype(jnp.bfloat16)
        spilled = jnp.zeros((SUB, cols), jnp.float32)
        over = jnp.zeros((SUB, cols), jnp.float32)
        target = jnp.zeros((SUB, cols), jnp.int32)
        for c in range(capacity):
            target = jnp.where(lane_slot == c, starts[owner * capacity + c] + lane_row, target)
            slot = previous * capacity + c
            start = starts[slot]
            past = jnp.where(owner > 0, start + SUB - owned, 0)
            tile = slots[pl.ds(pl.multiple_of(slot * SUB, SUB), SUB), :]
            tile = pltpu.roll(tile, start & (SUB - 1), 0)
            spilled = spilled + jnp.where(sub < past, tile, 0.0)
            over = jnp.where((spill_slot == c) & (spill_row < past), tile_weight, over)
        top = jnp.where(sub == SUB - 1, over, spilled * tile_weight)
        meta = jnp.where(sub == 0, target.astype(jnp.float32), tile_weight)
        out_ref[owner, data_rows:, :] = jnp.concatenate([top, meta], axis=0).astype(jnp.bfloat16)
        return carry

    lax.fori_loop(0, owners, message, 0, unroll=4)


def sky_kernel(capacity, got_ref, coadd_ref, map_ref):
    sources, message_rows, cols = got_ref.shape
    data_rows = capacity * SUB
    owned = coadd_ref.shape[0]
    per_chunk = cols // data_rows
    lane = iota((1, cols), 1)
    row = iota((owned, cols), 0)
    spilled = jnp.zeros((SUB, cols), jnp.float32)
    pieces = []
    for chunk in range(sources // per_chunk):
        target = jnp.zeros((1, cols), jnp.float32)
        weight = jnp.zeros((1, cols), jnp.float32)
        for k in range(per_chunk):
            tail = got_ref[chunk * per_chunk + k, data_rows:, :].astype(jnp.float32)
            spilled = spilled + tail[:SUB]
            here = (lane >= k * data_rows) & (lane < (k + 1) * data_rows)
            target = jnp.where(here, tail[SUB : SUB + 1], target)
            weight = jnp.where(here, tail[SUB + 1 : SUB + 2], weight)
        placed = jnp.where(row == target.astype(jnp.int32), weight, 0.0)
        pieces.append(placed.astype(jnp.bfloat16))
    placement = jnp.concatenate(pieces, axis=1)
    pixels = got_ref[:, :data_rows, :].reshape(sources * data_rows, cols)
    pixels = jnp.concatenate([pixels, jnp.ones(pixels.shape, jnp.bfloat16)], axis=1)
    sums = jnp.dot(placement, pixels, preferred_element_type=jnp.float32)
    sub = iota((SUB, cols), 0)
    wide = iota((SUB, cols), 1)
    last = sub == SUB - 1
    over = jnp.broadcast_to(spilled[SUB - 1 :], (SUB, cols))
    mine = ((wide >> (capacity.bit_length() - 1)) == sub) & ~last
    over = jnp.sum(jnp.where(mine, over, 0.0), axis=1, keepdims=True)
    rest = jnp.zeros((owned - SUB, cols), jnp.float32)
    pixel_sum = sums[:, :cols] + jnp.concatenate([jnp.where(last, 0.0, spilled), rest], axis=0)
    weight_sum = sums[:, cols:] + jnp.concatenate(
        [jnp.broadcast_to(over, (SUB, cols)), rest], axis=0
    )
    coadd_ref[...] = pixel_sum / jnp.maximum(weight_sum, 1.0)
    diagonal = jnp.where(row == iota((owned, cols), 1), weight_sum, 0.0)
    map_ref[...] = jnp.sum(diagonal, axis=0, keepdims=True)


def on_device(
    image,
    row_taps,
    col_taps,
    mix_coeff,
    shift_frac,
    ccd_visit,
    visit_weight,
    tile_block,
    tile_offset,
):
    rows, cols = image.shape[1:]
    tiles = tile_block.shape[0]
    sky = lax.axis_size("sky")
    capacity = max(2, tiles // sky)
    message_rows = capacity * SUB + TAIL
    fold = (row_taps.shape[1] + 1) // 2
    vmem = pl.BlockSpec(memory_space=pltpu.VMEM)
    smem = pl.BlockSpec(memory_space=pltpu.SMEM)
    messages = pl.pallas_call(
        functools.partial(window_kernel, capacity),
        out_shape=jax.ShapeDtypeStruct((sky, message_rows, cols), jnp.bfloat16),
        in_specs=[vmem] * 5 + [smem] * 4,
        out_specs=vmem,
        scratch_shapes=[
            pltpu.VMEM((rows + 2 * fold, cols), jnp.float32),
            pltpu.VMEM((3, 2 * fold, cols), jnp.float32),
            pltpu.VMEM((fold, 2 * cols, 2 * cols), jnp.bfloat16),
            pltpu.VMEM((rows, 2 * cols), jnp.float32),
            pltpu.VMEM((rows + 2 * SUB, cols), jnp.float32),
            pltpu.VMEM((sky * capacity * SUB, cols), jnp.float32),
            pltpu.SMEM((tiles,), jnp.int32),
            pltpu.SMEM((sky * capacity,), jnp.int32),
            pltpu.SMEM((sky,), jnp.int32),
        ],
        compiler_params=pltpu.CompilerParams(vmem_limit_bytes=32 * 1024 * 1024),
        name="match_warp_pack",
    )(
        image,
        row_taps,
        col_taps,
        mix_coeff,
        visit_weight.reshape(1, -1),
        shift_frac,
        ccd_visit,
        tile_block,
        tile_offset,
    )
    received = lax.all_to_all(messages, "sky", split_axis=0, concat_axis=0, tiled=True)
    coadd, weight_map = pl.pallas_call(
        functools.partial(sky_kernel, capacity),
        out_shape=(
            jax.ShapeDtypeStruct((BLK_DEV * SUB, cols), jnp.float32),
            jax.ShapeDtypeStruct((1, BLK_DEV * SUB), jnp.float32),
        ),
        in_specs=[vmem],
        out_specs=(vmem, vmem),
        compiler_params=pltpu.CompilerParams(vmem_limit_bytes=32 * 1024 * 1024),
        name="place_normalise",
    )(received)
    return coadd, weight_map.reshape(-1)


def solution(mesh):
    return jax.shard_map(
        on_device,
        mesh=mesh,
        in_specs=(
            P(("groups", "sky"), None, None),
            P(),
            P(),
            P(("groups", "sky"), None, None),
            P(("groups", "sky"), None),
            P(("groups", "sky")),
            P("groups"),
            P(("groups", "sky")),
            P(("groups", "sky")),
        ),
        out_specs=(P(("groups", "sky"), None), P(("groups", "sky"))),
        check_vma=False,
    )
```

time: 122 us -> 30.4 us (0.25)
  the two profiles are of different devices: /device:TPU:10 before, /device:TPU:0 now
where the time goes in v1:
time: 30.4 us; the launch traced here: 30.2 us
  blocking collectives  16.2 us (53%)
  Pallas kernels  10.1 us (33%)
  local copies, waits for them, and re-layouts  2.49 us (8%)
  between operations  1.35 us (4%)
    all_to_all x1, blocking collectives, on_device(): lax.all_to_all(messages, 'sky', split_axis=0, concat_axis=0, tiled=True)  16.2 us
    pallas_call x1, Pallas kernels, on_device(): pl.pallas_call(functools.partial(window_kernel, capacity), out_shape=jax....  9.31 us
    unnamed x17, local copies, waits for them, and re-layouts  2.49 us
    pallas_call x1, Pallas kernels, on_device(): pl.pallas_call(functools.partial(sky_kernel, capacity), out_shape=(jax.Sh...  0.83 us

profile of v1, /device:TPU:0, one launch (start us, length us, event | category | flops | bytes accessed | tf_op | source)
XLA Modules:
  0.0 30.2 jit_solution(17535408167732951452)
XLA Ops:
  0.6 0.0 copy-start.6
  1.3 0.0 copy-done.6
  1.3 0.0 copy-start.5
  1.3 0.8 %copy.11.row_ref = bf16[40,31]{1,0:T(8,128)(2,1)S(1)} copy(bf16[40,31]{0,1:T(8,128)(2,1)} %param.10) | data formatting | bytes 4960 | tf_op args[1]
  2.1 0.0 copy-done.5
  2.1 0.0 copy-start.4
  2.1 0.1 copy.12.col_ref
  2.2 0.0 copy-start.1
  2.2 0.0 copy-start.2
  2.2 0.0 copy-start.3
  2.3 0.5 %copy-done.4 = s32[64]{0:T(128)S(1)} copy-done((s32[64]{0:T(128)S(1)}, s32[64]{0:T(128)}, u32[]{:S(2)}) %copy-start.4) | copy-done | bytes 280
  2.8 0.1 copy-done.1
  2.9 0.0 copy-done.2
  2.9 0.0 copy-done.3
  2.9 0.0 copy-start
  2.9 0.9 %copy-done = bf16[1,512,128]{2,1,0:T(8,128)(2,1)S(1)} copy-done((bf16[1,512,128]{2,1,0:T(8,128)(2,1)S(1)}, bf16[1,512,128]{2,1,0:T(8,128)(2,1)}, u32[]{:S(2)}) %copy-start) | copy-done | bytes 131096
  3.8 9.3 %match_warp_pack.1 = bf16[16,48,128]{2,1,0:T(8,128)(2,1)S(1)} custom-call(bf16[1,512,128]{2,1,0:T(8,128)(2,1)S(1)} %copy-done, bf16[40,31]{1,0:T(8,128)(2,1)S(1)} %copy.11.row_ref, bf16[40,31]{1,0:T(8,128)(2,1)S(1)} %copy.12.col_ref, f32[1,3,40]{2,1,0:T(4,128)S(1)} %copy.13.mix_ref, bf16[1,4]{1,0:T(2,128)(2,1)S(1)} %bitcast.2, f32[1,2]{1,0:T(1,128)S(1)} %copy-done.2, ...), custom_call_target="tpu_custom_call" | custom-call | tf_op jit(solution)/shard_map/match_warp_pack/pallas_call | solution.py:312
  13.1 16.2 %all_to_all.5.got_ref = bf16[16,48,128]{2,1,0:T(8,128)(2,1)S(1)} all-to-all(bf16[16,48,128]{2,1,0:T(8,128)(2,1)S(1)} %match_warp_pack.1), channel_id=1, replica_groups=mesh['groups'=2,'sky'=16] {'sky'}, dimensions={0} | all-to-all | bytes 393216 | tf_op jit(solution)/shard_map/all_to_all | solution.py:341
  29.3 0.8 %place_normalise.1 = (f32[128,128]{1,0:T(8,128)}, f32[1,128]{1,0:T(1,128)}) custom-call(bf16[16,48,128]{2,1,0:T(8,128)(2,1)S(1)} %all_to_all.5.got_ref), custom_call_target="tpu_custom_call" | custom-call | tf_op jit(solution)/shard_map/place_normalise/pallas_call | solution.py:342
  (1 shorter events, 0.0 us)
Async XLA Ops:
  0.6 0.7 %copy-start.6 = (f32[1,3,40]{2,0,1:T(1,128)S(1)}, f32[1,3,40]{2,0,1:T(1,128)}, u32[]{:S(2)}) copy-start(f32[1,3,40]{2,0,1:T(1,128)} %param.12) | copy-start | bytes 1444
  1.3 0.8 %copy-start.5 = (bf16[40,31]{0,1:T(8,128)(2,1)S(1)}, bf16[40,31]{0,1:T(8,128)(2,1)}, u32[]{:S(2)}) copy-start(bf16[40,31]{0,1:T(8,128)(2,1)} %param.11) | copy-start | bytes 7444
  2.1 0.7 %copy-start.4 = (s32[64]{0:T(128)S(1)}, s32[64]{0:T(128)}, u32[]{:S(2)}) copy-start(s32[64]{0:T(128)} %offset_ref.1) | copy-start | bytes 772
  2.2 0.7 %copy-start.1 = (bf16[4]{0:T(256)(128)(2,1)S(1)}, bf16[4]{0:T(256)(128)(2,1)}, u32[]{:S(2)}) copy-start(bf16[4]{0:T(256)(128)(2,1)} %param.15) | copy-start | bytes 28
  2.2 0.7 %copy-start.2 = (f32[1,2]{1,0:T(1,128)S(1)}, f32[1,2]{1,0:T(1,128)}, u32[]{:S(2)}) copy-start(f32[1,2]{1,0:T(1,128)} %frac_ref.1) | copy-start | bytes 28
  2.2 0.7 %copy-start.3 = (s32[64]{0:T(128)S(1)}, s32[64]{0:T(128)}, u32[]{:S(2)}) copy-start(s32[64]{0:T(128)} %block_ref.1) | copy-start | bytes 772
  2.9 0.9 %copy-start = (bf16[1,512,128]{2,1,0:T(8,128)(2,1)S(1)}, bf16[1,512,128]{2,1,0:T(8,128)(2,1)}, u32[]{:S(2)}) copy-start(bf16[1,512,128]{2,1,0:T(8,128)(2,1)} %image_ref.1) | copy-start | bytes 393220

commit v2 on v1

v2 whole, which is shorter than its diff:
```python
import functools

import jax
import jax.numpy as jnp
from jax import lax
from jax.experimental import pallas as pl
from jax.experimental.pallas import tpu as pltpu
from jax.sharding import PartitionSpec as P

BLK_DEV = 16
SUB = 8
LARGE_VMEM = 56 * 1024 * 1024
SMALL_VMEM = 16 * 1024 * 1024
EMPTY = -64
TAPS_DOWN = 6


def iota(shape, axis):
    return lax.broadcasted_iota(jnp.int32, shape, axis)


def weight_of(visit_ref, weight_ref):
    values = weight_ref[...].astype(jnp.float32)
    chosen = jnp.where(iota(values.shape, 1) == visit_ref[0], values, 0.0)
    return jnp.sum(chosen, axis=1, keepdims=True)


def lanczos_rows(frac_ref, cols):
    row = iota((2 * SUB, cols), 0)
    tap = jnp.where(row < SUB, row, row - SUB)
    fraction = jnp.where(row < SUB, frac_ref[0, 1], frac_ref[0, 0])
    angles = jnp.pi * ((tap - 2).astype(jnp.float32) - fraction)
    third = angles / 3.0
    kernel = jnp.sin(angles) / angles * (jnp.sin(third) / third)
    kernel = jnp.where(tap < TAPS_DOWN, kernel, 0.0)
    across, down = kernel[:SUB], kernel[SUB:]
    across = across / jnp.sum(across, axis=0, keepdims=True)
    down = down / jnp.sum(down, axis=0, keepdims=True)
    return across, down


def combined_taps(row_ref, col_ref, mix_ref, lifted, base):
    taps, basis = row_ref.shape
    count, cols = base.shape[1:]
    half = taps // 2
    l, s = iota((cols, taps), 0), iota((cols, taps), 1)
    turned = ((s + l == half) | (s + l == half + cols)).astype(jnp.float32).astype(jnp.bfloat16)
    across = jnp.dot(turned, row_ref[...], preferred_element_type=jnp.float32)
    across = across.astype(jnp.bfloat16)
    lifted[0:1] = jnp.zeros((1, basis), jnp.float32)
    lifted[1:] = col_ref[...].astype(jnp.float32)
    down = lifted[...]
    scaled = jnp.concatenate([down * mix_ref[term] for term in range(3)], axis=0)
    high = scaled.astype(jnp.bfloat16)
    low = (scaled - high.astype(jnp.float32)).astype(jnp.bfloat16)
    found = lax.dot_general(
        jnp.concatenate([high, low], axis=0),
        across,
        (((1,), (1,)), ((), ())),
        preferred_element_type=jnp.float32,
    )
    found = found[: 3 * count] + found[3 * count :]
    lane = iota((count, cols), 1)
    lane = jnp.where(lane < cols // 2, lane, lane - cols).astype(jnp.float32)
    base[0] = found[:count] + (2.0 / cols) * lane * found[count : 2 * count]
    base[1] = found[count : 2 * count]
    base[2] = found[2 * count :]


def build_band(base, row, half, band, first):
    cols = base.shape[2]
    blocks = cols // SUB
    sub = iota((SUB, cols), 0)
    lane = iota((SUB, cols), 1)
    first_u = (2.0 * sub.astype(jnp.float32) + 1.0) / cols - 1.0

    def spin(term):
        taps = jnp.broadcast_to(base[term, pl.ds(row, 1), :], (SUB, cols))
        return pltpu.roll(taps, 0, 1, stride=1, stride_axis=0)

    def keep(block, value):
        if block * SUB >= half and (block + 1) * SUB - 1 + half < cols:
            return value
        return jnp.where(jnp.abs(lane - sub - block * SUB) <= half, value, 0.0)

    slope = spin(1)
    level = spin(0) + first_u * slope
    rise = spin(2)
    for pair in range(blocks // 2):
        two = []
        for block in (2 * pair, 2 * pair + 1):
            value = level + (2.0 * SUB * block / cols) * slope
            value = keep(block, pltpu.roll(value, SUB * block, 1) if block else value)
            other = keep(block, pltpu.roll(rise, SUB * block, 1) if block else rise)
            two.append(jnp.concatenate([value, other], axis=1))
        at = first + pair * 2 * SUB
        band[at : at + 2 * SUB, :] = jnp.concatenate(two, axis=0).astype(jnp.bfloat16)


def window_kernel(
    capacity,
    image_hbm,
    row_hbm,
    col_hbm,
    mix_hbm,
    weight_hbm,
    frac_hbm,
    visit_hbm,
    block_hbm,
    offset_hbm,
    out_ref,
    image_ref,
    row_ref,
    col_ref,
    mix_ref,
    weight_ref,
    frac_ref,
    visit_ref,
    block_ref,
    offset_ref,
    copied,
    padded,
    lifted,
    base,
    band_a,
    band_b,
    moved_a,
    moved_b,
    total,
    spread,
    slots,
    slot_of,
    starts,
    counts,
):
    rows, cols = image_ref.shape[1:]
    half = row_ref.shape[0] // 2
    fold = half + 1
    tiles = slot_of.shape[0]
    owners = out_ref.shape[0]
    data_rows = capacity * SUB
    owned = BLK_DEV * SUB

    pairs = (
        (row_hbm, row_ref),
        (col_hbm, col_ref),
        (mix_hbm, mix_ref),
        (image_hbm, image_ref),
        (frac_hbm, frac_ref),
        (visit_hbm, visit_ref),
        (weight_hbm, weight_ref),
        (block_hbm, block_ref),
        (offset_hbm, offset_ref),
    )
    copies = [
        pltpu.make_async_copy(source, target, copied.at[index])
        for index, (source, target) in enumerate(pairs)
    ]
    for copy in copies:
        copy.start()

    @pl.loop(0, owners)
    def _(owner):
        counts[owner] = 0

    if owners * capacity > tiles:
        slots[...] = jnp.zeros(slots.shape, jnp.float32)

        @pl.loop(0, owners * capacity)
        def _(slot):
            starts[slot] = EMPTY

    padded[:fold] = jnp.zeros((fold, cols), jnp.float32)
    padded[fold + rows :] = jnp.zeros((fold, cols), jnp.float32)
    spread[:SUB] = jnp.zeros((SUB, cols), jnp.float32)
    spread[SUB + rows :] = jnp.zeros((SUB, cols), jnp.float32)
    total[...] = jnp.zeros(total.shape, jnp.float32)
    for copy in copies:
        copy.wait()

    combined_taps(row_ref, col_ref, mix_ref, lifted, base)
    padded[fold : fold + rows] = image_ref[0].astype(jnp.float32)
    across, down = lanczos_rows(frac_ref, cols)
    weight = weight_of(visit_ref, weight_ref)

    per_group = moved_a.shape[0]
    steps = fold // (2 * per_group)

    def build(group, band, moved):
        for index in range(per_group):
            r = group * per_group + index
            for part in range(2):
                build_band(base, r + part * fold, half, band, (2 * index + part) * cols)
            moved[index] = padded[pl.ds(r, rows + fold), :].astype(jnp.bfloat16)

    def multiply(band, moved):
        parts = []
        for index in range(per_group):
            parts += [moved[index, :rows, :], moved[index, fold:, :]]
        total[...] += jnp.dot(
            jnp.concatenate(parts, axis=1), band[...], preferred_element_type=jnp.float32
        )

    def assign(tile):
        block = block_ref[tile]
        owner = lax.div(block, BLK_DEV)
        rank = counts[owner]
        counts[owner] = rank + 1
        slot = owner * capacity + rank
        slot_of[tile] = slot
        starts[slot] = (block - owner * BLK_DEV) * SUB + offset_ref[tile]

    build(0, band_a, moved_a)

    @pl.loop(0, steps)
    def _(step):
        build(2 * step + 1, band_b, moved_b)
        multiply(band_a, moved_a)
        build(lax.rem(2 * step + 2, 2 * steps), band_a, moved_a)
        multiply(band_b, moved_b)
        for index in range(tiles // steps):
            assign(step * (tiles // steps) + index)

    lane = iota((1, cols), 1)
    taps_across = [
        jnp.where((lane + m - 2 >= 0) & (lane + m - 2 < cols), across[m : m + 1], 0.0)
        for m in range(TAPS_DOWN)
    ]
    chunk = 64
    for index in range(rows // chunk):
        first = index * chunk
        position = (2 * (iota((chunk, cols), 0) + first) + 1).astype(jnp.float32) / rows - 1.0
        both = total[first : first + chunk, :]
        matched = both[:, :cols] + position * both[:, cols:]
        result = taps_across[2] * matched
        for m in range(TAPS_DOWN):
            if m != 2:
                result = result + taps_across[m] * pltpu.roll(matched, (2 - m) % cols, 1)
        spread[first + SUB : first + SUB + chunk, :] = result

    for tile in range(tiles):
        first = tile * SUB + SUB - 2
        result = down[0:1] * spread[first : first + SUB, :]
        for m in range(1, TAPS_DOWN):
            result = result + down[m : m + 1] * spread[first + m : first + m + SUB, :]
        slots[pl.ds(pl.multiple_of(slot_of[tile] * SUB, SUB), SUB), :] = result

    sub = iota((SUB, cols), 0)
    wide = iota((SUB, cols), 1)
    segment = wide >> (data_rows.bit_length() - 1)
    lane_row = wide & (SUB - 1)
    lane_slot = (wide >> 3) & (capacity - 1)
    spill_slot = wide & (capacity - 1)
    spill_row = wide >> (capacity.bit_length() - 1)
    tile_weight = jnp.broadcast_to(weight, (SUB, cols))

    def message(owner, carry):
        previous = jnp.maximum(owner - 1, 0)
        first = owner * data_rows
        out_ref[owner, :data_rows, :] = slots[
            pl.ds(pl.multiple_of(first, data_rows), data_rows), :
        ].astype(jnp.bfloat16)
        spilled = jnp.zeros((SUB, cols), jnp.float32)
        over = jnp.zeros((SUB, cols), jnp.float32)
        target = jnp.zeros((SUB, cols), jnp.int32)
        for c in range(capacity):
            target = jnp.where(lane_slot == c, starts[owner * capacity + c] + lane_row, target)
            slot = previous * capacity + c
            start = starts[slot]
            past = jnp.where(owner > 0, start + SUB - owned, 0)
            tile = slots[pl.ds(pl.multiple_of(slot * SUB, SUB), SUB), :]
            tile = pltpu.roll(tile, start & (SUB - 1), 0)
            spilled = spilled + jnp.where(sub < past, tile, 0.0)
            over = jnp.where((spill_slot == c) & (spill_row < past), tile_weight, over)
        meta = jnp.where(segment == 1, target.astype(jnp.float32), tile_weight)
        meta = jnp.where(segment == 0, over, meta)
        tail = jnp.where(sub == SUB - 1, meta, spilled * tile_weight)
        out_ref[owner, data_rows:, :] = tail.astype(jnp.bfloat16)
        return carry

    lax.fori_loop(0, owners, message, 0, unroll=min(owners, 16))


def sky_kernel(capacity, got_ref, coadd_ref, map_ref):
    sources, message_rows, cols = got_ref.shape
    data_rows = capacity * SUB
    owned = coadd_ref.shape[0]
    per_chunk = cols // data_rows
    chunks = sources // per_chunk
    place = iota((chunks, cols), 0)
    wide = iota((chunks, cols), 1)
    row = iota((owned, cols), 0)
    spilled = jnp.zeros((SUB, cols), jnp.float32)
    target = jnp.zeros((chunks, cols), jnp.float32)
    weight = jnp.zeros((chunks, cols), jnp.float32)
    for k in range(per_chunk):
        heads = jnp.zeros((chunks, cols), jnp.float32)
        for chunk in range(chunks):
            tail = got_ref[chunk * per_chunk + k, data_rows:, :].astype(jnp.float32)
            spilled = spilled + tail
            heads = jnp.where(place == chunk, tail[SUB - 1 :], heads)
        here = (wide >= k * data_rows) & (wide < (k + 1) * data_rows)
        target = jnp.where(here, pltpu.roll(heads, (k - 1) * data_rows % cols, 1), target)
        weight = jnp.where(here, pltpu.roll(heads, (k - 2) * data_rows % cols, 1), weight)
    target = target.astype(jnp.int32)
    pieces = [
        jnp.where(row == target[chunk : chunk + 1], weight[chunk : chunk + 1], 0.0)
        for chunk in range(chunks)
    ]
    placement = jnp.concatenate(pieces, axis=1).astype(jnp.bfloat16)
    pixels = got_ref[:, :data_rows, :].reshape(sources * data_rows, cols)
    pixels = jnp.concatenate([pixels, jnp.ones(pixels.shape, jnp.bfloat16)], axis=1)
    sums = jnp.dot(placement, pixels, preferred_element_type=jnp.float32)
    sub = iota((SUB, cols), 0)
    wide = iota((SUB, cols), 1)
    last = sub == SUB - 1
    over = jnp.broadcast_to(spilled[SUB - 1 :], (SUB, cols))
    mine = ((wide >> (capacity.bit_length() - 1)) == sub) & ~last
    over = jnp.sum(jnp.where(mine, over, 0.0), axis=1, keepdims=True)
    rest = jnp.zeros((owned - SUB, cols), jnp.float32)
    pixel_sum = sums[:, :cols] + jnp.concatenate([jnp.where(last, 0.0, spilled), rest], axis=0)
    weight_sum = sums[:, cols:] + jnp.concatenate(
        [jnp.broadcast_to(over, (SUB, cols)), rest], axis=0
    )
    coadd_ref[...] = pixel_sum / jnp.maximum(weight_sum, 1.0)
    diagonal = jnp.where(row == iota((owned, cols), 1), weight_sum, 0.0)
    map_ref[...] = jnp.sum(diagonal, axis=0, keepdims=True)


def on_device(
    image,
    row_taps,
    col_taps,
    mix_coeff,
    shift_frac,
    ccd_visit,
    visit_weight,
    tile_block,
    tile_offset,
):
    rows, cols = image.shape[1:]
    tiles = tile_block.shape[0]
    sky = lax.axis_size("sky")
    capacity = max(2, tiles // sky)
    taps, basis = row_taps.shape[1], row_taps.shape[0]
    fold = taps // 2 + 1
    visits = visit_weight.shape[0]
    per_group = 2
    anywhere = pl.BlockSpec(memory_space=pl.ANY)
    vmem = pl.BlockSpec(memory_space=pltpu.VMEM)
    messages = pl.pallas_call(
        functools.partial(window_kernel, capacity),
        out_shape=jax.ShapeDtypeStruct((sky, capacity * SUB + SUB, cols), jnp.bfloat16),
        in_specs=[anywhere] * 9,
        out_specs=vmem,
        scratch_shapes=[
            pltpu.VMEM((1, rows, cols), jnp.bfloat16),
            pltpu.VMEM((taps, basis), jnp.bfloat16),
            pltpu.VMEM((taps, basis), jnp.bfloat16),
            pltpu.VMEM((3, 1, basis), jnp.float32),
            pltpu.VMEM((1, visits), jnp.bfloat16),
            pltpu.SMEM((1, 2), jnp.float32),
            pltpu.SMEM((1,), jnp.int32),
            pltpu.SMEM((tiles,), jnp.int32),
            pltpu.SMEM((tiles,), jnp.int32),
            pltpu.SemaphoreType.DMA((9,)),
            pltpu.VMEM((rows + 2 * fold, cols), jnp.float32),
            pltpu.VMEM((2 * fold, basis), jnp.float32),
            pltpu.VMEM((3, 2 * fold, cols), jnp.float32),
            pltpu.VMEM((per_group * 2 * cols, 2 * cols), jnp.bfloat16),
            pltpu.VMEM((per_group * 2 * cols, 2 * cols), jnp.bfloat16),
            pltpu.VMEM((per_group, rows + fold, cols), jnp.bfloat16),
            pltpu.VMEM((per_group, rows + fold, cols), jnp.bfloat16),
            pltpu.VMEM((rows, 2 * cols), jnp.float32),
            pltpu.VMEM((rows + 2 * SUB, cols), jnp.float32),
            pltpu.VMEM((sky * capacity * SUB, cols), jnp.float32),
            pltpu.SMEM((tiles,), jnp.int32),
            pltpu.SMEM((sky * capacity,), jnp.int32),
            pltpu.SMEM((sky,), jnp.int32),
        ],
        compiler_params=pltpu.CompilerParams(vmem_limit_bytes=LARGE_VMEM),
        name="match_warp_pack",
    )(
        image,
        row_taps.T,
        col_taps.T,
        mix_coeff.transpose(1, 0, 2),
        visit_weight.reshape(1, -1),
        shift_frac,
        ccd_visit,
        tile_block,
        tile_offset,
    )
    received = lax.all_to_all(messages, "sky", split_axis=0, concat_axis=0, tiled=True)
    coadd, weight_map = pl.pallas_call(
        functools.partial(sky_kernel, capacity),
        out_shape=(
            jax.ShapeDtypeStruct((BLK_DEV * SUB, cols), jnp.float32),
            jax.ShapeDtypeStruct((1, BLK_DEV * SUB), jnp.float32),
        ),
        in_specs=[vmem],
        out_specs=(vmem, vmem),
        compiler_params=pltpu.CompilerParams(vmem_limit_bytes=SMALL_VMEM),
        name="place_normalise",
    )(received)
    return coadd, weight_map.reshape(-1)


def solution(mesh):
    return jax.shard_map(
        on_device,
        mesh=mesh,
        in_specs=(
            P(("groups", "sky"), None, None),
            P(),
            P(),
            P(("groups", "sky"), None, None),
            P(("groups", "sky"), None),
            P(("groups", "sky")),
            P("groups"),
            P(("groups", "sky")),
            P(("groups", "sky")),
        ),
        out_specs=(P(("groups", "sky"), None), P(("groups", "sky"))),
        check_vma=False,
    )
```

time: 30.4 us -> 23.7 us (0.78)
  Pallas kernels: 10.1 us -> 6.19 us
  local copies, waits for them, and re-layouts: 2.49 us -> 0 us
    pallas_call x1, Pallas kernels: 9.31 us -> 5.32 us  [on_device(): pl.pallas_call(functools.partial(window_kernel, capacity), out_shape=jax....]
    unnamed x17 -> x0, local copies, waits for them, and re-layouts: 2.49 us -> none
    all_to_all x1, blocking collectives: 16.2 us -> 15.9 us  [on_device(): lax.all_to_all(messages, 'sky', split_axis=0, concat_axis=0, tiled=True)]
where the time goes in v2:
time: 23.7 us; the launch traced here: 23.3 us
  blocking collectives  15.9 us (67%)
  Pallas kernels  6.19 us (26%)
  between operations  1.29 us (5%)
    all_to_all x1, blocking collectives, on_device(): lax.all_to_all(messages, 'sky', split_axis=0, concat_axis=0, tiled=True)  15.9 us
    pallas_call x1, Pallas kernels, on_device(): pl.pallas_call(functools.partial(window_kernel, capacity), out_shape=jax....  5.32 us
    pallas_call x1, Pallas kernels, on_device(): pl.pallas_call(functools.partial(sky_kernel, capacity), out_shape=(jax.Sh...  0.88 us

profile of v2, /device:TPU:0, one launch (start us, length us, event | category | flops | bytes accessed | tf_op | source)
XLA Modules:
  0.0 23.3 jit_solution(6119395789297579011)
XLA Ops:
  1.3 5.3 %match_warp_pack.1 = bf16[16,40,128]{2,1,0:T(8,128)(2,1)} custom-call(bf16[1,512,128]{2,1,0:T(8,128)(2,1)} %image_hbm.1, bf16[31,40]{1,0:T(8,128)(2,1)} %bitcast.5, bf16[31,40]{1,0:T(8,128)(2,1)} %bitcast.6, f32[3,1,40]{2,1,0:T(1,128)} %bitcast.7, bf16[1,4]{1,0:T(2,128)(2,1)} %bitcast.8, f32[1,2]{1,0:T(1,128)} %frac_hbm.1, s32[1]{0:T(128)S(6)} %copy.11.visit_hbm, ...), custom_call_target="tpu_custom_call" | custom-call | tf_op jit(solution)/shard_map/match_warp_pack/pallas_call | solution.py:351
  6.6 15.9 %all_to_all.5.got_ref = bf16[16,40,128]{2,1,0:T(8,128)(2,1)S(1)} all-to-all(bf16[16,40,128]{2,1,0:T(8,128)(2,1)} %match_warp_pack.1), channel_id=1, replica_groups=mesh['groups'=2,'sky'=16] {'sky'}, dimensions={0} | all-to-all | bytes 327680 | tf_op jit(solution)/shard_map/all_to_all | solution.py:394
  22.5 0.9 %place_normalise.1 = (f32[128,128]{1,0:T(8,128)}, f32[1,128]{1,0:T(1,128)}) custom-call(bf16[16,40,128]{2,1,0:T(8,128)(2,1)S(1)} %all_to_all.5.got_ref), custom_call_target="tpu_custom_call" | custom-call | tf_op jit(solution)/shard_map/place_normalise/pallas_call | solution.py:395

commit v3 on v2

--- a/solution.py
+++ b/solution.py
@@ -9,7 +9,7 @@
 
 BLK_DEV = 16
 SUB = 8
-LARGE_VMEM = 56 * 1024 * 1024
+LARGE_VMEM = 32 * 1024 * 1024
 SMALL_VMEM = 16 * 1024 * 1024
 EMPTY = -64
 TAPS_DOWN = 6
@@ -105,9 +105,9 @@
     mix_hbm,
     weight_hbm,
     frac_hbm,
-    visit_hbm,
     block_hbm,
     offset_hbm,
+    visit_ref,
     out_ref,
     image_ref,
     row_ref,
@@ -115,7 +115,6 @@
     mix_ref,
     weight_ref,
     frac_ref,
-    visit_ref,
     block_ref,
     offset_ref,
     copied,
@@ -147,7 +146,6 @@
         (mix_hbm, mix_ref),
         (image_hbm, image_ref),
         (frac_hbm, frac_ref),
-        (visit_hbm, visit_ref),
         (weight_hbm, weight_ref),
         (block_hbm, block_ref),
         (offset_hbm, offset_ref),
@@ -350,8 +348,8 @@
     vmem = pl.BlockSpec(memory_space=pltpu.VMEM)
     messages = pl.pallas_call(
         functools.partial(window_kernel, capacity),
-        out_shape=jax.ShapeDtypeStruct((sky, capacity * SUB + SUB, cols), jnp.bfloat16),
-        in_specs=[anywhere] * 9,
+        out_shape=pltpu.VMEM((sky, capacity * SUB + SUB, cols), jnp.bfloat16),
+        in_specs=[anywhere] * 8 + [pl.BlockSpec(memory_space=pltpu.SMEM)],
         out_specs=vmem,
         scratch_shapes=[
             pltpu.VMEM((1, rows, cols), jnp.bfloat16),
@@ -360,10 +358,9 @@
             pltpu.VMEM((3, 1, basis), jnp.float32),
             pltpu.VMEM((1, visits), jnp.bfloat16),
             pltpu.SMEM((1, 2), jnp.float32),
-            pltpu.SMEM((1,), jnp.int32),
             pltpu.SMEM((tiles,), jnp.int32),
             pltpu.SMEM((tiles,), jnp.int32),
-            pltpu.SemaphoreType.DMA((9,)),
+            pltpu.SemaphoreType.DMA((8,)),
             pltpu.VMEM((rows + 2 * fold, cols), jnp.float32),
             pltpu.VMEM((2 * fold, basis), jnp.float32),
             pltpu.VMEM((3, 2 * fold, cols), jnp.float32),
@@ -381,15 +378,20 @@
         compiler_params=pltpu.CompilerParams(vmem_limit_bytes=LARGE_VMEM),
         name="match_warp_pack",
     )(
-        image,
-        row_taps.T,
-        col_taps.T,
-        mix_coeff.transpose(1, 0, 2),
-        visit_weight.reshape(1, -1),
-        shift_frac,
+        *[
+            pltpu.with_memory_space_constraint(value, pltpu.HBM)
+            for value in (
+                image,
+                row_taps.T,
+                col_taps.T,
+                mix_coeff.transpose(1, 0, 2),
+                visit_weight.reshape(1, -1),
+                shift_frac,
+                tile_block,
+                tile_offset,
+            )
+        ],
         ccd_visit,
-        tile_block,
-        tile_offset,
     )
     received = lax.all_to_all(messages, "sky", split_axis=0, concat_axis=0, tiled=True)
     coadd, weight_map = pl.pallas_call(

time: 23.7 us -> 22.8 us (0.962)
  Pallas kernels: 6.19 us -> 5.57 us
  blocking collectives: 15.9 us -> 15.6 us
    pallas_call x1, Pallas kernels: 5.32 us -> 4.7 us  [on_device(): pl.pallas_call(functools.partial(window_kernel, capacity), out_shape=pltp...]
where the time goes in v3:
time: 22.8 us; the launch traced here: 22.5 us
  blocking collectives  15.6 us (68%)
  Pallas kernels  5.57 us (24%)
  between operations  1.29 us (6%)
    all_to_all x1, blocking collectives, on_device(): lax.all_to_all(messages, 'sky', split_axis=0, concat_axis=0, tiled=True)  15.6 us
    pallas_call x1, Pallas kernels, on_device(): pl.pallas_call(functools.partial(window_kernel, capacity), out_shape=pltp...  4.7 us
    pallas_call x1, Pallas kernels, on_device(): pl.pallas_call(functools.partial(sky_kernel, capacity), out_shape=(jax.Sh...  0.88 us

profile of v3, /device:TPU:0, one launch (start us, length us, event | category | flops | bytes accessed | tf_op | source)
XLA Modules:
  0.0 22.5 jit_solution(14170408081766544621)
XLA Ops:
  1.3 4.7 %match_warp_pack.1 = bf16[16,40,128]{2,1,0:T(8,128)(2,1)S(1)} custom-call(bf16[1,512,128]{2,1,0:T(8,128)(2,1)} %image_hbm.1, bf16[31,40]{1,0:T(8,128)(2,1)} %bitcast.5, bf16[31,40]{1,0:T(8,128)(2,1)} %bitcast.6, f32[3,1,40]{2,1,0:T(1,128)} %bitcast.7, bf16[1,4]{1,0:T(2,128)(2,1)} %bitcast.8, f32[1,2]{1,0:T(1,128)} %frac_hbm.1, s32[64]{0:T(128)} %block_hbm.1, ...), custom_call_target="tpu_custom_call" | custom-call | tf_op jit(solution)/shard_map/match_warp_pack/pallas_call | solution.py:349
  6.0 15.6 %all_to_all.5.got_ref = bf16[16,40,128]{2,1,0:T(8,128)(2,1)S(1)} all-to-all(bf16[16,40,128]{2,1,0:T(8,128)(2,1)S(1)} %match_warp_pack.1), channel_id=1, replica_groups=mesh['groups'=2,'sky'=16] {'sky'}, dimensions={0} | all-to-all | bytes 327680 | tf_op jit(solution)/shard_map/all_to_all | solution.py:396
  21.6 0.9 %place_normalise.1 = (f32[128,128]{1,0:T(8,128)}, f32[1,128]{1,0:T(1,128)}) custom-call(bf16[16,40,128]{2,1,0:T(8,128)(2,1)S(1)} %all_to_all.5.got_ref), custom_call_target="tpu_custom_call" | custom-call | tf_op jit(solution)/shard_map/place_normalise/pallas_call | solution.py:397

commit v4 on v3

--- a/solution.py
+++ b/solution.py
@@ -127,7 +127,7 @@
     moved_b,
     total,
     spread,
-    slots,
+    sky,
     slot_of,
     starts,
     counts,
@@ -137,7 +137,6 @@
     fold = half + 1
     tiles = slot_of.shape[0]
     owners = out_ref.shape[0]
-    data_rows = capacity * SUB
     owned = BLK_DEV * SUB
 
     pairs = (
@@ -162,7 +161,6 @@
         counts[owner] = 0
 
     if owners * capacity > tiles:
-        slots[...] = jnp.zeros(slots.shape, jnp.float32)
 
         @pl.loop(0, owners * capacity)
         def _(slot):
@@ -205,7 +203,7 @@
         rank = counts[owner]
         counts[owner] = rank + 1
         slot = owner * capacity + rank
-        slot_of[tile] = slot
+        slot_of[tile] = block * SUB + offset_ref[tile]
         starts[slot] = (block - owner * BLK_DEV) * SUB + offset_ref[tile]
 
     build(0, band_a, moved_a)
@@ -236,93 +234,41 @@
                 result = result + taps_across[m] * pltpu.roll(matched, (2 - m) % cols, 1)
         spread[first + SUB : first + SUB + chunk, :] = result
 
+    sky[...] = jnp.zeros(sky.shape, jnp.float32)
     for tile in range(tiles):
         first = tile * SUB + SUB - 2
         result = down[0:1] * spread[first : first + SUB, :]
         for m in range(1, TAPS_DOWN):
             result = result + down[m : m + 1] * spread[first + m : first + m + SUB, :]
-        slots[pl.ds(pl.multiple_of(slot_of[tile] * SUB, SUB), SUB), :] = result
-
-    sub = iota((SUB, cols), 0)
+        result = result.astype(jnp.bfloat16).astype(jnp.float32) * weight
+        lands = pl.ds(slot_of[tile], SUB)
+        sky[lands, :] = sky[lands, :] + result
+
     wide = iota((SUB, cols), 1)
-    segment = wide >> (data_rows.bit_length() - 1)
-    lane_row = wide & (SUB - 1)
-    lane_slot = (wide >> 3) & (capacity - 1)
-    spill_slot = wide & (capacity - 1)
-    spill_row = wide >> (capacity.bit_length() - 1)
     tile_weight = jnp.broadcast_to(weight, (SUB, cols))
 
     def message(owner, carry):
-        previous = jnp.maximum(owner - 1, 0)
-        first = owner * data_rows
-        out_ref[owner, :data_rows, :] = slots[
-            pl.ds(pl.multiple_of(first, data_rows), data_rows), :
-        ].astype(jnp.bfloat16)
-        spilled = jnp.zeros((SUB, cols), jnp.float32)
-        over = jnp.zeros((SUB, cols), jnp.float32)
-        target = jnp.zeros((SUB, cols), jnp.int32)
+        first = pl.multiple_of(owner * owned, owned)
+        out_ref[owner, :owned, :] = sky[pl.ds(first, owned), :]
+        found = jnp.zeros((SUB, cols), jnp.float32)
         for c in range(capacity):
-            target = jnp.where(lane_slot == c, starts[owner * capacity + c] + lane_row, target)
-            slot = previous * capacity + c
-            start = starts[slot]
-            past = jnp.where(owner > 0, start + SUB - owned, 0)
-            tile = slots[pl.ds(pl.multiple_of(slot * SUB, SUB), SUB), :]
-            tile = pltpu.roll(tile, start & (SUB - 1), 0)
-            spilled = spilled + jnp.where(sub < past, tile, 0.0)
-            over = jnp.where((spill_slot == c) & (spill_row < past), tile_weight, over)
-        meta = jnp.where(segment == 1, target.astype(jnp.float32), tile_weight)
-        meta = jnp.where(segment == 0, over, meta)
-        tail = jnp.where(sub == SUB - 1, meta, spilled * tile_weight)
-        out_ref[owner, data_rows:, :] = tail.astype(jnp.bfloat16)
+            start = starts[owner * capacity + c]
+            found = found + jnp.where((wide >= start) & (wide < start + SUB), tile_weight, 0.0)
+            start = starts[jnp.maximum(owner - 1, 0) * capacity + c] - owned
+            start = jnp.where(owner > 0, start, EMPTY)
+            found = found + jnp.where((wide >= start) & (wide < start + SUB), tile_weight, 0.0)
+        out_ref[owner, owned:, :] = found
         return carry
 
     lax.fori_loop(0, owners, message, 0, unroll=min(owners, 16))
 
 
-def sky_kernel(capacity, got_ref, coadd_ref, map_ref):
-    sources, message_rows, cols = got_ref.shape
-    data_rows = capacity * SUB
-    owned = coadd_ref.shape[0]
-    per_chunk = cols // data_rows
-    chunks = sources // per_chunk
-    place = iota((chunks, cols), 0)
-    wide = iota((chunks, cols), 1)
-    row = iota((owned, cols), 0)
-    spilled = jnp.zeros((SUB, cols), jnp.float32)
-    target = jnp.zeros((chunks, cols), jnp.float32)
-    weight = jnp.zeros((chunks, cols), jnp.float32)
-    for k in range(per_chunk):
-        heads = jnp.zeros((chunks, cols), jnp.float32)
-        for chunk in range(chunks):
-            tail = got_ref[chunk * per_chunk + k, data_rows:, :].astype(jnp.float32)
-            spilled = spilled + tail
-            heads = jnp.where(place == chunk, tail[SUB - 1 :], heads)
-        here = (wide >= k * data_rows) & (wide < (k + 1) * data_rows)
-        target = jnp.where(here, pltpu.roll(heads, (k - 1) * data_rows % cols, 1), target)
-        weight = jnp.where(here, pltpu.roll(heads, (k - 2) * data_rows % cols, 1), weight)
-    target = target.astype(jnp.int32)
-    pieces = [
-        jnp.where(row == target[chunk : chunk + 1], weight[chunk : chunk + 1], 0.0)
-        for chunk in range(chunks)
-    ]
-    placement = jnp.concatenate(pieces, axis=1).astype(jnp.bfloat16)
-    pixels = got_ref[:, :data_rows, :].reshape(sources * data_rows, cols)
-    pixels = jnp.concatenate([pixels, jnp.ones(pixels.shape, jnp.bfloat16)], axis=1)
-    sums = jnp.dot(placement, pixels, preferred_element_type=jnp.float32)
-    sub = iota((SUB, cols), 0)
-    wide = iota((SUB, cols), 1)
-    last = sub == SUB - 1
-    over = jnp.broadcast_to(spilled[SUB - 1 :], (SUB, cols))
-    mine = ((wide >> (capacity.bit_length() - 1)) == sub) & ~last
-    over = jnp.sum(jnp.where(mine, over, 0.0), axis=1, keepdims=True)
-    rest = jnp.zeros((owned - SUB, cols), jnp.float32)
-    pixel_sum = sums[:, :cols] + jnp.concatenate([jnp.where(last, 0.0, spilled), rest], axis=0)
-    weight_sum = sums[:, cols:] + jnp.concatenate(
-        [jnp.broadcast_to(over, (SUB, cols)), rest], axis=0
-    )
-    coadd_ref[...] = pixel_sum / jnp.maximum(weight_sum, 1.0)
-    diagonal = jnp.where(row == iota((owned, cols), 1), weight_sum, 0.0)
-    map_ref[...] = jnp.sum(diagonal, axis=0, keepdims=True)
+def sky_kernel(got_ref, coadd_ref, map_ref):
+    owned, cols = coadd_ref.shape
+    weights = got_ref[0, owned : owned + 1, :]
+    column = jnp.transpose(jnp.broadcast_to(weights, (owned, cols)))
+    coadd_ref[...] = got_ref[0, :owned, :] / jnp.maximum(column, 1.0)
+    map_ref[...] = weights
 
 
 def on_device(
@@ -348,7 +294,7 @@
     vmem = pl.BlockSpec(memory_space=pltpu.VMEM)
     messages = pl.pallas_call(
         functools.partial(window_kernel, capacity),
-        out_shape=pltpu.VMEM((sky, capacity * SUB + SUB, cols), jnp.bfloat16),
+        out_shape=jax.ShapeDtypeStruct((sky, BLK_DEV * SUB + SUB, cols), jnp.float32),
         in_specs=[anywhere] * 8 + [pl.BlockSpec(memory_space=pltpu.SMEM)],
         out_specs=vmem,
         scratch_shapes=[
@@ -370,7 +316,7 @@
             pltpu.VMEM((per_group, rows + fold, cols), jnp.bfloat16),
             pltpu.VMEM((rows, 2 * cols), jnp.float32),
             pltpu.VMEM((rows + 2 * SUB, cols), jnp.float32),
-            pltpu.VMEM((sky * capacity * SUB, cols), jnp.float32),
+            pltpu.VMEM((sky * BLK_DEV * SUB + SUB, cols), jnp.float32),
             pltpu.SMEM((tiles,), jnp.int32),
             pltpu.SMEM((sky * capacity,), jnp.int32),
             pltpu.SMEM((sky,), jnp.int32),
@@ -393,9 +339,9 @@
         ],
         ccd_visit,
     )
-    received = lax.all_to_all(messages, "sky", split_axis=0, concat_axis=0, tiled=True)
+    received = lax.psum_scatter(messages, "sky", scatter_dimension=0, tiled=True)
     coadd, weight_map = pl.pallas_call(
-        functools.partial(sky_kernel, capacity),
+        sky_kernel,
         out_shape=(
             jax.ShapeDtypeStruct((BLK_DEV * SUB, cols), jnp.float32),
             jax.ShapeDtypeStruct((1, BLK_DEV * SUB), jnp.float32),

time: 22.8 us -> 82 us (3.60)
  waiting for transfers between devices: 0 us -> 59.6 us
  blocking collectives: 15.6 us -> 0 us
  between operations: 1.29 us -> 14.7 us
  Pallas kernels: 5.57 us -> 6.51 us
  local copies, waits for them, and re-layouts: 0 us -> 0.88 us
    unnamed x0 -> x2, waiting for transfers between devices: none -> 59.6 us
    all_to_all x1 -> x0, blocking collectives: 15.6 us -> none  [on_device(): lax.all_to_all(messages, 'sky', split_axis=0, concat_axis=0, tiled=True)]
    pallas_call x2, Pallas kernels: 5.57 us -> 6.51 us  [the longest x1 5.77 us: on_device(): pl.pallas_call(functools.partial(window_kernel, capacity), out_shape=jax....]
    unnamed x0 -> x2, local copies, waits for them, and re-layouts: none -> 0.88 us
  transfers between devices with their start and end apart: 0 -> 1, of which waited for: 0 -> 1; matrix products, arithmetic and copies ran while one was open for 0% -> 0% of each run, Pallas kernels for 0% -> 0%
where the time goes in v4:
time: 82 us; the launch traced here: 81.8 us
  waiting for transfers between devices  59.6 us (73%)
  between operations  14.7 us (18%)
  Pallas kernels  6.51 us (8%)
  local copies, waits for them, and re-layouts  0.88 us (1%)
    unnamed x2, waiting for transfers between devices  59.6 us
    pallas_call x1, Pallas kernels, on_device(): pl.pallas_call(functools.partial(window_kernel, capacity), out_shape=jax....  5.77 us
  transfers between devices with their start and end apart: 1, of which 1 were waited for; matrix products, arithmetic and copies ran while one was open for 0% of the time, Pallas kernels for 0%

profile of v4, /device:TPU:0, one launch (start us, length us, event | category | flops | bytes accessed | tf_op | source)
XLA Modules:
  0.0 81.8 jit_solution(8829611352214160424)
XLA Ops:
  7.2 0.0 reduce-scatter.4.cloned.1.call-start
  7.9 5.8 %match_warp_pack.1 = f32[16,136,128]{2,1,0:T(8,128)} custom-call(bf16[1,512,128]{2,1,0:T(8,128)(2,1)} %image_hbm.1, bf16[31,40]{1,0:T(8,128)(2,1)} %bitcast.6, bf16[31,40]{1,0:T(8,128)(2,1)} %bitcast.7, f32[3,1,40]{2,1,0:T(1,128)} %bitcast.8, bf16[1,4]{1,0:T(2,128)(2,1)} %bitcast.9, f32[1,2]{1,0:T(1,128)} %frac_hbm.1, s32[64]{0:T(128)} %block_hbm.1, ...), custom_call_target="tpu_custom_call" | custom-call | tf_op jit(solution)/shard_map/match_warp_pack/pallas_call | solution.py:295
  13.6 0.0 reduce-scatter.4.cloned.1.call-update
  13.7 59.6 %reduce-scatter.4.cloned.1.call-done.got_ref = f32[1,136,128]{2,1,0:T(8,128)} async-done(((f32[16,136,128]{2,1,0:T(8,128)}), f32[1,136,128]{2,1,0:T(8,128)}) %reduce-scatter.4.cloned.1.call-update) | async-done | bytes 69648
  73.3 0.0 copy-start
  73.3 0.9 %copy-done = f32[1,136,128]{2,1,0:T(8,128)S(1)} copy-done((f32[1,136,128]{2,1,0:T(8,128)S(1)}, f32[1,136,128]{2,1,0:T(8,128)}, u32[]{:S(2)}) %copy-start) | copy-done | bytes 69656
  74.2 0.7 place_normalise.1
Async XLA Ops:
  7.2 66.1 %reduce-scatter.4.cloned.1.call-start = ((), (), s32[]{:S(2)}) async-start(), calls=%async_computation.1 | async-start | bytes 1183744
  73.3 0.9 %copy-start = (f32[1,136,128]{2,1,0:T(8,128)S(1)}, f32[1,136,128]{2,1,0:T(8,128)}, u32[]{:S(2)}) copy-start(f32[1,136,128]{2,1,0:T(8,128)} %reduce-scatter.4.cloned.1.call-done.got_ref) | copy-start | bytes 208900
Sparse Core Ops, SparseCore 0:
  13.8 59.4 reduce-scatter.3

commit v5 on v3

--- a/solution.py
+++ b/solution.py
@@ -343,7 +343,7 @@
     taps, basis = row_taps.shape[1], row_taps.shape[0]
     fold = taps // 2 + 1
     visits = visit_weight.shape[0]
-    per_group = 2
+    per_group = 4
     anywhere = pl.BlockSpec(memory_space=pl.ANY)
     vmem = pl.BlockSpec(memory_space=pltpu.VMEM)
     messages = pl.pallas_call(

time: 22.8 us -> 23.1 us (1.013)
  Pallas kernels: 5.57 us -> 5.87 us
    pallas_call x1, Pallas kernels: 4.7 us -> 4.99 us  [on_device(): pl.pallas_call(functools.partial(window_kernel, capacity), out_shape=pltp...]
where the time goes in v5:
time: 23.1 us; the launch traced here: 22.8 us
  blocking collectives  15.6 us (68%)
  Pallas kernels  5.87 us (25%)
  between operations  1.29 us (6%)
    all_to_all x1, blocking collectives, on_device(): lax.all_to_all(messages, 'sky', split_axis=0, concat_axis=0, tiled=True)  15.6 us
    pallas_call x1, Pallas kernels, on_device(): pl.pallas_call(functools.partial(window_kernel, capacity), out_shape=pltp...  4.99 us
    pallas_call x1, Pallas kernels, on_device(): pl.pallas_call(functools.partial(sky_kernel, capacity), out_shape=(jax.Sh...  0.88 us

profile of v5, /device:TPU:0, one launch (start us, length us, event | category | flops | bytes accessed | tf_op | source)
XLA Modules:
  0.0 22.8 jit_solution(14615080845203999664)
XLA Ops:
  1.3 5.0 %match_warp_pack.1 = bf16[16,40,128]{2,1,0:T(8,128)(2,1)S(1)} custom-call(bf16[1,512,128]{2,1,0:T(8,128)(2,1)} %image_hbm.1, bf16[31,40]{1,0:T(8,128)(2,1)} %bitcast.5, bf16[31,40]{1,0:T(8,128)(2,1)} %bitcast.6, f32[3,1,40]{2,1,0:T(1,128)} %bitcast.7, bf16[1,4]{1,0:T(2,128)(2,1)} %bitcast.8, f32[1,2]{1,0:T(1,128)} %frac_hbm.1, s32[64]{0:T(128)} %block_hbm.1, ...), custom_call_target="tpu_custom_call" | custom-call | tf_op jit(solution)/shard_map/match_warp_pack/pallas_call | solution.py:349
  6.3 15.6 %all_to_all.5.got_ref = bf16[16,40,128]{2,1,0:T(8,128)(2,1)S(1)} all-to-all(bf16[16,40,128]{2,1,0:T(8,128)(2,1)S(1)} %match_warp_pack.1), channel_id=1, replica_groups=mesh['groups'=2,'sky'=16] {'sky'}, dimensions={0} | all-to-all | bytes 327680 | tf_op jit(solution)/shard_map/all_to_all | solution.py:396
  21.9 0.9 %place_normalise.1 = (f32[128,128]{1,0:T(8,128)}, f32[1,128]{1,0:T(1,128)}) custom-call(bf16[16,40,128]{2,1,0:T(8,128)(2,1)S(1)} %all_to_all.5.got_ref), custom_call_target="tpu_custom_call" | custom-call | tf_op jit(solution)/shard_map/place_normalise/pallas_call | solution.py:397

commit v6 on v5

--- a/solution.py
+++ b/solution.py
@@ -343,7 +343,7 @@
     taps, basis = row_taps.shape[1], row_taps.shape[0]
     fold = taps // 2 + 1
     visits = visit_weight.shape[0]
-    per_group = 4
+    per_group = 1
     anywhere = pl.BlockSpec(memory_space=pl.ANY)
     vmem = pl.BlockSpec(memory_space=pltpu.VMEM)
     messages = pl.pallas_call(

time: 23.1 us -> 23.8 us (1.030)
  Pallas kernels: 5.87 us -> 6.61 us
    pallas_call x1, Pallas kernels: 4.99 us -> 5.73 us  [on_device(): pl.pallas_call(functools.partial(window_kernel, capacity), out_shape=pltp...]
where the time goes in v6:
time: 23.8 us; the launch traced here: 23.5 us
  blocking collectives  15.6 us (66%)
  Pallas kernels  6.61 us (28%)
  between operations  1.29 us (5%)
    all_to_all x1, blocking collectives, on_device(): lax.all_to_all(messages, 'sky', split_axis=0, concat_axis=0, tiled=True)  15.6 us
    pallas_call x1, Pallas kernels, on_device(): pl.pallas_call(functools.partial(window_kernel, capacity), out_shape=pltp...  5.73 us
    pallas_call x1, Pallas kernels, on_device(): pl.pallas_call(functools.partial(sky_kernel, capacity), out_shape=(jax.Sh...  0.88 us

profile of v6, /device:TPU:0, one launch (start us, length us, event | category | flops | bytes accessed | tf_op | source)
XLA Modules:
  0.0 23.5 jit_solution(5288196571035535570)
XLA Ops:
  1.3 5.7 %match_warp_pack.1 = bf16[16,40,128]{2,1,0:T(8,128)(2,1)S(1)} custom-call(bf16[1,512,128]{2,1,0:T(8,128)(2,1)} %image_hbm.1, bf16[31,40]{1,0:T(8,128)(2,1)} %bitcast.5, bf16[31,40]{1,0:T(8,128)(2,1)} %bitcast.6, f32[3,1,40]{2,1,0:T(1,128)} %bitcast.7, bf16[1,4]{1,0:T(2,128)(2,1)} %bitcast.8, f32[1,2]{1,0:T(1,128)} %frac_hbm.1, s32[64]{0:T(128)} %block_hbm.1, ...), custom_call_target="tpu_custom_call" | custom-call | tf_op jit(solution)/shard_map/match_warp_pack/pallas_call | solution.py:349
  7.0 15.6 %all_to_all.5.got_ref = bf16[16,40,128]{2,1,0:T(8,128)(2,1)S(1)} all-to-all(bf16[16,40,128]{2,1,0:T(8,128)(2,1)S(1)} %match_warp_pack.1), channel_id=1, replica_groups=mesh['groups'=2,'sky'=16] {'sky'}, dimensions={0} | all-to-all | bytes 327680 | tf_op jit(solution)/shard_map/all_to_all | solution.py:396
  22.7 0.9 %place_normalise.1 = (f32[128,128]{1,0:T(8,128)}, f32[1,128]{1,0:T(1,128)}) custom-call(bf16[16,40,128]{2,1,0:T(8,128)(2,1)S(1)} %all_to_all.5.got_ref), custom_call_target="tpu_custom_call" | custom-call | tf_op jit(solution)/shard_map/place_normalise/pallas_call | solution.py:397

commit v7 on v5

--- a/solution.py
+++ b/solution.py
@@ -172,7 +172,6 @@
     padded[fold + rows :] = jnp.zeros((fold, cols), jnp.float32)
     spread[:SUB] = jnp.zeros((SUB, cols), jnp.float32)
     spread[SUB + rows :] = jnp.zeros((SUB, cols), jnp.float32)
-    total[...] = jnp.zeros(total.shape, jnp.float32)
     for copy in copies:
         copy.wait()
 
@@ -182,7 +181,7 @@
     weight = weight_of(visit_ref, weight_ref)
 
     per_group = moved_a.shape[0]
-    steps = fold // (2 * per_group)
+    groups = fold // per_group
 
     def build(group, band, moved):
         for index in range(per_group):
@@ -191,13 +190,14 @@
                 build_band(base, r + part * fold, half, band, (2 * index + part) * cols)
             moved[index] = padded[pl.ds(r, rows + fold), :].astype(jnp.bfloat16)
 
-    def multiply(band, moved):
+    def multiply(group, band, moved):
         parts = []
         for index in range(per_group):
             parts += [moved[index, :rows, :], moved[index, fold:, :]]
-        total[...] += jnp.dot(
+        product = jnp.dot(
             jnp.concatenate(parts, axis=1), band[...], preferred_element_type=jnp.float32
         )
+        total[...] = product if group == 0 else total[...] + product
 
     def assign(tile):
         block = block_ref[tile]
@@ -208,16 +208,14 @@
         slot_of[tile] = slot
         starts[slot] = (block - owner * BLK_DEV) * SUB + offset_ref[tile]
 
-    build(0, band_a, moved_a)
-
-    @pl.loop(0, steps)
-    def _(step):
-        build(2 * step + 1, band_b, moved_b)
-        multiply(band_a, moved_a)
-        build(lax.rem(2 * step + 2, 2 * steps), band_a, moved_a)
-        multiply(band_b, moved_b)
-        for index in range(tiles // steps):
-            assign(step * (tiles // steps) + index)
+    held = ((band_a, moved_a), (band_b, moved_b))
+    build(0, *held[0])
+    for group in range(groups):
+        if group + 1 < groups:
+            build(group + 1, *held[(group + 1) % 2])
+        multiply(group, *held[group % 2])
+        for tile in range(group * tiles // groups, (group + 1) * tiles // groups):
+            assign(tile)
 
     lane = iota((1, cols), 1)
     taps_across = [

time: 23.1 us -> 22.3 us (0.965)
  Pallas kernels: 5.87 us -> 5.14 us
    pallas_call x1, Pallas kernels: 4.99 us -> 4.27 us  [on_device(): pl.pallas_call(functools.partial(window_kernel, capacity), out_shape=pltp...]
where the time goes in v7:
time: 22.3 us; the launch traced here: 22.1 us
  blocking collectives  15.6 us (70%)
  Pallas kernels  5.14 us (23%)
  between operations  1.29 us (6%)
    all_to_all x1, blocking collectives, on_device(): lax.all_to_all(messages, 'sky', split_axis=0, concat_axis=0, tiled=True)  15.6 us
    pallas_call x1, Pallas kernels, on_device(): pl.pallas_call(functools.partial(window_kernel, capacity), out_shape=pltp...  4.27 us
    pallas_call x1, Pallas kernels, on_device(): pl.pallas_call(functools.partial(sky_kernel, capacity), out_shape=(jax.Sh...  0.88 us

profile of v7, /device:TPU:0, one launch (start us, length us, event | category | flops | bytes accessed | tf_op | source)
XLA Modules:
  0.0 22.1 jit_solution(5898035505854677418)
XLA Ops:
  1.3 4.3 %match_warp_pack.1 = bf16[16,40,128]{2,1,0:T(8,128)(2,1)S(1)} custom-call(bf16[1,512,128]{2,1,0:T(8,128)(2,1)} %image_hbm.1, bf16[31,40]{1,0:T(8,128)(2,1)} %bitcast.5, bf16[31,40]{1,0:T(8,128)(2,1)} %bitcast.6, f32[3,1,40]{2,1,0:T(1,128)} %bitcast.7, bf16[1,4]{1,0:T(2,128)(2,1)} %bitcast.8, f32[1,2]{1,0:T(1,128)} %frac_hbm.1, s32[64]{0:T(128)} %block_hbm.1, ...), custom_call_target="tpu_custom_call" | custom-call | tf_op jit(solution)/shard_map/match_warp_pack/pallas_call | solution.py:347
  5.6 15.6 %all_to_all.5.got_ref = bf16[16,40,128]{2,1,0:T(8,128)(2,1)S(1)} all-to-all(bf16[16,40,128]{2,1,0:T(8,128)(2,1)S(1)} %match_warp_pack.1), channel_id=1, replica_groups=mesh['groups'=2,'sky'=16] {'sky'}, dimensions={0} | all-to-all | bytes 327680 | tf_op jit(solution)/shard_map/all_to_all | solution.py:394
  21.2 0.9 %place_normalise.1 = (f32[128,128]{1,0:T(8,128)}, f32[1,128]{1,0:T(1,128)}) custom-call(bf16[16,40,128]{2,1,0:T(8,128)(2,1)S(1)} %all_to_all.5.got_ref), custom_call_target="tpu_custom_call" | custom-call | tf_op jit(solution)/shard_map/place_normalise/pallas_call | solution.py:395

commit v8 on v7

--- a/solution.py
+++ b/solution.py
@@ -67,34 +67,36 @@
     base[2] = found[2 * count :]
 
 
-def build_band(base, row, half, band, first):
+def build_band(base, row, band, first):
     cols = base.shape[2]
-    blocks = cols // SUB
-    sub = iota((SUB, cols), 0)
-    lane = iota((SUB, cols), 1)
+    shape = (2 * SUB, cols)
+    sub = iota(shape, 0)
+    lane = iota(shape, 1)
+    lane = jnp.where(lane < cols // 2, lane, lane - cols)
     first_u = (2.0 * sub.astype(jnp.float32) + 1.0) / cols - 1.0
 
     def spin(term):
-        taps = jnp.broadcast_to(base[term, pl.ds(row, 1), :], (SUB, cols))
+        taps = jnp.broadcast_to(base[term, pl.ds(row, 1), :], shape)
         return pltpu.roll(taps, 0, 1, stride=1, stride_axis=0)
-
-    def keep(block, value):
-        if block * SUB >= half and (block + 1) * SUB - 1 + half < cols:
-            return value
-        return jnp.where(jnp.abs(lane - sub - block * SUB) <= half, value, 0.0)
 
     slope = spin(1)
     level = spin(0) + first_u * slope
     rise = spin(2)
-    for pair in range(blocks // 2):
-        two = []
-        for block in (2 * pair, 2 * pair + 1):
-            value = level + (2.0 * SUB * block / cols) * slope
-            value = keep(block, pltpu.roll(value, SUB * block, 1) if block else value)
-            other = keep(block, pltpu.roll(rise, SUB * block, 1) if block else rise)
-            two.append(jnp.concatenate([value, other], axis=1))
-        at = first + pair * 2 * SUB
-        band[at : at + 2 * SUB, :] = jnp.concatenate(two, axis=0).astype(jnp.bfloat16)
+    whole = rise.astype(jnp.bfloat16)
+    pairs = cols // (2 * SUB)
+    for pair in range(pairs):
+        shift = 2 * SUB * pair
+        value = level + (2.0 * shift / cols) * slope
+        other = whole
+        if pair == 0 or pair == pairs - 1:
+            inside = lane >= 0 if pair == 0 else lane < 2 * SUB
+            value = jnp.where(inside, value, 0.0)
+            other = jnp.where(inside, rise, 0.0).astype(jnp.bfloat16)
+        value = value.astype(jnp.bfloat16)
+        if pair:
+            value, other = pltpu.roll(value, shift, 1), pltpu.roll(other, shift, 1)
+        at = first + shift
+        band[at : at + 2 * SUB, :] = jnp.concatenate([value, other], axis=1)
 
 
 def window_kernel(
@@ -123,8 +125,7 @@
     base,
     band_a,
     band_b,
-    moved_a,
-    moved_b,
+    blocks,
     total,
     spread,
     slots,
@@ -133,8 +134,8 @@
     counts,
 ):
     rows, cols = image_ref.shape[1:]
-    half = row_ref.shape[0] // 2
-    fold = half + 1
+    fold = row_ref.shape[0] // 2 + 1
+    deep = rows // fold
     tiles = slot_of.shape[0]
     owners = out_ref.shape[0]
     data_rows = capacity * SUB
@@ -180,20 +181,26 @@
     across, down = lanczos_rows(frac_ref, cols)
     weight = weight_of(visit_ref, weight_ref)
 
-    per_group = moved_a.shape[0]
+    for index in range(3 * fold - 1):
+        blocks[index * deep : (index + 1) * deep, :] = padded[
+            pl.ds(index, deep, stride=fold), :
+        ].astype(jnp.bfloat16)
+
+    per_group = band_a.shape[0] // (2 * cols)
     groups = fold // per_group
 
-    def build(group, band, moved):
+    def build(group, band):
         for index in range(per_group):
-            r = group * per_group + index
             for part in range(2):
-                build_band(base, r + part * fold, half, band, (2 * index + part) * cols)
-            moved[index] = padded[pl.ds(r, rows + fold), :].astype(jnp.bfloat16)
-
-    def multiply(group, band, moved):
+                row = group * per_group + index + part * fold
+                build_band(base, row, band, (2 * index + part) * cols)
+
+    def multiply(group, band):
         parts = []
         for index in range(per_group):
-            parts += [moved[index, :rows, :], moved[index, fold:, :]]
+            for part in range(2):
+                first = (group * per_group + index + part * fold) * deep
+                parts.append(blocks[first : first + rows, :])
         product = jnp.dot(
             jnp.concatenate(parts, axis=1), band[...], preferred_element_type=jnp.float32
         )
@@ -208,12 +215,12 @@
         slot_of[tile] = slot
         starts[slot] = (block - owner * BLK_DEV) * SUB + offset_ref[tile]
 
-    held = ((band_a, moved_a), (band_b, moved_b))
-    build(0, *held[0])
+    held = (band_a, band_b)
+    build(0, held[0])
     for group in range(groups):
         if group + 1 < groups:
-            build(group + 1, *held[(group + 1) % 2])
-        multiply(group, *held[group % 2])
+            build(group + 1, held[(group + 1) % 2])
+        multiply(group, held[group % 2])
         for tile in range(group * tiles // groups, (group + 1) * tiles // groups):
             assign(tile)
 
@@ -222,17 +229,17 @@
         jnp.where((lane + m - 2 >= 0) & (lane + m - 2 < cols), across[m : m + 1], 0.0)
         for m in range(TAPS_DOWN)
     ]
-    chunk = 64
-    for index in range(rows // chunk):
-        first = index * chunk
-        position = (2 * (iota((chunk, cols), 0) + first) + 1).astype(jnp.float32) / rows - 1.0
-        both = total[first : first + chunk, :]
+    for phase in range(fold):
+        first = phase * deep
+        position = 2 * (fold * iota((deep, cols), 0) + phase) + 1
+        position = position.astype(jnp.float32) / rows - 1.0
+        both = total[first : first + deep, :]
         matched = both[:, :cols] + position * both[:, cols:]
         result = taps_across[2] * matched
         for m in range(TAPS_DOWN):
             if m != 2:
                 result = result + taps_across[m] * pltpu.roll(matched, (2 - m) % cols, 1)
-        spread[first + SUB : first + SUB + chunk, :] = result
+        spread[pl.ds(SUB + phase, deep, stride=fold), :] = result
 
     for tile in range(tiles):
         first = tile * SUB + SUB - 2
@@ -364,8 +371,7 @@
             pltpu.VMEM((3, 2 * fold, cols), jnp.float32),
             pltpu.VMEM((per_group * 2 * cols, 2 * cols), jnp.bfloat16),
             pltpu.VMEM((per_group * 2 * cols, 2 * cols), jnp.bfloat16),
-            pltpu.VMEM((per_group, rows + fold, cols), jnp.bfloat16),
-            pltpu.VMEM((per_group, rows + fold, cols), jnp.bfloat16),
+            pltpu.VMEM(((3 * fold - 1) * (rows // fold), cols), jnp.bfloat16),
             pltpu.VMEM((rows, 2 * cols), jnp.float32),
             pltpu.VMEM((rows + 2 * SUB, cols), jnp.float32),
             pltpu.VMEM((sky * capacity * SUB, cols), jnp.float32),

time: 22.3 us -> 21.9 us (0.982)
  Pallas kernels: 5.14 us -> 4.68 us
    pallas_call x1, Pallas kernels: 4.27 us -> 3.8 us  [on_device(): pl.pallas_call(functools.partial(window_kernel, capacity), out_shape=pltp...]
where the time goes in v8:
time: 21.9 us; the launch traced here: 21.6 us
  blocking collectives  15.6 us (71%)
  Pallas kernels  4.68 us (21%)
  between operations  1.29 us (6%)
    all_to_all x1, blocking collectives, on_device(): lax.all_to_all(messages, 'sky', split_axis=0, concat_axis=0, tiled=True)  15.6 us
    pallas_call x1, Pallas kernels, on_device(): pl.pallas_call(functools.partial(window_kernel, capacity), out_shape=pltp...  3.8 us
    pallas_call x1, Pallas kernels, on_device(): pl.pallas_call(functools.partial(sky_kernel, capacity), out_shape=(jax.Sh...  0.88 us

profile of v8, /device:TPU:0, one launch (start us, length us, event | category | flops | bytes accessed | tf_op | source)
XLA Modules:
  0.0 21.6 jit_solution(9571796186562267708)
XLA Ops:
  1.3 3.8 %match_warp_pack.1 = bf16[16,40,128]{2,1,0:T(8,128)(2,1)S(1)} custom-call(bf16[1,512,128]{2,1,0:T(8,128)(2,1)} %image_hbm.1, bf16[31,40]{1,0:T(8,128)(2,1)} %bitcast.5, bf16[31,40]{1,0:T(8,128)(2,1)} %bitcast.6, f32[3,1,40]{2,1,0:T(1,128)} %bitcast.7, bf16[1,4]{1,0:T(2,128)(2,1)} %bitcast.8, f32[1,2]{1,0:T(1,128)} %frac_hbm.1, s32[64]{0:T(128)} %block_hbm.1, ...), custom_call_target="tpu_custom_call" | custom-call | tf_op jit(solution)/shard_map/match_warp_pack/pallas_call | solution.py:354
  5.1 15.6 %all_to_all.5.got_ref = bf16[16,40,128]{2,1,0:T(8,128)(2,1)S(1)} all-to-all(bf16[16,40,128]{2,1,0:T(8,128)(2,1)S(1)} %match_warp_pack.1), channel_id=1, replica_groups=mesh['groups'=2,'sky'=16] {'sky'}, dimensions={0} | all-to-all | bytes 327680 | tf_op jit(solution)/shard_map/all_to_all | solution.py:400
  20.7 0.9 %place_normalise.1 = (f32[128,128]{1,0:T(8,128)}, f32[1,128]{1,0:T(1,128)}) custom-call(bf16[16,40,128]{2,1,0:T(8,128)(2,1)S(1)} %all_to_all.5.got_ref), custom_call_target="tpu_custom_call" | custom-call | tf_op jit(solution)/shard_map/place_normalise/pallas_call | solution.py:401

commit v9 on v8

--- a/solution.py
+++ b/solution.py
@@ -1,4 +1,5 @@
 import functools
+import itertools
 
 import jax
 import jax.numpy as jnp
@@ -97,6 +98,10 @@
             value, other = pltpu.roll(value, shift, 1), pltpu.roll(other, shift, 1)
         at = first + shift
         band[at : at + 2 * SUB, :] = jnp.concatenate([value, other], axis=1)
+
+
+def group_edges(fold):
+    return [0, fold // 8, fold // 2, fold]
 
 
 def window_kernel(
@@ -186,23 +191,24 @@
             pl.ds(index, deep, stride=fold), :
         ].astype(jnp.bfloat16)
 
-    per_group = band_a.shape[0] // (2 * cols)
-    groups = fold // per_group
+    edges = group_edges(fold)
+    groups = len(edges) - 1
 
     def build(group, band):
-        for index in range(per_group):
+        for index, r in enumerate(range(edges[group], edges[group + 1])):
             for part in range(2):
-                row = group * per_group + index + part * fold
-                build_band(base, row, band, (2 * index + part) * cols)
+                build_band(base, r + part * fold, band, (2 * index + part) * cols)
 
     def multiply(group, band):
         parts = []
-        for index in range(per_group):
+        for r in range(edges[group], edges[group + 1]):
             for part in range(2):
-                first = (group * per_group + index + part * fold) * deep
+                first = (r + part * fold) * deep
                 parts.append(blocks[first : first + rows, :])
         product = jnp.dot(
-            jnp.concatenate(parts, axis=1), band[...], preferred_element_type=jnp.float32
+            jnp.concatenate(parts, axis=1),
+            band[: len(parts) * cols, :],
+            preferred_element_type=jnp.float32,
         )
         total[...] = product if group == 0 else total[...] + product
 
@@ -348,7 +354,7 @@
     taps, basis = row_taps.shape[1], row_taps.shape[0]
     fold = taps // 2 + 1
     visits = visit_weight.shape[0]
-    per_group = 4
+    largest = max(b - a for a, b in itertools.pairwise(group_edges(fold)))
     anywhere = pl.BlockSpec(memory_space=pl.ANY)
     vmem = pl.BlockSpec(memory_space=pltpu.VMEM)
     messages = pl.pallas_call(
@@ -369,8 +375,8 @@
             pltpu.VMEM((rows + 2 * fold, cols), jnp.float32),
             pltpu.VMEM((2 * fold, basis), jnp.float32),
             pltpu.VMEM((3, 2 * fold, cols), jnp.float32),
-            pltpu.VMEM((per_group * 2 * cols, 2 * cols), jnp.bfloat16),
-            pltpu.VMEM((per_group * 2 * cols, 2 * cols), jnp.bfloat16),
+            pltpu.VMEM((largest * 2 * cols, 2 * cols), jnp.bfloat16),
+            pltpu.VMEM((largest * 2 * cols, 2 * cols), jnp.bfloat16),
             pltpu.VMEM(((3 * fold - 1) * (rows // fold), cols), jnp.bfloat16),
             pltpu.VMEM((rows, 2 * cols), jnp.float32),
             pltpu.VMEM((rows + 2 * SUB, cols), jnp.float32),

time: 21.9 us -> 21.9 us (level)
  no operation moved by 1% of the time
where the time goes in v9:
time: 21.9 us; the launch traced here: 21.6 us
  blocking collectives  15.6 us (71%)
  Pallas kernels  4.67 us (21%)
  between operations  1.29 us (6%)
    all_to_all x1, blocking collectives, on_device(): lax.all_to_all(messages, 'sky', split_axis=0, concat_axis=0, tiled=True)  15.6 us
    pallas_call x1, Pallas kernels, on_device(): pl.pallas_call(functools.partial(window_kernel, capacity), out_shape=pltp...  3.8 us
    pallas_call x1, Pallas kernels, on_device(): pl.pallas_call(functools.partial(sky_kernel, capacity), out_shape=(jax.Sh...  0.88 us

profile of v9, /device:TPU:0, one launch (start us, length us, event | category | flops | bytes accessed | tf_op | source)
XLA Modules:
  0.0 21.6 jit_solution(7138451994395832658)
XLA Ops:
  1.3 3.8 %match_warp_pack.1 = bf16[16,40,128]{2,1,0:T(8,128)(2,1)S(1)} custom-call(bf16[1,512,128]{2,1,0:T(8,128)(2,1)} %image_hbm.1, bf16[31,40]{1,0:T(8,128)(2,1)} %bitcast.5, bf16[31,40]{1,0:T(8,128)(2,1)} %bitcast.6, f32[3,1,40]{2,1,0:T(1,128)} %bitcast.7, bf16[1,4]{1,0:T(2,128)(2,1)} %bitcast.8, f32[1,2]{1,0:T(1,128)} %frac_hbm.1, s32[64]{0:T(128)} %block_hbm.1, ...), custom_call_target="tpu_custom_call" | custom-call | tf_op jit(solution)/shard_map/match_warp_pack/pallas_call | solution.py:360
  5.1 15.6 %all_to_all.5.got_ref = bf16[16,40,128]{2,1,0:T(8,128)(2,1)S(1)} all-to-all(bf16[16,40,128]{2,1,0:T(8,128)(2,1)S(1)} %match_warp_pack.1), channel_id=1, replica_groups=mesh['groups'=2,'sky'=16] {'sky'}, dimensions={0} | all-to-all | bytes 327680 | tf_op jit(solution)/shard_map/all_to_all | solution.py:406
  20.7 0.9 %place_normalise.1 = (f32[128,128]{1,0:T(8,128)}, f32[1,128]{1,0:T(1,128)}) custom-call(bf16[16,40,128]{2,1,0:T(8,128)(2,1)S(1)} %all_to_all.5.got_ref), custom_call_target="tpu_custom_call" | custom-call | tf_op jit(solution)/shard_map/place_normalise/pallas_call | solution.py:407

commit v10 on v9

--- a/solution.py
+++ b/solution.py
@@ -235,24 +235,30 @@
         jnp.where((lane + m - 2 >= 0) & (lane + m - 2 < cols), across[m : m + 1], 0.0)
         for m in range(TAPS_DOWN)
     ]
-    for phase in range(fold):
-        first = phase * deep
+    def warp_across(phase, carry):
+        first = pl.multiple_of(phase * deep, deep)
         position = 2 * (fold * iota((deep, cols), 0) + phase) + 1
         position = position.astype(jnp.float32) / rows - 1.0
-        both = total[first : first + deep, :]
+        both = total[pl.ds(first, deep), :]
         matched = both[:, :cols] + position * both[:, cols:]
         result = taps_across[2] * matched
         for m in range(TAPS_DOWN):
             if m != 2:
                 result = result + taps_across[m] * pltpu.roll(matched, (2 - m) % cols, 1)
         spread[pl.ds(SUB + phase, deep, stride=fold), :] = result
-
-    for tile in range(tiles):
+        return carry
+
+    lax.fori_loop(0, fold, warp_across, 0, unroll=4)
+
+    def warp_down(tile, carry):
         first = tile * SUB + SUB - 2
-        result = down[0:1] * spread[first : first + SUB, :]
+        result = down[0:1] * spread[pl.ds(first, SUB), :]
         for m in range(1, TAPS_DOWN):
-            result = result + down[m : m + 1] * spread[first + m : first + m + SUB, :]
+            result = result + down[m : m + 1] * spread[pl.ds(first + m, SUB), :]
         slots[pl.ds(pl.multiple_of(slot_of[tile] * SUB, SUB), SUB), :] = result
+        return carry
+
+    lax.fori_loop(0, tiles, warp_down, 0, unroll=16)
 
     sub = iota((SUB, cols), 0)
     wide = iota((SUB, cols), 1)
@@ -287,7 +293,7 @@
         out_ref[owner, data_rows:, :] = tail.astype(jnp.bfloat16)
         return carry
 
-    lax.fori_loop(0, owners, message, 0, unroll=min(owners, 16))
+    lax.fori_loop(0, owners, message, 0, unroll=4)
 
 
 def sky_kernel(capacity, got_ref, coadd_ref, map_ref):

time: 21.9 us -> 22.3 us (1.018)
  Pallas kernels: 4.67 us -> 5.12 us
    pallas_call x1, Pallas kernels: 3.8 us -> 4.24 us  [on_device(): pl.pallas_call(functools.partial(window_kernel, capacity), out_shape=pltp...]
where the time goes in v10:
time: 22.3 us; the launch traced here: 22 us
  blocking collectives  15.6 us (70%)
  Pallas kernels  5.12 us (23%)
  between operations  1.29 us (6%)
    all_to_all x1, blocking collectives, on_device(): lax.all_to_all(messages, 'sky', split_axis=0, concat_axis=0, tiled=True)  15.6 us
    pallas_call x1, Pallas kernels, on_device(): pl.pallas_call(functools.partial(window_kernel, capacity), out_shape=pltp...  4.24 us
    pallas_call x1, Pallas kernels, on_device(): pl.pallas_call(functools.partial(sky_kernel, capacity), out_shape=(jax.Sh...  0.88 us

profile of v10, /device:TPU:0, one launch (start us, length us, event | category | flops | bytes accessed | tf_op | source)
XLA Modules:
  0.0 22.0 jit_solution(6589250423059761572)
XLA Ops:
  1.3 4.2 %match_warp_pack.1 = bf16[16,40,128]{2,1,0:T(8,128)(2,1)S(1)} custom-call(bf16[1,512,128]{2,1,0:T(8,128)(2,1)} %image_hbm.1, bf16[31,40]{1,0:T(8,128)(2,1)} %bitcast.5, bf16[31,40]{1,0:T(8,128)(2,1)} %bitcast.6, f32[3,1,40]{2,1,0:T(1,128)} %bitcast.7, bf16[1,4]{1,0:T(2,128)(2,1)} %bitcast.8, f32[1,2]{1,0:T(1,128)} %frac_hbm.1, s32[64]{0:T(128)} %block_hbm.1, ...), custom_call_target="tpu_custom_call" | custom-call | tf_op jit(solution)/shard_map/match_warp_pack/pallas_call | solution.py:366
  5.5 15.6 %all_to_all.5.got_ref = bf16[16,40,128]{2,1,0:T(8,128)(2,1)S(1)} all-to-all(bf16[16,40,128]{2,1,0:T(8,128)(2,1)S(1)} %match_warp_pack.1), channel_id=1, replica_groups=mesh['groups'=2,'sky'=16] {'sky'}, dimensions={0} | all-to-all | bytes 327680 | tf_op jit(solution)/shard_map/all_to_all | solution.py:412
  21.2 0.9 %place_normalise.1 = (f32[128,128]{1,0:T(8,128)}, f32[1,128]{1,0:T(1,128)}) custom-call(bf16[16,40,128]{2,1,0:T(8,128)(2,1)S(1)} %all_to_all.5.got_ref), custom_call_target="tpu_custom_call" | custom-call | tf_op jit(solution)/shard_map/place_normalise/pallas_call | solution.py:413

commit v11 on v9

--- a/solution.py
+++ b/solution.py
@@ -133,15 +133,14 @@
     blocks,
     total,
     spread,
-    slots,
-    slot_of,
+    tile_of,
     starts,
     counts,
 ):
     rows, cols = image_ref.shape[1:]
     fold = row_ref.shape[0] // 2 + 1
     deep = rows // fold
-    tiles = slot_of.shape[0]
+    tiles = block_ref.shape[0]
     owners = out_ref.shape[0]
     data_rows = capacity * SUB
     owned = BLK_DEV * SUB
@@ -168,11 +167,11 @@
         counts[owner] = 0
 
     if owners * capacity > tiles:
-        slots[...] = jnp.zeros(slots.shape, jnp.float32)
 
         @pl.loop(0, owners * capacity)
         def _(slot):
             starts[slot] = EMPTY
+            tile_of[slot] = 0
 
     padded[:fold] = jnp.zeros((fold, cols), jnp.float32)
     padded[fold + rows :] = jnp.zeros((fold, cols), jnp.float32)
@@ -218,7 +217,7 @@
         rank = counts[owner]
         counts[owner] = rank + 1
         slot = owner * capacity + rank
-        slot_of[tile] = slot
+        tile_of[slot] = tile
         starts[slot] = (block - owner * BLK_DEV) * SUB + offset_ref[tile]
 
     held = (band_a, band_b)
@@ -247,13 +246,6 @@
                 result = result + taps_across[m] * pltpu.roll(matched, (2 - m) % cols, 1)
         spread[pl.ds(SUB + phase, deep, stride=fold), :] = result
 
-    for tile in range(tiles):
-        first = tile * SUB + SUB - 2
-        result = down[0:1] * spread[first : first + SUB, :]
-        for m in range(1, TAPS_DOWN):
-            result = result + down[m : m + 1] * spread[first + m : first + m + SUB, :]
-        slots[pl.ds(pl.multiple_of(slot_of[tile] * SUB, SUB), SUB), :] = result
-
     sub = iota((SUB, cols), 0)
     wide = iota((SUB, cols), 1)
     segment = wide >> (data_rows.bit_length() - 1)
@@ -263,31 +255,38 @@
     spill_row = wide >> (capacity.bit_length() - 1)
     tile_weight = jnp.broadcast_to(weight, (SUB, cols))
 
+    def warped(slot):
+        first = tile_of[slot] * SUB + SUB - 2
+        result = down[0:1] * spread[pl.ds(first, SUB), :]
+        for m in range(1, TAPS_DOWN):
+            result = result + down[m : m + 1] * spread[pl.ds(first + m, SUB), :]
+        return result
+
     def message(owner, carry):
-        previous = jnp.maximum(owner - 1, 0)
-        first = owner * data_rows
-        out_ref[owner, :data_rows, :] = slots[
-            pl.ds(pl.multiple_of(first, data_rows), data_rows), :
-        ].astype(jnp.bfloat16)
-        spilled = jnp.zeros((SUB, cols), jnp.float32)
-        over = jnp.zeros((SUB, cols), jnp.float32)
+        spilled, over = carry
         target = jnp.zeros((SUB, cols), jnp.int32)
+        next_spilled = jnp.zeros((SUB, cols), jnp.float32)
+        next_over = jnp.zeros((SUB, cols), jnp.float32)
+        tiles_here = []
         for c in range(capacity):
-            target = jnp.where(lane_slot == c, starts[owner * capacity + c] + lane_row, target)
-            slot = previous * capacity + c
+            slot = owner * capacity + c
             start = starts[slot]
-            past = jnp.where(owner > 0, start + SUB - owned, 0)
-            tile = slots[pl.ds(pl.multiple_of(slot * SUB, SUB), SUB), :]
-            tile = pltpu.roll(tile, start & (SUB - 1), 0)
-            spilled = spilled + jnp.where(sub < past, tile, 0.0)
-            over = jnp.where((spill_slot == c) & (spill_row < past), tile_weight, over)
+            past = start + SUB - owned
+            tile = warped(slot)
+            tiles_here.append(tile)
+            target = jnp.where(lane_slot == c, start + lane_row, target)
+            turned = pltpu.roll(tile, start & (SUB - 1), 0)
+            next_spilled = next_spilled + jnp.where(sub < past, turned, 0.0)
+            next_over = jnp.where((spill_slot == c) & (spill_row < past), tile_weight, next_over)
         meta = jnp.where(segment == 1, target.astype(jnp.float32), tile_weight)
         meta = jnp.where(segment == 0, over, meta)
         tail = jnp.where(sub == SUB - 1, meta, spilled * tile_weight)
+        out_ref[owner, :data_rows, :] = jnp.concatenate(tiles_here, axis=0).astype(jnp.bfloat16)
         out_ref[owner, data_rows:, :] = tail.astype(jnp.bfloat16)
-        return carry
-
-    lax.fori_loop(0, owners, message, 0, unroll=min(owners, 16))
+        return next_spilled, next_over
+
+    nothing = jnp.zeros((SUB, cols), jnp.float32)
+    lax.fori_loop(0, owners, message, (nothing, nothing), unroll=min(owners, 16))
 
 
 def sky_kernel(capacity, got_ref, coadd_ref, map_ref):
@@ -380,8 +379,7 @@
             pltpu.VMEM(((3 * fold - 1) * (rows // fold), cols), jnp.bfloat16),
             pltpu.VMEM((rows, 2 * cols), jnp.float32),
             pltpu.VMEM((rows + 2 * SUB, cols), jnp.float32),
-            pltpu.VMEM((sky * capacity * SUB, cols), jnp.float32),
-            pltpu.SMEM((tiles,), jnp.int32),
+            pltpu.SMEM((sky * capacity,), jnp.int32),
             pltpu.SMEM((sky * capacity,), jnp.int32),
             pltpu.SMEM((sky,), jnp.int32),
         ],

time: 21.9 us -> 21.9 us (level)
  no operation moved by 1% of the time
where the time goes in v11:
time: 21.9 us; the launch traced here: 21.6 us
  blocking collectives  15.7 us (72%)
  Pallas kernels  4.66 us (21%)
  between operations  1.29 us (6%)
    all_to_all x1, blocking collectives, on_device(): lax.all_to_all(messages, 'sky', split_axis=0, concat_axis=0, tiled=True)  15.7 us
    pallas_call x1, Pallas kernels, on_device(): pl.pallas_call(functools.partial(window_kernel, capacity), out_shape=pltp...  3.78 us
    pallas_call x1, Pallas kernels, on_device(): pl.pallas_call(functools.partial(sky_kernel, capacity), out_shape=(jax.Sh...  0.88 us

profile of v11, /device:TPU:0, one launch (start us, length us, event | category | flops | bytes accessed | tf_op | source)
XLA Modules:
  0.0 21.6 jit_solution(14828845334001500591)
XLA Ops:
  1.3 3.8 %match_warp_pack.1 = bf16[16,40,128]{2,1,0:T(8,128)(2,1)S(1)} custom-call(bf16[1,512,128]{2,1,0:T(8,128)(2,1)} %image_hbm.1, bf16[31,40]{1,0:T(8,128)(2,1)} %bitcast.5, bf16[31,40]{1,0:T(8,128)(2,1)} %bitcast.6, f32[3,1,40]{2,1,0:T(1,128)} %bitcast.7, bf16[1,4]{1,0:T(2,128)(2,1)} %bitcast.8, f32[1,2]{1,0:T(1,128)} %frac_hbm.1, s32[64]{0:T(128)} %block_hbm.1, ...), custom_call_target="tpu_custom_call" | custom-call | tf_op jit(solution)/shard_map/match_warp_pack/pallas_call | solution.py:359
  5.1 15.7 %all_to_all.5.got_ref = bf16[16,40,128]{2,1,0:T(8,128)(2,1)S(1)} all-to-all(bf16[16,40,128]{2,1,0:T(8,128)(2,1)S(1)} %match_warp_pack.1), channel_id=1, replica_groups=mesh['groups'=2,'sky'=16] {'sky'}, dimensions={0} | all-to-all | bytes 327680 | tf_op jit(solution)/shard_map/all_to_all | solution.py:404
  20.7 0.9 %place_normalise.1 = (f32[128,128]{1,0:T(8,128)}, f32[1,128]{1,0:T(1,128)}) custom-call(bf16[16,40,128]{2,1,0:T(8,128)(2,1)S(1)} %all_to_all.5.got_ref), custom_call_target="tpu_custom_call" | custom-call | tf_op jit(solution)/shard_map/place_normalise/pallas_call | solution.py:405

commit v12 on v11

--- a/solution.py
+++ b/solution.py
@@ -98,6 +98,10 @@
             value, other = pltpu.roll(value, shift, 1), pltpu.roll(other, shift, 1)
         at = first + shift
         band[at : at + 2 * SUB, :] = jnp.concatenate([value, other], axis=1)
+
+
+def first_member(owners):
+    return owners // 2
 
 
 def group_edges(fold):
@@ -281,8 +285,9 @@
         meta = jnp.where(segment == 1, target.astype(jnp.float32), tile_weight)
         meta = jnp.where(segment == 0, over, meta)
         tail = jnp.where(sub == SUB - 1, meta, spilled * tile_weight)
-        out_ref[owner, :data_rows, :] = jnp.concatenate(tiles_here, axis=0).astype(jnp.bfloat16)
-        out_ref[owner, data_rows:, :] = tail.astype(jnp.bfloat16)
+        place = lax.rem(owner + owners - first_member(owners), owners)
+        out_ref[place, :data_rows, :] = jnp.concatenate(tiles_here, axis=0).astype(jnp.bfloat16)
+        out_ref[place, data_rows:, :] = tail.astype(jnp.bfloat16)
         return next_spilled, next_over
 
     nothing = jnp.zeros((SUB, cols), jnp.float32)
@@ -401,7 +406,10 @@
         ],
         ccd_visit,
     )
-    received = lax.all_to_all(messages, "sky", split_axis=0, concat_axis=0, tiled=True)
+    order = [(place + first_member(sky)) % sky for place in range(sky)]
+    received = lax.all_to_all(
+        messages, "sky", split_axis=0, concat_axis=0, axis_index_groups=[order], tiled=True
+    )
     coadd, weight_map = pl.pallas_call(
         functools.partial(sky_kernel, capacity),
         out_shape=(

time: 21.9 us -> 20.1 us (0.918)
  blocking collectives: 15.7 us -> 13.8 us
    all_to_all x1, blocking collectives: 15.7 us -> 13.8 us  [on_device(): lax.all_to_all(messages, 'sky', split_axis=0, concat_axis=0, axis_index_g...]
where the time goes in v12:
time: 20.1 us; the launch traced here: 19.8 us
  blocking collectives  13.8 us (69%)
  Pallas kernels  4.66 us (23%)
  between operations  1.29 us (6%)
    all_to_all x1, blocking collectives, on_device(): lax.all_to_all(messages, 'sky', split_axis=0, concat_axis=0, axis_index_g...  13.8 us
    pallas_call x1, Pallas kernels, on_device(): pl.pallas_call(functools.partial(window_kernel, capacity), out_shape=pltp...  3.78 us
    pallas_call x1, Pallas kernels, on_device(): pl.pallas_call(functools.partial(sky_kernel, capacity), out_shape=(jax.Sh...  0.88 us

profile of v12, /device:TPU:0, one launch (start us, length us, event | category | flops | bytes accessed | tf_op | source)
XLA Modules:
  0.0 19.8 jit_solution(11594051781862652949)
XLA Ops:
  1.3 3.8 %match_warp_pack.1 = bf16[16,40,128]{2,1,0:T(8,128)(2,1)S(1)} custom-call(bf16[1,512,128]{2,1,0:T(8,128)(2,1)} %image_hbm.1, bf16[31,40]{1,0:T(8,128)(2,1)} %bitcast.5, bf16[31,40]{1,0:T(8,128)(2,1)} %bitcast.6, f32[3,1,40]{2,1,0:T(1,128)} %bitcast.7, bf16[1,4]{1,0:T(2,128)(2,1)} %bitcast.8, f32[1,2]{1,0:T(1,128)} %frac_hbm.1, s32[64]{0:T(128)} %block_hbm.1, ...), custom_call_target="tpu_custom_call" | custom-call | tf_op jit(solution)/shard_map/match_warp_pack/pallas_call | solution.py:364
  5.1 13.8 %all_to_all.5.got_ref = bf16[16,40,128]{2,1,0:T(8,128)(2,1)S(1)} all-to-all(bf16[16,40,128]{2,1,0:T(8,128)(2,1)S(1)} %match_warp_pack.1), channel_id=1, replica_groups={{8,9,10,11,12,13,14,15,0,1,2,3,4,5,6,7},{24,25,26,27,28,29,30,31,16,17,..., dimensions={0} | all-to-all | bytes 327680 | tf_op jit(solution)/shard_map/all_to_all | solution.py:410
  18.9 0.9 %place_normalise.1 = (f32[128,128]{1,0:T(8,128)}, f32[1,128]{1,0:T(1,128)}) custom-call(bf16[16,40,128]{2,1,0:T(8,128)(2,1)S(1)} %all_to_all.5.got_ref), custom_call_target="tpu_custom_call" | custom-call | tf_op jit(solution)/shard_map/place_normalise/pallas_call | solution.py:413

commit v13 on v12

--- a/solution.py
+++ b/solution.py
@@ -100,8 +100,10 @@
         band[at : at + 2 * SUB, :] = jnp.concatenate([value, other], axis=1)
 
 
-def first_member(owners):
-    return owners // 2
+def place_of(owner, owners):
+    slow = 1 << ((owners.bit_length() - 1) // 2)
+    fast = owners // slow
+    return owner % fast * slow + (owner // fast + slow // 2) % slow
 
 
 def group_edges(fold):
@@ -285,7 +287,7 @@
         meta = jnp.where(segment == 1, target.astype(jnp.float32), tile_weight)
         meta = jnp.where(segment == 0, over, meta)
         tail = jnp.where(sub == SUB - 1, meta, spilled * tile_weight)
-        place = lax.rem(owner + owners - first_member(owners), owners)
+        place = place_of(owner, owners)
         out_ref[place, :data_rows, :] = jnp.concatenate(tiles_here, axis=0).astype(jnp.bfloat16)
         out_ref[place, data_rows:, :] = tail.astype(jnp.bfloat16)
         return next_spilled, next_over
@@ -406,7 +408,7 @@
         ],
         ccd_visit,
     )
-    order = [(place + first_member(sky)) % sky for place in range(sky)]
+    order = sorted(range(sky), key=lambda owner: place_of(owner, sky))
     received = lax.all_to_all(
         messages, "sky", split_axis=0, concat_axis=0, axis_index_groups=[order], tiled=True
     )

time: 20.1 us -> 19.6 us (0.975)
  blocking collectives: 13.8 us -> 13.4 us
    all_to_all x1, blocking collectives: 13.8 us -> 13.4 us  [on_device(): lax.all_to_all(messages, 'sky', split_axis=0, concat_axis=0, axis_index_g...]
where the time goes in v13:
time: 19.6 us; the launch traced here: 19.4 us
  blocking collectives  13.4 us (68%)
  Pallas kernels  4.66 us (24%)
  between operations  1.29 us (7%)
    all_to_all x1, blocking collectives, on_device(): lax.all_to_all(messages, 'sky', split_axis=0, concat_axis=0, axis_index_g...  13.4 us
    pallas_call x1, Pallas kernels, on_device(): pl.pallas_call(functools.partial(window_kernel, capacity), out_shape=pltp...  3.78 us
    pallas_call x1, Pallas kernels, on_device(): pl.pallas_call(functools.partial(sky_kernel, capacity), out_shape=(jax.Sh...  0.88 us

profile of v13, /device:TPU:0, one launch (start us, length us, event | category | flops | bytes accessed | tf_op | source)
XLA Modules:
  0.0 19.4 jit_solution(8599836828601380890)
XLA Ops:
  1.3 3.8 %match_warp_pack.1 = bf16[16,40,128]{2,1,0:T(8,128)(2,1)S(1)} custom-call(bf16[1,512,128]{2,1,0:T(8,128)(2,1)} %image_hbm.1, bf16[31,40]{1,0:T(8,128)(2,1)} %bitcast.5, bf16[31,40]{1,0:T(8,128)(2,1)} %bitcast.6, f32[3,1,40]{2,1,0:T(1,128)} %bitcast.7, bf16[1,4]{1,0:T(2,128)(2,1)} %bitcast.8, f32[1,2]{1,0:T(1,128)} %frac_hbm.1, s32[64]{0:T(128)} %block_hbm.1, ...), custom_call_target="tpu_custom_call" | custom-call | tf_op jit(solution)/shard_map/match_warp_pack/pallas_call | solution.py:366
  5.1 13.4 %all_to_all.5.got_ref = bf16[16,40,128]{2,1,0:T(8,128)(2,1)S(1)} all-to-all(bf16[16,40,128]{2,1,0:T(8,128)(2,1)S(1)} %match_warp_pack.1), channel_id=1, replica_groups={{8,12,0,4,9,13,1,5,10,14,2,6,11,15,3,7},{24,28,16,20,25,29,17,21,26,30,..., dimensions={0} | all-to-all | bytes 327680 | tf_op jit(solution)/shard_map/all_to_all | solution.py:412
  18.5 0.9 %place_normalise.1 = (f32[128,128]{1,0:T(8,128)}, f32[1,128]{1,0:T(1,128)}) custom-call(bf16[16,40,128]{2,1,0:T(8,128)(2,1)S(1)} %all_to_all.5.got_ref), custom_call_target="tpu_custom_call" | custom-call | tf_op jit(solution)/shard_map/place_normalise/pallas_call | solution.py:415

commit v14 on v13

--- a/solution.py
+++ b/solution.py
@@ -103,7 +103,7 @@
 def place_of(owner, owners):
     slow = 1 << ((owners.bit_length() - 1) // 2)
     fast = owners // slow
-    return owner % fast * slow + (owner // fast + slow // 2) % slow
+    return (owner + fast // 2) % fast * slow + (owner // fast + 1) % slow
 
 
 def group_edges(fold):

time: 19.6 us -> 19.6 us (level)
  no operation moved by 1% of the time
where the time goes in v14:
time: 19.6 us; the launch traced here: 19.4 us
  blocking collectives  13.4 us (68%)
  Pallas kernels  4.66 us (24%)
  between operations  1.29 us (7%)
    all_to_all x1, blocking collectives, on_device(): lax.all_to_all(messages, 'sky', split_axis=0, concat_axis=0, axis_index_g...  13.4 us
    pallas_call x1, Pallas kernels, on_device(): pl.pallas_call(functools.partial(window_kernel, capacity), out_shape=pltp...  3.78 us
    pallas_call x1, Pallas kernels, on_device(): pl.pallas_call(functools.partial(sky_kernel, capacity), out_shape=(jax.Sh...  0.88 us

profile of v14, /device:TPU:0, one launch (start us, length us, event | category | flops | bytes accessed | tf_op | source)
XLA Modules:
  0.0 19.4 jit_solution(12179373540143038229)
XLA Ops:
  1.3 3.8 %match_warp_pack.1 = bf16[16,40,128]{2,1,0:T(8,128)(2,1)S(1)} custom-call(bf16[1,512,128]{2,1,0:T(8,128)(2,1)} %image_hbm.1, bf16[31,40]{1,0:T(8,128)(2,1)} %bitcast.5, bf16[31,40]{1,0:T(8,128)(2,1)} %bitcast.6, f32[3,1,40]{2,1,0:T(1,128)} %bitcast.7, bf16[1,4]{1,0:T(2,128)(2,1)} %bitcast.8, f32[1,2]{1,0:T(1,128)} %frac_hbm.1, s32[64]{0:T(128)} %block_hbm.1, ...), custom_call_target="tpu_custom_call" | custom-call | tf_op jit(solution)/shard_map/match_warp_pack/pallas_call | solution.py:366
  5.1 13.4 %all_to_all.5.got_ref = bf16[16,40,128]{2,1,0:T(8,128)(2,1)S(1)} all-to-all(bf16[16,40,128]{2,1,0:T(8,128)(2,1)S(1)} %match_warp_pack.1), channel_id=1, replica_groups={{14,2,6,10,15,3,7,11,12,0,4,8,13,1,5,9},{30,18,22,26,31,19,23,27,28,16,..., dimensions={0} | all-to-all | bytes 327680 | tf_op jit(solution)/shard_map/all_to_all | solution.py:412
  18.5 0.9 %place_normalise.1 = (f32[128,128]{1,0:T(8,128)}, f32[1,128]{1,0:T(1,128)}) custom-call(bf16[16,40,128]{2,1,0:T(8,128)(2,1)S(1)} %all_to_all.5.got_ref), custom_call_target="tpu_custom_call" | custom-call | tf_op jit(solution)/shard_map/place_normalise/pallas_call | solution.py:415

commit v15 on v14

--- a/solution.py
+++ b/solution.py
@@ -103,7 +103,7 @@
 def place_of(owner, owners):
     slow = 1 << ((owners.bit_length() - 1) // 2)
     fast = owners // slow
-    return (owner + fast // 2) % fast * slow + (owner // fast + 1) % slow
+    return (owner + fast // 2) % fast * slow + (owner // fast + slow // 2) % slow
 
 
 def group_edges(fold):

time: 19.6 us -> 19 us (0.969)
  blocking collectives: 13.4 us -> 12.8 us
    all_to_all x1, blocking collectives: 13.4 us -> 12.8 us  [on_device(): lax.all_to_all(messages, 'sky', split_axis=0, concat_axis=0, axis_index_g...]
where the time goes in v15:
time: 19 us; the launch traced here: 18.8 us
  blocking collectives  12.8 us (67%)
  Pallas kernels  4.66 us (25%)
  between operations  1.29 us (7%)
    all_to_all x1, blocking collectives, on_device(): lax.all_to_all(messages, 'sky', split_axis=0, concat_axis=0, axis_index_g...  12.8 us
    pallas_call x1, Pallas kernels, on_device(): pl.pallas_call(functools.partial(window_kernel, capacity), out_shape=pltp...  3.78 us
    pallas_call x1, Pallas kernels, on_device(): pl.pallas_call(functools.partial(sky_kernel, capacity), out_shape=(jax.Sh...  0.88 us

profile of v15, /device:TPU:0, one launch (start us, length us, event | category | flops | bytes accessed | tf_op | source)
XLA Modules:
  0.0 18.8 jit_solution(5216653820878848470)
XLA Ops:
  1.3 3.8 %match_warp_pack.1 = bf16[16,40,128]{2,1,0:T(8,128)(2,1)S(1)} custom-call(bf16[1,512,128]{2,1,0:T(8,128)(2,1)} %image_hbm.1, bf16[31,40]{1,0:T(8,128)(2,1)} %bitcast.5, bf16[31,40]{1,0:T(8,128)(2,1)} %bitcast.6, f32[3,1,40]{2,1,0:T(1,128)} %bitcast.7, bf16[1,4]{1,0:T(2,128)(2,1)} %bitcast.8, f32[1,2]{1,0:T(1,128)} %frac_hbm.1, s32[64]{0:T(128)} %block_hbm.1, ...), custom_call_target="tpu_custom_call" | custom-call | tf_op jit(solution)/shard_map/match_warp_pack/pallas_call | solution.py:366
  5.1 12.8 %all_to_all.5.got_ref = bf16[16,40,128]{2,1,0:T(8,128)(2,1)S(1)} all-to-all(bf16[16,40,128]{2,1,0:T(8,128)(2,1)S(1)} %match_warp_pack.1), channel_id=1, replica_groups={{10,14,2,6,11,15,3,7,8,12,0,4,9,13,1,5},{26,30,18,22,27,31,19,23,24,28,..., dimensions={0} | all-to-all | bytes 327680 | tf_op jit(solution)/shard_map/all_to_all | solution.py:412
  17.9 0.9 %place_normalise.1 = (f32[128,128]{1,0:T(8,128)}, f32[1,128]{1,0:T(1,128)}) custom-call(bf16[16,40,128]{2,1,0:T(8,128)(2,1)S(1)} %all_to_all.5.got_ref), custom_call_target="tpu_custom_call" | custom-call | tf_op jit(solution)/shard_map/place_normalise/pallas_call | solution.py:415

commit v16 on v15

--- a/solution.py
+++ b/solution.py
@@ -40,14 +40,14 @@
     return across, down
 
 
-def combined_taps(row_ref, col_ref, mix_ref, lifted, base):
+def combined_taps(row_ref, col_ref, mix_ref, turned, lifted, base):
     taps, basis = row_ref.shape
     count, cols = base.shape[1:]
     half = taps // 2
-    l, s = iota((cols, taps), 0), iota((cols, taps), 1)
-    turned = ((s + l == half) | (s + l == half + cols)).astype(jnp.float32).astype(jnp.bfloat16)
-    across = jnp.dot(turned, row_ref[...], preferred_element_type=jnp.float32)
-    across = across.astype(jnp.bfloat16)
+    rows = row_ref[...].astype(jnp.float32)
+    for tap in range(taps):
+        turned[(half - tap) % cols, :] = rows[tap]
+    across = turned[...].astype(jnp.bfloat16)
     lifted[0:1] = jnp.zeros((1, basis), jnp.float32)
     lifted[1:] = col_ref[...].astype(jnp.float32)
     down = lifted[...]
@@ -132,6 +132,7 @@
     offset_ref,
     copied,
     padded,
+    turned,
     lifted,
     base,
     band_a,
@@ -183,18 +184,22 @@
     padded[fold + rows :] = jnp.zeros((fold, cols), jnp.float32)
     spread[:SUB] = jnp.zeros((SUB, cols), jnp.float32)
     spread[SUB + rows :] = jnp.zeros((SUB, cols), jnp.float32)
-    for copy in copies:
+    turned[...] = jnp.zeros(turned.shape, jnp.float32)
+    for copy in copies[:4]:
         copy.wait()
 
-    combined_taps(row_ref, col_ref, mix_ref, lifted, base)
+    combined_taps(row_ref, col_ref, mix_ref, turned, lifted, base)
     padded[fold : fold + rows] = image_ref[0].astype(jnp.float32)
-    across, down = lanczos_rows(frac_ref, cols)
-    weight = weight_of(visit_ref, weight_ref)
 
     for index in range(3 * fold - 1):
         blocks[index * deep : (index + 1) * deep, :] = padded[
             pl.ds(index, deep, stride=fold), :
         ].astype(jnp.bfloat16)
+
+    for copy in copies[4:]:
+        copy.wait()
+    across, down = lanczos_rows(frac_ref, cols)
+    weight = weight_of(visit_ref, weight_ref)
 
     edges = group_edges(fold)
     groups = len(edges) - 1
@@ -379,6 +384,7 @@
             pltpu.SMEM((tiles,), jnp.int32),
             pltpu.SemaphoreType.DMA((8,)),
             pltpu.VMEM((rows + 2 * fold, cols), jnp.float32),
+            pltpu.VMEM((cols, basis), jnp.float32),
             pltpu.VMEM((2 * fold, basis), jnp.float32),
             pltpu.VMEM((3, 2 * fold, cols), jnp.float32),
             pltpu.VMEM((largest * 2 * cols, 2 * cols), jnp.bfloat16),

time: 19 us -> 19.1 us (level)
  no operation moved by 1% of the time
where the time goes in v16:
time: 19.1 us; the launch traced here: 18.8 us
  blocking collectives  12.8 us (67%)
  Pallas kernels  4.74 us (25%)
  between operations  1.29 us (7%)
    all_to_all x1, blocking collectives, on_device(): lax.all_to_all(messages, 'sky', split_axis=0, concat_axis=0, axis_index_g...  12.8 us
    pallas_call x1, Pallas kernels, on_device(): pl.pallas_call(functools.partial(window_kernel, capacity), out_shape=pltp...  3.86 us
    pallas_call x1, Pallas kernels, on_device(): pl.pallas_call(functools.partial(sky_kernel, capacity), out_shape=(jax.Sh...  0.88 us

profile of v16, /device:TPU:0, one launch (start us, length us, event | category | flops | bytes accessed | tf_op | source)
XLA Modules:
  0.0 18.8 jit_solution(10357112934253845921)
XLA Ops:
  1.3 3.9 %match_warp_pack.1 = bf16[16,40,128]{2,1,0:T(8,128)(2,1)S(1)} custom-call(bf16[1,512,128]{2,1,0:T(8,128)(2,1)} %image_hbm.1, bf16[31,40]{1,0:T(8,128)(2,1)} %bitcast.5, bf16[31,40]{1,0:T(8,128)(2,1)} %bitcast.6, f32[3,1,40]{2,1,0:T(1,128)} %bitcast.7, bf16[1,4]{1,0:T(2,128)(2,1)} %bitcast.8, f32[1,2]{1,0:T(1,128)} %frac_hbm.1, s32[64]{0:T(128)} %block_hbm.1, ...), custom_call_target="tpu_custom_call" | custom-call | tf_op jit(solution)/shard_map/match_warp_pack/pallas_call | solution.py:371
  5.1 12.8 %all_to_all.5.got_ref = bf16[16,40,128]{2,1,0:T(8,128)(2,1)S(1)} all-to-all(bf16[16,40,128]{2,1,0:T(8,128)(2,1)S(1)} %match_warp_pack.1), channel_id=1, replica_groups={{10,14,2,6,11,15,3,7,8,12,0,4,9,13,1,5},{26,30,18,22,27,31,19,23,24,28,..., dimensions={0} | all-to-all | bytes 327680 | tf_op jit(solution)/shard_map/all_to_all | solution.py:418
  18.0 0.9 %place_normalise.1 = (f32[128,128]{1,0:T(8,128)}, f32[1,128]{1,0:T(1,128)}) custom-call(bf16[16,40,128]{2,1,0:T(8,128)(2,1)S(1)} %all_to_all.5.got_ref), custom_call_target="tpu_custom_call" | custom-call | tf_op jit(solution)/shard_map/place_normalise/pallas_call | solution.py:421

commit v17 on v15

--- a/solution.py
+++ b/solution.py
@@ -103,7 +103,7 @@
 def place_of(owner, owners):
     slow = 1 << ((owners.bit_length() - 1) // 2)
     fast = owners // slow
-    return (owner + fast // 2) % fast * slow + (owner // fast + slow // 2) % slow
+    return (owner // fast + slow // 2) % slow * fast + (owner + fast // 2) % fast
 
 
 def group_edges(fold):

time: 19 us -> 18.1 us (0.953)
  the two profiles are of different devices: /device:TPU:0 before, /device:TPU:1 now
where the time goes in v17:
time: 18.1 us; the launch traced here: 17.8 us
  blocking collectives  11.9 us (66%)
  Pallas kernels  4.67 us (26%)
  between operations  1.29 us (7%)
    all_to_all x1, blocking collectives, on_device(): lax.all_to_all(messages, 'sky', split_axis=0, concat_axis=0, axis_index_g...  11.9 us
    pallas_call x1, Pallas kernels, on_device(): pl.pallas_call(functools.partial(window_kernel, capacity), out_shape=pltp...  3.79 us
    pallas_call x1, Pallas kernels, on_device(): pl.pallas_call(functools.partial(sky_kernel, capacity), out_shape=(jax.Sh...  0.88 us

profile of v17, /device:TPU:1, one launch (start us, length us, event | category | flops | bytes accessed | tf_op | source)
XLA Modules:
  0.0 17.8 jit_solution(521995075801617896)
XLA Ops:
  1.3 3.8 %match_warp_pack.1 = bf16[16,40,128]{2,1,0:T(8,128)(2,1)S(1)} custom-call(bf16[1,512,128]{2,1,0:T(8,128)(2,1)} %image_hbm.1, bf16[31,40]{1,0:T(8,128)(2,1)} %bitcast.5, bf16[31,40]{1,0:T(8,128)(2,1)} %bitcast.6, f32[3,1,40]{2,1,0:T(1,128)} %bitcast.7, bf16[1,4]{1,0:T(2,128)(2,1)} %bitcast.8, f32[1,2]{1,0:T(1,128)} %frac_hbm.1, s32[64]{0:T(128)} %block_hbm.1, ...), custom_call_target="tpu_custom_call" | custom-call | tf_op jit(solution)/shard_map/match_warp_pack/pallas_call | solution.py:366
  5.1 11.9 %all_to_all.5.got_ref = bf16[16,40,128]{2,1,0:T(8,128)(2,1)S(1)} all-to-all(bf16[16,40,128]{2,1,0:T(8,128)(2,1)S(1)} %match_warp_pack.1), channel_id=1, replica_groups={{10,11,8,9,14,15,12,13,2,3,0,1,6,7,4,5},{26,27,24,25,30,31,28,29,18,19,..., dimensions={0} | all-to-all | bytes 327680 | tf_op jit(solution)/shard_map/all_to_all | solution.py:412
  16.9 0.9 %place_normalise.1 = (f32[128,128]{1,0:T(8,128)}, f32[1,128]{1,0:T(1,128)}) custom-call(bf16[16,40,128]{2,1,0:T(8,128)(2,1)S(1)} %all_to_all.5.got_ref), custom_call_target="tpu_custom_call" | custom-call | tf_op jit(solution)/shard_map/place_normalise/pallas_call | solution.py:415

commit v18 on v17

--- a/solution.py
+++ b/solution.py
@@ -103,7 +103,7 @@
 def place_of(owner, owners):
     slow = 1 << ((owners.bit_length() - 1) // 2)
     fast = owners // slow
-    return (owner // fast + slow // 2) % slow * fast + (owner + fast // 2) % fast
+    return (slow // 2 + slow - owner // fast) % slow * fast + (owner + fast // 2) % fast
 
 
 def group_edges(fold):

time: 18.1 us -> 18.7 us (1.033)
  the two profiles are of different devices: /device:TPU:1 before, /device:TPU:0 now
where the time goes in v18:
time: 18.7 us; the launch traced here: 18.4 us
  blocking collectives  12.5 us (67%)
  Pallas kernels  4.66 us (25%)
  between operations  1.29 us (7%)
    all_to_all x1, blocking collectives, on_device(): lax.all_to_all(messages, 'sky', split_axis=0, concat_axis=0, axis_index_g...  12.5 us
    pallas_call x1, Pallas kernels, on_device(): pl.pallas_call(functools.partial(window_kernel, capacity), out_shape=pltp...  3.78 us
    pallas_call x1, Pallas kernels, on_device(): pl.pallas_call(functools.partial(sky_kernel, capacity), out_shape=(jax.Sh...  0.88 us

profile of v18, /device:TPU:0, one launch (start us, length us, event | category | flops | bytes accessed | tf_op | source)
XLA Modules:
  0.0 18.4 jit_solution(10299564025286907105)
XLA Ops:
  1.3 3.8 %match_warp_pack.1 = bf16[16,40,128]{2,1,0:T(8,128)(2,1)S(1)} custom-call(bf16[1,512,128]{2,1,0:T(8,128)(2,1)} %image_hbm.1, bf16[31,40]{1,0:T(8,128)(2,1)} %bitcast.5, bf16[31,40]{1,0:T(8,128)(2,1)} %bitcast.6, f32[3,1,40]{2,1,0:T(1,128)} %bitcast.7, bf16[1,4]{1,0:T(2,128)(2,1)} %bitcast.8, f32[1,2]{1,0:T(1,128)} %frac_hbm.1, s32[64]{0:T(128)} %block_hbm.1, ...), custom_call_target="tpu_custom_call" | custom-call | tf_op jit(solution)/shard_map/match_warp_pack/pallas_call | solution.py:366
  5.1 12.5 %all_to_all.5.got_ref = bf16[16,40,128]{2,1,0:T(8,128)(2,1)S(1)} all-to-all(bf16[16,40,128]{2,1,0:T(8,128)(2,1)S(1)} %match_warp_pack.1), channel_id=1, replica_groups={{10,11,8,9,6,7,4,5,2,3,0,1,14,15,12,13},{26,27,24,25,22,23,20,21,18,19,..., dimensions={0} | all-to-all | bytes 327680 | tf_op jit(solution)/shard_map/all_to_all | solution.py:412
  17.5 0.9 %place_normalise.1 = (f32[128,128]{1,0:T(8,128)}, f32[1,128]{1,0:T(1,128)}) custom-call(bf16[16,40,128]{2,1,0:T(8,128)(2,1)S(1)} %all_to_all.5.got_ref), custom_call_target="tpu_custom_call" | custom-call | tf_op jit(solution)/shard_map/place_normalise/pallas_call | solution.py:415

commit v19 on v17

--- a/solution.py
+++ b/solution.py
@@ -198,6 +198,7 @@
 
     edges = group_edges(fold)
     groups = len(edges) - 1
+    pieces = 2
 
     def build(group, band):
         for index, r in enumerate(range(edges[group], edges[group + 1])):
@@ -205,17 +206,20 @@
                 build_band(base, r + part * fold, band, (2 * index + part) * cols)
 
     def multiply(group, band):
-        parts = []
-        for r in range(edges[group], edges[group + 1]):
-            for part in range(2):
-                first = (r + part * fold) * deep
-                parts.append(blocks[first : first + rows, :])
-        product = jnp.dot(
-            jnp.concatenate(parts, axis=1),
-            band[: len(parts) * cols, :],
-            preferred_element_type=jnp.float32,
-        )
-        total[...] = product if group == 0 else total[...] + product
+        for piece in range(pieces):
+            height = rows // pieces
+            parts = []
+            for r in range(edges[group], edges[group + 1]):
+                for part in range(2):
+                    first = (r + part * fold) * deep + piece * height
+                    parts.append(blocks[first : first + height, :])
+            product = jnp.dot(
+                jnp.concatenate(parts, axis=1),
+                band[: len(parts) * cols, :],
+                preferred_element_type=jnp.float32,
+            )
+            here = slice(piece * height, (piece + 1) * height)
+            total[here, :] = product if group == 0 else total[here, :] + product
 
     def assign(tile):
         block = block_ref[tile]

time: 18.1 us -> 18.7 us (1.033)
  Pallas kernels: 4.67 us -> 5.28 us
    pallas_call x1, Pallas kernels: 3.79 us -> 4.41 us  [on_device(): pl.pallas_call(functools.partial(window_kernel, capacity), out_shape=pltp...]
where the time goes in v19:
time: 18.7 us; the launch traced here: 18.4 us
  blocking collectives  11.9 us (64%)
  Pallas kernels  5.28 us (28%)
  between operations  1.29 us (7%)
    all_to_all x1, blocking collectives, on_device(): lax.all_to_all(messages, 'sky', split_axis=0, concat_axis=0, axis_index_g...  11.9 us
    pallas_call x1, Pallas kernels, on_device(): pl.pallas_call(functools.partial(window_kernel, capacity), out_shape=pltp...  4.41 us
    pallas_call x1, Pallas kernels, on_device(): pl.pallas_call(functools.partial(sky_kernel, capacity), out_shape=(jax.Sh...  0.88 us

profile of v19, /device:TPU:1, one launch (start us, length us, event | category | flops | bytes accessed | tf_op | source)
XLA Modules:
  0.0 18.4 jit_solution(16215164329982420559)
XLA Ops:
  1.3 4.4 %match_warp_pack.1 = bf16[16,40,128]{2,1,0:T(8,128)(2,1)S(1)} custom-call(bf16[1,512,128]{2,1,0:T(8,128)(2,1)} %image_hbm.1, bf16[31,40]{1,0:T(8,128)(2,1)} %bitcast.5, bf16[31,40]{1,0:T(8,128)(2,1)} %bitcast.6, f32[3,1,40]{2,1,0:T(1,128)} %bitcast.7, bf16[1,4]{1,0:T(2,128)(2,1)} %bitcast.8, f32[1,2]{1,0:T(1,128)} %frac_hbm.1, s32[64]{0:T(128)} %block_hbm.1, ...), custom_call_target="tpu_custom_call" | custom-call | tf_op jit(solution)/shard_map/match_warp_pack/pallas_call | solution.py:370
  5.7 11.9 %all_to_all.5.got_ref = bf16[16,40,128]{2,1,0:T(8,128)(2,1)S(1)} all-to-all(bf16[16,40,128]{2,1,0:T(8,128)(2,1)S(1)} %match_warp_pack.1), channel_id=1, replica_groups={{10,11,8,9,14,15,12,13,2,3,0,1,6,7,4,5},{26,27,24,25,30,31,28,29,18,19,..., dimensions={0} | all-to-all | bytes 327680 | tf_op jit(solution)/shard_map/all_to_all | solution.py:416
  17.6 0.9 %place_normalise.1 = (f32[128,128]{1,0:T(8,128)}, f32[1,128]{1,0:T(1,128)}) custom-call(bf16[16,40,128]{2,1,0:T(8,128)(2,1)S(1)} %all_to_all.5.got_ref), custom_call_target="tpu_custom_call" | custom-call | tf_op jit(solution)/shard_map/place_normalise/pallas_call | solution.py:419

commit v20 on v17

--- a/solution.py
+++ b/solution.py
@@ -13,6 +13,7 @@
 LARGE_VMEM = 32 * 1024 * 1024
 SMALL_VMEM = 16 * 1024 * 1024
 EMPTY = -64
+IMAGE_PIECES = 8
 TAPS_DOWN = 6
 
 
@@ -151,19 +152,21 @@
     data_rows = capacity * SUB
     owned = BLK_DEV * SUB
 
-    pairs = (
+    piece = rows // IMAGE_PIECES
+    parts = [pl.ds(index * piece, piece) for index in range(IMAGE_PIECES)]
+    small = [
         (row_hbm, row_ref),
         (col_hbm, col_ref),
         (mix_hbm, mix_ref),
-        (image_hbm, image_ref),
+        (block_hbm, block_ref),
+        (offset_hbm, offset_ref),
         (frac_hbm, frac_ref),
         (weight_hbm, weight_ref),
-        (block_hbm, block_ref),
-        (offset_hbm, offset_ref),
-    )
+    ]
+    large = [(image_hbm.at[:, part, :], image_ref.at[:, part, :]) for part in parts]
     copies = [
         pltpu.make_async_copy(source, target, copied.at[index])
-        for index, (source, target) in enumerate(pairs)
+        for index, (source, target) in enumerate(small[:3] + large + small[3:])
     ]
     for copy in copies:
         copy.start()
@@ -183,10 +186,11 @@
     padded[fold + rows :] = jnp.zeros((fold, cols), jnp.float32)
     spread[:SUB] = jnp.zeros((SUB, cols), jnp.float32)
     spread[SUB + rows :] = jnp.zeros((SUB, cols), jnp.float32)
-    for copy in copies:
+    for copy in copies[:3]:
         copy.wait()
-
     combined_taps(row_ref, col_ref, mix_ref, lifted, base)
+    for copy in copies[3:]:
+        copy.wait()
     padded[fold : fold + rows] = image_ref[0].astype(jnp.float32)
     across, down = lanczos_rows(frac_ref, cols)
     weight = weight_of(visit_ref, weight_ref)
@@ -377,7 +381,7 @@
             pltpu.SMEM((1, 2), jnp.float32),
             pltpu.SMEM((tiles,), jnp.int32),
             pltpu.SMEM((tiles,), jnp.int32),
-            pltpu.SemaphoreType.DMA((8,)),
+            pltpu.SemaphoreType.DMA((7 + IMAGE_PIECES,)),
             pltpu.VMEM((rows + 2 * fold, cols), jnp.float32),
             pltpu.VMEM((2 * fold, basis), jnp.float32),
             pltpu.VMEM((3, 2 * fold, cols), jnp.float32),

time: 18.1 us -> 18.2 us (level)
  no operation moved by 1% of the time
where the time goes in v20:
time: 18.2 us; the launch traced here: 18 us
  blocking collectives  11.9 us (65%)
  Pallas kernels  4.84 us (27%)
  between operations  1.29 us (7%)
    all_to_all x1, blocking collectives, on_device(): lax.all_to_all(messages, 'sky', split_axis=0, concat_axis=0, axis_index_g...  11.9 us
    pallas_call x1, Pallas kernels, on_device(): pl.pallas_call(functools.partial(window_kernel, capacity), out_shape=pltp...  3.96 us
    pallas_call x1, Pallas kernels, on_device(): pl.pallas_call(functools.partial(sky_kernel, capacity), out_shape=(jax.Sh...  0.88 us

profile of v20, /device:TPU:1, one launch (start us, length us, event | category | flops | bytes accessed | tf_op | source)
XLA Modules:
  0.0 18.0 jit_solution(9624810557932469861)
XLA Ops:
  1.3 4.0 %match_warp_pack.1 = bf16[16,40,128]{2,1,0:T(8,128)(2,1)S(1)} custom-call(bf16[1,512,128]{2,1,0:T(8,128)(2,1)} %image_hbm.1, bf16[31,40]{1,0:T(8,128)(2,1)} %bitcast.5, bf16[31,40]{1,0:T(8,128)(2,1)} %bitcast.6, f32[3,1,40]{2,1,0:T(1,128)} %bitcast.7, bf16[1,4]{1,0:T(2,128)(2,1)} %bitcast.8, f32[1,2]{1,0:T(1,128)} %frac_hbm.1, s32[64]{0:T(128)} %block_hbm.1, ...), custom_call_target="tpu_custom_call" | custom-call | tf_op jit(solution)/shard_map/match_warp_pack/pallas_call | solution.py:370
  5.2 11.9 %all_to_all.5.got_ref = bf16[16,40,128]{2,1,0:T(8,128)(2,1)S(1)} all-to-all(bf16[16,40,128]{2,1,0:T(8,128)(2,1)S(1)} %match_warp_pack.1), channel_id=1, replica_groups={{10,11,8,9,14,15,12,13,2,3,0,1,6,7,4,5},{26,27,24,25,30,31,28,29,18,19,..., dimensions={0} | all-to-all | bytes 327680 | tf_op jit(solution)/shard_map/all_to_all | solution.py:416
  17.1 0.9 %place_normalise.1 = (f32[128,128]{1,0:T(8,128)}, f32[1,128]{1,0:T(1,128)}) custom-call(bf16[16,40,128]{2,1,0:T(8,128)(2,1)S(1)} %all_to_all.5.got_ref), custom_call_target="tpu_custom_call" | custom-call | tf_op jit(solution)/shard_map/place_normalise/pallas_call | solution.py:419

commit v21 on v17

--- a/solution.py
+++ b/solution.py
@@ -152,10 +152,10 @@
     owned = BLK_DEV * SUB
 
     pairs = (
+        (image_hbm, image_ref),
         (row_hbm, row_ref),
         (col_hbm, col_ref),
         (mix_hbm, mix_ref),
-        (image_hbm, image_ref),
         (frac_hbm, frac_ref),
         (weight_hbm, weight_ref),
         (block_hbm, block_ref),

time: 18.1 us -> 18 us (level)
  no operation moved by 1% of the time
where the time goes in v21:
time: 18 us; the launch traced here: 17.8 us
  blocking collectives  11.9 us (66%)
  Pallas kernels  4.62 us (26%)
  between operations  1.29 us (7%)
    all_to_all x1, blocking collectives, on_device(): lax.all_to_all(messages, 'sky', split_axis=0, concat_axis=0, axis_index_g...  11.9 us
    pallas_call x1, Pallas kernels, on_device(): pl.pallas_call(functools.partial(window_kernel, capacity), out_shape=pltp...  3.74 us
    pallas_call x1, Pallas kernels, on_device(): pl.pallas_call(functools.partial(sky_kernel, capacity), out_shape=(jax.Sh...  0.88 us

profile of v21, /device:TPU:1, one launch (start us, length us, event | category | flops | bytes accessed | tf_op | source)
XLA Modules:
  0.0 17.8 jit_solution(201375868558556780)
XLA Ops:
  1.3 3.7 %match_warp_pack.1 = bf16[16,40,128]{2,1,0:T(8,128)(2,1)S(1)} custom-call(bf16[1,512,128]{2,1,0:T(8,128)(2,1)} %image_hbm.1, bf16[31,40]{1,0:T(8,128)(2,1)} %bitcast.5, bf16[31,40]{1,0:T(8,128)(2,1)} %bitcast.6, f32[3,1,40]{2,1,0:T(1,128)} %bitcast.7, bf16[1,4]{1,0:T(2,128)(2,1)} %bitcast.8, f32[1,2]{1,0:T(1,128)} %frac_hbm.1, s32[64]{0:T(128)} %block_hbm.1, ...), custom_call_target="tpu_custom_call" | custom-call | tf_op jit(solution)/shard_map/match_warp_pack/pallas_call | solution.py:366
  5.0 11.9 %all_to_all.5.got_ref = bf16[16,40,128]{2,1,0:T(8,128)(2,1)S(1)} all-to-all(bf16[16,40,128]{2,1,0:T(8,128)(2,1)S(1)} %match_warp_pack.1), channel_id=1, replica_groups={{10,11,8,9,14,15,12,13,2,3,0,1,6,7,4,5},{26,27,24,25,30,31,28,29,18,19,..., dimensions={0} | all-to-all | bytes 327680 | tf_op jit(solution)/shard_map/all_to_all | solution.py:412
  16.9 0.9 %place_normalise.1 = (f32[128,128]{1,0:T(8,128)}, f32[1,128]{1,0:T(1,128)}) custom-call(bf16[16,40,128]{2,1,0:T(8,128)(2,1)S(1)} %all_to_all.5.got_ref), custom_call_target="tpu_custom_call" | custom-call | tf_op jit(solution)/shard_map/place_normalise/pallas_call | solution.py:415

commit v22 on v21

--- a/solution.py
+++ b/solution.py
@@ -229,9 +229,9 @@
     held = (band_a, band_b)
     build(0, held[0])
     for group in range(groups):
+        multiply(group, held[group % 2])
         if group + 1 < groups:
             build(group + 1, held[(group + 1) % 2])
-        multiply(group, held[group % 2])
         for tile in range(group * tiles // groups, (group + 1) * tiles // groups):
             assign(tile)
 

time: 18 us -> 18 us (level)
  no operation moved by 1% of the time
where the time goes in v22:
time: 18 us; the launch traced here: 17.8 us
  blocking collectives  11.9 us (66%)
  Pallas kernels  4.62 us (26%)
  between operations  1.29 us (7%)
    all_to_all x1, blocking collectives, on_device(): lax.all_to_all(messages, 'sky', split_axis=0, concat_axis=0, axis_index_g...  11.9 us
    pallas_call x1, Pallas kernels, on_device(): pl.pallas_call(functools.partial(window_kernel, capacity), out_shape=pltp...  3.74 us
    pallas_call x1, Pallas kernels, on_device(): pl.pallas_call(functools.partial(sky_kernel, capacity), out_shape=(jax.Sh...  0.88 us

profile of v22, /device:TPU:1, one launch (start us, length us, event | category | flops | bytes accessed | tf_op | source)
XLA Modules:
  0.0 17.8 jit_solution(201375868558556780)
XLA Ops:
  1.3 3.7 %match_warp_pack.1 = bf16[16,40,128]{2,1,0:T(8,128)(2,1)S(1)} custom-call(bf16[1,512,128]{2,1,0:T(8,128)(2,1)} %image_hbm.1, bf16[31,40]{1,0:T(8,128)(2,1)} %bitcast.5, bf16[31,40]{1,0:T(8,128)(2,1)} %bitcast.6, f32[3,1,40]{2,1,0:T(1,128)} %bitcast.7, bf16[1,4]{1,0:T(2,128)(2,1)} %bitcast.8, f32[1,2]{1,0:T(1,128)} %frac_hbm.1, s32[64]{0:T(128)} %block_hbm.1, ...), custom_call_target="tpu_custom_call" | custom-call | tf_op jit(solution)/shard_map/match_warp_pack/pallas_call | solution.py:366
  5.0 11.9 %all_to_all.5.got_ref = bf16[16,40,128]{2,1,0:T(8,128)(2,1)S(1)} all-to-all(bf16[16,40,128]{2,1,0:T(8,128)(2,1)S(1)} %match_warp_pack.1), channel_id=1, replica_groups={{10,11,8,9,14,15,12,13,2,3,0,1,6,7,4,5},{26,27,24,25,30,31,28,29,18,19,..., dimensions={0} | all-to-all | bytes 327680 | tf_op jit(solution)/shard_map/all_to_all | solution.py:412
  16.9 0.9 %place_normalise.1 = (f32[128,128]{1,0:T(8,128)}, f32[1,128]{1,0:T(1,128)}) custom-call(bf16[16,40,128]{2,1,0:T(8,128)(2,1)S(1)} %all_to_all.5.got_ref), custom_call_target="tpu_custom_call" | custom-call | tf_op jit(solution)/shard_map/place_normalise/pallas_call | solution.py:415

commit v23 on v21

--- a/solution.py
+++ b/solution.py
@@ -103,7 +103,10 @@
 def place_of(owner, owners):
     slow = 1 << ((owners.bit_length() - 1) // 2)
     fast = owners // slow
-    return (owner // fast + slow // 2) % slow * fast + (owner + fast // 2) % fast
+    half = slow // 2
+    far = owner // fast // half
+    block = far * (owner // fast - half) + (1 - far) * (slow - 1 - owner // fast)
+    return block * fast + (owner + fast // 2) % fast
 
 
 def group_edges(fold):

time: 18 us -> 18.3 us (1.017)
  the two profiles are of different devices: /device:TPU:1 before, /device:TPU:0 now
where the time goes in v23:
time: 18.3 us; the launch traced here: 18 us
  blocking collectives  12.1 us (66%)
  Pallas kernels  4.62 us (25%)
  between operations  1.29 us (7%)
    all_to_all x1, blocking collectives, on_device(): lax.all_to_all(messages, 'sky', split_axis=0, concat_axis=0, axis_index_g...  12.1 us
    pallas_call x1, Pallas kernels, on_device(): pl.pallas_call(functools.partial(window_kernel, capacity), out_shape=pltp...  3.74 us
    pallas_call x1, Pallas kernels, on_device(): pl.pallas_call(functools.partial(sky_kernel, capacity), out_shape=(jax.Sh...  0.88 us

profile of v23, /device:TPU:0, one launch (start us, length us, event | category | flops | bytes accessed | tf_op | source)
XLA Modules:
  0.0 18.0 jit_solution(2143497204398317347)
XLA Ops:
  1.3 3.7 %match_warp_pack.1 = bf16[16,40,128]{2,1,0:T(8,128)(2,1)S(1)} custom-call(bf16[1,512,128]{2,1,0:T(8,128)(2,1)} %image_hbm.1, bf16[31,40]{1,0:T(8,128)(2,1)} %bitcast.5, bf16[31,40]{1,0:T(8,128)(2,1)} %bitcast.6, f32[3,1,40]{2,1,0:T(1,128)} %bitcast.7, bf16[1,4]{1,0:T(2,128)(2,1)} %bitcast.8, f32[1,2]{1,0:T(1,128)} %frac_hbm.1, s32[64]{0:T(128)} %block_hbm.1, ...), custom_call_target="tpu_custom_call" | custom-call | tf_op jit(solution)/shard_map/match_warp_pack/pallas_call | solution.py:369
  5.0 12.1 %all_to_all.5.got_ref = bf16[16,40,128]{2,1,0:T(8,128)(2,1)S(1)} all-to-all(bf16[16,40,128]{2,1,0:T(8,128)(2,1)S(1)} %match_warp_pack.1), channel_id=1, replica_groups={{10,11,8,9,14,15,12,13,6,7,4,5,2,3,0,1},{26,27,24,25,30,31,28,29,22,23,..., dimensions={0} | all-to-all | bytes 327680 | tf_op jit(solution)/shard_map/all_to_all | solution.py:415
  17.1 0.9 %place_normalise.1 = (f32[128,128]{1,0:T(8,128)}, f32[1,128]{1,0:T(1,128)}) custom-call(bf16[16,40,128]{2,1,0:T(8,128)(2,1)S(1)} %all_to_all.5.got_ref), custom_call_target="tpu_custom_call" | custom-call | tf_op jit(solution)/shard_map/place_normalise/pallas_call | solution.py:418

commit v24 on v21

--- a/solution.py
+++ b/solution.py
@@ -183,10 +183,11 @@
     padded[fold + rows :] = jnp.zeros((fold, cols), jnp.float32)
     spread[:SUB] = jnp.zeros((SUB, cols), jnp.float32)
     spread[SUB + rows :] = jnp.zeros((SUB, cols), jnp.float32)
-    for copy in copies:
+    for copy in copies[1:4]:
         copy.wait()
-
     combined_taps(row_ref, col_ref, mix_ref, lifted, base)
+    for copy in copies[:1] + copies[4:]:
+        copy.wait()
     padded[fold : fold + rows] = image_ref[0].astype(jnp.float32)
     across, down = lanczos_rows(frac_ref, cols)
     weight = weight_of(visit_ref, weight_ref)

time: 18 us -> 17.8 us (0.989)
  no operation moved by 1% of the time
where the time goes in v24:
time: 17.8 us; the launch traced here: 17.7 us
  blocking collectives  11.9 us (67%)
  Pallas kernels  4.5 us (25%)
  between operations  1.29 us (7%)
    all_to_all x1, blocking collectives, on_device(): lax.all_to_all(messages, 'sky', split_axis=0, concat_axis=0, axis_index_g...  11.9 us
    pallas_call x1, Pallas kernels, on_device(): pl.pallas_call(functools.partial(window_kernel, capacity), out_shape=pltp...  3.62 us
    pallas_call x1, Pallas kernels, on_device(): pl.pallas_call(functools.partial(sky_kernel, capacity), out_shape=(jax.Sh...  0.88 us

profile of v24, /device:TPU:1, one launch (start us, length us, event | category | flops | bytes accessed | tf_op | source)
XLA Modules:
  0.0 17.7 jit_solution(1135611575882112542)
XLA Ops:
  1.3 3.6 %match_warp_pack.1 = bf16[16,40,128]{2,1,0:T(8,128)(2,1)S(1)} custom-call(bf16[1,512,128]{2,1,0:T(8,128)(2,1)} %image_hbm.1, bf16[31,40]{1,0:T(8,128)(2,1)} %bitcast.5, bf16[31,40]{1,0:T(8,128)(2,1)} %bitcast.6, f32[3,1,40]{2,1,0:T(1,128)} %bitcast.7, bf16[1,4]{1,0:T(2,128)(2,1)} %bitcast.8, f32[1,2]{1,0:T(1,128)} %frac_hbm.1, s32[64]{0:T(128)} %block_hbm.1, ...), custom_call_target="tpu_custom_call" | custom-call | tf_op jit(solution)/shard_map/match_warp_pack/pallas_call | solution.py:367
  4.9 11.9 %all_to_all.5.got_ref = bf16[16,40,128]{2,1,0:T(8,128)(2,1)S(1)} all-to-all(bf16[16,40,128]{2,1,0:T(8,128)(2,1)S(1)} %match_warp_pack.1), channel_id=1, replica_groups={{10,11,8,9,14,15,12,13,2,3,0,1,6,7,4,5},{26,27,24,25,30,31,28,29,18,19,..., dimensions={0} | all-to-all | bytes 327680 | tf_op jit(solution)/shard_map/all_to_all | solution.py:413
  16.8 0.9 %place_normalise.1 = (f32[128,128]{1,0:T(8,128)}, f32[1,128]{1,0:T(1,128)}) custom-call(bf16[16,40,128]{2,1,0:T(8,128)(2,1)S(1)} %all_to_all.5.got_ref), custom_call_target="tpu_custom_call" | custom-call | tf_op jit(solution)/shard_map/place_normalise/pallas_call | solution.py:416

commit v25 on v24

--- a/solution.py
+++ b/solution.py
@@ -241,12 +241,11 @@
         jnp.where((lane + m - 2 >= 0) & (lane + m - 2 < cols), across[m : m + 1], 0.0)
         for m in range(TAPS_DOWN)
     ]
+    position = (2 * fold * iota((deep, cols), 0) + 1).astype(jnp.float32) / rows - 1.0
     for phase in range(fold):
         first = phase * deep
-        position = 2 * (fold * iota((deep, cols), 0) + phase) + 1
-        position = position.astype(jnp.float32) / rows - 1.0
         both = total[first : first + deep, :]
-        matched = both[:, :cols] + position * both[:, cols:]
+        matched = both[:, :cols] + (position + 2.0 * phase / rows) * both[:, cols:]
         result = taps_across[2] * matched
         for m in range(TAPS_DOWN):
             if m != 2:
@@ -258,8 +257,8 @@
     segment = wide >> (data_rows.bit_length() - 1)
     lane_row = wide & (SUB - 1)
     lane_slot = (wide >> 3) & (capacity - 1)
-    spill_slot = wide & (capacity - 1)
     spill_row = wide >> (capacity.bit_length() - 1)
+    spill_rows = [jnp.where(wide & (capacity - 1) == c, spill_row, owned) for c in range(capacity)]
     tile_weight = jnp.broadcast_to(weight, (SUB, cols))
 
     def warped(slot):
@@ -281,11 +280,11 @@
             past = start + SUB - owned
             tile = warped(slot)
             tiles_here.append(tile)
-            target = jnp.where(lane_slot == c, start + lane_row, target)
+            target = jnp.where(lane_slot == c, start, target)
             turned = pltpu.roll(tile, start & (SUB - 1), 0)
             next_spilled = next_spilled + jnp.where(sub < past, turned, 0.0)
-            next_over = jnp.where((spill_slot == c) & (spill_row < past), tile_weight, next_over)
-        meta = jnp.where(segment == 1, target.astype(jnp.float32), tile_weight)
+            next_over = jnp.where(spill_rows[c] < past, tile_weight, next_over)
+        meta = jnp.where(segment == 1, (target + lane_row).astype(jnp.float32), tile_weight)
         meta = jnp.where(segment == 0, over, meta)
         tail = jnp.where(sub == SUB - 1, meta, spilled * tile_weight)
         place = place_of(owner, owners)

time: 17.8 us -> 17.8 us (level)
  no operation moved by 1% of the time
where the time goes in v25:
time: 17.8 us; the launch traced here: 17.7 us
  blocking collectives  11.9 us (67%)
  Pallas kernels  4.49 us (25%)
  between operations  1.29 us (7%)
    all_to_all x1, blocking collectives, on_device(): lax.all_to_all(messages, 'sky', split_axis=0, concat_axis=0, axis_index_g...  11.9 us
    pallas_call x1, Pallas kernels, on_device(): pl.pallas_call(functools.partial(window_kernel, capacity), out_shape=pltp...  3.61 us
    pallas_call x1, Pallas kernels, on_device(): pl.pallas_call(functools.partial(sky_kernel, capacity), out_shape=(jax.Sh...  0.88 us

profile of v25, /device:TPU:1, one launch (start us, length us, event | category | flops | bytes accessed | tf_op | source)
XLA Modules:
  0.0 17.7 jit_solution(1300551012996259790)
XLA Ops:
  1.3 3.6 %match_warp_pack.1 = bf16[16,40,128]{2,1,0:T(8,128)(2,1)S(1)} custom-call(bf16[1,512,128]{2,1,0:T(8,128)(2,1)} %image_hbm.1, bf16[31,40]{1,0:T(8,128)(2,1)} %bitcast.5, bf16[31,40]{1,0:T(8,128)(2,1)} %bitcast.6, f32[3,1,40]{2,1,0:T(1,128)} %bitcast.7, bf16[1,4]{1,0:T(2,128)(2,1)} %bitcast.8, f32[1,2]{1,0:T(1,128)} %frac_hbm.1, s32[64]{0:T(128)} %block_hbm.1, ...), custom_call_target="tpu_custom_call" | custom-call | tf_op jit(solution)/shard_map/match_warp_pack/pallas_call | solution.py:366
  4.9 11.9 %all_to_all.5.got_ref = bf16[16,40,128]{2,1,0:T(8,128)(2,1)S(1)} all-to-all(bf16[16,40,128]{2,1,0:T(8,128)(2,1)S(1)} %match_warp_pack.1), channel_id=1, replica_groups={{10,11,8,9,14,15,12,13,2,3,0,1,6,7,4,5},{26,27,24,25,30,31,28,29,18,19,..., dimensions={0} | all-to-all | bytes 327680 | tf_op jit(solution)/shard_map/all_to_all | solution.py:412
  16.8 0.9 %place_normalise.1 = (f32[128,128]{1,0:T(8,128)}, f32[1,128]{1,0:T(1,128)}) custom-call(bf16[16,40,128]{2,1,0:T(8,128)(2,1)S(1)} %all_to_all.5.got_ref), custom_call_target="tpu_custom_call" | custom-call | tf_op jit(solution)/shard_map/place_normalise/pallas_call | solution.py:415

commit v26 on v25

--- a/solution.py
+++ b/solution.py
@@ -103,7 +103,7 @@
 def place_of(owner, owners):
     slow = 1 << ((owners.bit_length() - 1) // 2)
     fast = owners // slow
-    return (owner // fast + slow // 2) % slow * fast + (owner + fast // 2) % fast
+    return (owner // fast + slow // 2 + 1) % slow * fast + (owner + fast // 2) % fast
 
 
 def group_edges(fold):

time: 17.8 us -> 18.7 us (1.051)
  blocking collectives: 11.9 us -> 12.8 us
    all_to_all x1, blocking collectives: 11.9 us -> 12.8 us  [on_device(): lax.all_to_all(messages, 'sky', split_axis=0, concat_axis=0, axis_index_g...]
where the time goes in v26:
time: 18.7 us; the launch traced here: 18.6 us
  blocking collectives  12.8 us (68%)
  Pallas kernels  4.49 us (24%)
  between operations  1.29 us (7%)
    all_to_all x1, blocking collectives, on_device(): lax.all_to_all(messages, 'sky', split_axis=0, concat_axis=0, axis_index_g...  12.8 us
    pallas_call x1, Pallas kernels, on_device(): pl.pallas_call(functools.partial(window_kernel, capacity), out_shape=pltp...  3.62 us
    pallas_call x1, Pallas kernels, on_device(): pl.pallas_call(functools.partial(sky_kernel, capacity), out_shape=(jax.Sh...  0.88 us

profile of v26, /device:TPU:1, one launch (start us, length us, event | category | flops | bytes accessed | tf_op | source)
XLA Modules:
  0.0 18.6 jit_solution(16154602399562202916)
XLA Ops:
  1.3 3.6 %match_warp_pack.1 = bf16[16,40,128]{2,1,0:T(8,128)(2,1)S(1)} custom-call(bf16[1,512,128]{2,1,0:T(8,128)(2,1)} %image_hbm.1, bf16[31,40]{1,0:T(8,128)(2,1)} %bitcast.5, bf16[31,40]{1,0:T(8,128)(2,1)} %bitcast.6, f32[3,1,40]{2,1,0:T(1,128)} %bitcast.7, bf16[1,4]{1,0:T(2,128)(2,1)} %bitcast.8, f32[1,2]{1,0:T(1,128)} %frac_hbm.1, s32[64]{0:T(128)} %block_hbm.1, ...), custom_call_target="tpu_custom_call" | custom-call | tf_op jit(solution)/shard_map/match_warp_pack/pallas_call | solution.py:366
  4.9 12.8 %all_to_all.5.got_ref = bf16[16,40,128]{2,1,0:T(8,128)(2,1)S(1)} all-to-all(bf16[16,40,128]{2,1,0:T(8,128)(2,1)S(1)} %match_warp_pack.1), channel_id=1, replica_groups={{6,7,4,5,10,11,8,9,14,15,12,13,2,3,0,1},{22,23,20,21,26,27,24,25,30,31,..., dimensions={0} | all-to-all | bytes 327680 | tf_op jit(solution)/shard_map/all_to_all | solution.py:412
  17.7 0.9 %place_normalise.1 = (f32[128,128]{1,0:T(8,128)}, f32[1,128]{1,0:T(1,128)}) custom-call(bf16[16,40,128]{2,1,0:T(8,128)(2,1)S(1)} %all_to_all.5.got_ref), custom_call_target="tpu_custom_call" | custom-call | tf_op jit(solution)/shard_map/place_normalise/pallas_call | solution.py:415

commit v27 on v26

--- a/solution.py
+++ b/solution.py
@@ -103,7 +103,9 @@
 def place_of(owner, owners):
     slow = 1 << ((owners.bit_length() - 1) // 2)
     fast = owners // slow
-    return (owner // fast + slow // 2 + 1) % slow * fast + (owner + fast // 2) % fast
+    block = (owner // fast + slow // 2) % slow
+    pair = (owner % fast // 2 + fast // 4) % (fast // 2)
+    return (pair * slow + block) * 2 + owner % 2
 
 
 def group_edges(fold):

time: 18.7 us -> 18.9 us (1.011)
  the two profiles are of different devices: /device:TPU:1 before, /device:TPU:0 now
where the time goes in v27:
time: 18.9 us; the launch traced here: 18.7 us
  blocking collectives  12.9 us (68%)
  Pallas kernels  4.49 us (24%)
  between operations  1.29 us (7%)
    all_to_all x1, blocking collectives, on_device(): lax.all_to_all(messages, 'sky', split_axis=0, concat_axis=0, axis_index_g...  12.9 us
    pallas_call x1, Pallas kernels, on_device(): pl.pallas_call(functools.partial(window_kernel, capacity), out_shape=pltp...  3.62 us
    pallas_call x1, Pallas kernels, on_device(): pl.pallas_call(functools.partial(sky_kernel, capacity), out_shape=(jax.Sh...  0.88 us

profile of v27, /device:TPU:0, one launch (start us, length us, event | category | flops | bytes accessed | tf_op | source)
XLA Modules:
  0.0 18.7 jit_solution(4908007890728671621)
XLA Ops:
  1.3 3.6 %match_warp_pack.1 = bf16[16,40,128]{2,1,0:T(8,128)(2,1)S(1)} custom-call(bf16[1,512,128]{2,1,0:T(8,128)(2,1)} %image_hbm.1, bf16[31,40]{1,0:T(8,128)(2,1)} %bitcast.5, bf16[31,40]{1,0:T(8,128)(2,1)} %bitcast.6, f32[3,1,40]{2,1,0:T(1,128)} %bitcast.7, bf16[1,4]{1,0:T(2,128)(2,1)} %bitcast.8, f32[1,2]{1,0:T(1,128)} %frac_hbm.1, s32[64]{0:T(128)} %block_hbm.1, ...), custom_call_target="tpu_custom_call" | custom-call | tf_op jit(solution)/shard_map/match_warp_pack/pallas_call | solution.py:368
  4.9 12.9 %all_to_all.5.got_ref = bf16[16,40,128]{2,1,0:T(8,128)(2,1)S(1)} all-to-all(bf16[16,40,128]{2,1,0:T(8,128)(2,1)S(1)} %match_warp_pack.1), channel_id=1, replica_groups={{10,11,14,15,2,3,6,7,8,9,12,13,0,1,4,5},{26,27,30,31,18,19,22,23,24,25,..., dimensions={0} | all-to-all | bytes 327680 | tf_op jit(solution)/shard_map/all_to_all | solution.py:414
  17.9 0.9 %place_normalise.1 = (f32[128,128]{1,0:T(8,128)}, f32[1,128]{1,0:T(1,128)}) custom-call(bf16[16,40,128]{2,1,0:T(8,128)(2,1)S(1)} %all_to_all.5.got_ref), custom_call_target="tpu_custom_call" | custom-call | tf_op jit(solution)/shard_map/place_normalise/pallas_call | solution.py:417

commit v28 on v25

--- a/solution.py
+++ b/solution.py
@@ -107,7 +107,7 @@
 
 
 def group_edges(fold):
-    return [0, fold // 8, fold // 2, fold]
+    return [0, fold // 2, fold]
 
 
 def window_kernel(
@@ -186,6 +186,17 @@
     for copy in copies[1:4]:
         copy.wait()
     combined_taps(row_ref, col_ref, mix_ref, lifted, base)
+
+    edges = group_edges(fold)
+    groups = len(edges) - 1
+
+    def build(group, band):
+        for index, r in enumerate(range(edges[group], edges[group + 1])):
+            for part in range(2):
+                build_band(base, r + part * fold, band, (2 * index + part) * cols)
+
+    held = (band_a, band_b)
+    build(0, held[0])
     for copy in copies[:1] + copies[4:]:
         copy.wait()
     padded[fold : fold + rows] = image_ref[0].astype(jnp.float32)
@@ -196,14 +207,6 @@
         blocks[index * deep : (index + 1) * deep, :] = padded[
             pl.ds(index, deep, stride=fold), :
         ].astype(jnp.bfloat16)
-
-    edges = group_edges(fold)
-    groups = len(edges) - 1
-
-    def build(group, band):
-        for index, r in enumerate(range(edges[group], edges[group + 1])):
-            for part in range(2):
-                build_band(base, r + part * fold, band, (2 * index + part) * cols)
 
     def multiply(group, band):
         parts = []
@@ -227,8 +230,6 @@
         tile_of[slot] = tile
         starts[slot] = (block - owner * BLK_DEV) * SUB + offset_ref[tile]
 
-    held = (band_a, band_b)
-    build(0, held[0])
     for group in range(groups):
         if group + 1 < groups:
             build(group + 1, held[(group + 1) % 2])

time: 17.8 us -> 17.9 us (level)
  no operation moved by 1% of the time
where the time goes in v28:
time: 17.9 us; the launch traced here: 17.7 us
  blocking collectives  11.9 us (66%)
  Pallas kernels  4.53 us (25%)
  between operations  1.29 us (7%)
    all_to_all x1, blocking collectives, on_device(): lax.all_to_all(messages, 'sky', split_axis=0, concat_axis=0, axis_index_g...  11.9 us
    pallas_call x1, Pallas kernels, on_device(): pl.pallas_call(functools.partial(window_kernel, capacity), out_shape=pltp...  3.65 us
    pallas_call x1, Pallas kernels, on_device(): pl.pallas_call(functools.partial(sky_kernel, capacity), out_shape=(jax.Sh...  0.88 us

profile of v28, /device:TPU:1, one launch (start us, length us, event | category | flops | bytes accessed | tf_op | source)
XLA Modules:
  0.0 17.7 jit_solution(9888996182989273313)
XLA Ops:
  1.3 3.7 %match_warp_pack.1 = bf16[16,40,128]{2,1,0:T(8,128)(2,1)S(1)} custom-call(bf16[1,512,128]{2,1,0:T(8,128)(2,1)} %image_hbm.1, bf16[31,40]{1,0:T(8,128)(2,1)} %bitcast.5, bf16[31,40]{1,0:T(8,128)(2,1)} %bitcast.6, f32[3,1,40]{2,1,0:T(1,128)} %bitcast.7, bf16[1,4]{1,0:T(2,128)(2,1)} %bitcast.8, f32[1,2]{1,0:T(1,128)} %frac_hbm.1, s32[64]{0:T(128)} %block_hbm.1, ...), custom_call_target="tpu_custom_call" | custom-call | tf_op jit(solution)/shard_map/match_warp_pack/pallas_call | solution.py:367
  4.9 11.9 %all_to_all.5.got_ref = bf16[16,40,128]{2,1,0:T(8,128)(2,1)S(1)} all-to-all(bf16[16,40,128]{2,1,0:T(8,128)(2,1)S(1)} %match_warp_pack.1), channel_id=1, replica_groups={{10,11,8,9,14,15,12,13,2,3,0,1,6,7,4,5},{26,27,24,25,30,31,28,29,18,19,..., dimensions={0} | all-to-all | bytes 327680 | tf_op jit(solution)/shard_map/all_to_all | solution.py:413
  16.8 0.9 %place_normalise.1 = (f32[128,128]{1,0:T(8,128)}, f32[1,128]{1,0:T(1,128)}) custom-call(bf16[16,40,128]{2,1,0:T(8,128)(2,1)S(1)} %all_to_all.5.got_ref), custom_call_target="tpu_custom_call" | custom-call | tf_op jit(solution)/shard_map/place_normalise/pallas_call | solution.py:416

commit v29 on v28

--- a/solution.py
+++ b/solution.py
@@ -107,7 +107,7 @@
 
 
 def group_edges(fold):
-    return [0, fold // 2, fold]
+    return [0, fold // 8, fold // 2, fold]
 
 
 def window_kernel(

time: 17.9 us -> 17.9 us (level)
  no operation moved by 1% of the time
where the time goes in v29:
time: 17.9 us; the launch traced here: 17.7 us
  blocking collectives  11.9 us (66%)
  Pallas kernels  4.58 us (26%)
  between operations  1.29 us (7%)
    all_to_all x1, blocking collectives, on_device(): lax.all_to_all(messages, 'sky', split_axis=0, concat_axis=0, axis_index_g...  11.9 us
    pallas_call x1, Pallas kernels, on_device(): pl.pallas_call(functools.partial(window_kernel, capacity), out_shape=pltp...  3.7 us
    pallas_call x1, Pallas kernels, on_device(): pl.pallas_call(functools.partial(sky_kernel, capacity), out_shape=(jax.Sh...  0.88 us

profile of v29, /device:TPU:1, one launch (start us, length us, event | category | flops | bytes accessed | tf_op | source)
XLA Modules:
  0.0 17.7 jit_solution(3907654525796991628)
XLA Ops:
  1.3 3.7 %match_warp_pack.1 = bf16[16,40,128]{2,1,0:T(8,128)(2,1)S(1)} custom-call(bf16[1,512,128]{2,1,0:T(8,128)(2,1)} %image_hbm.1, bf16[31,40]{1,0:T(8,128)(2,1)} %bitcast.5, bf16[31,40]{1,0:T(8,128)(2,1)} %bitcast.6, f32[3,1,40]{2,1,0:T(1,128)} %bitcast.7, bf16[1,4]{1,0:T(2,128)(2,1)} %bitcast.8, f32[1,2]{1,0:T(1,128)} %frac_hbm.1, s32[64]{0:T(128)} %block_hbm.1, ...), custom_call_target="tpu_custom_call" | custom-call | tf_op jit(solution)/shard_map/match_warp_pack/pallas_call | solution.py:367
  5.0 11.9 %all_to_all.5.got_ref = bf16[16,40,128]{2,1,0:T(8,128)(2,1)S(1)} all-to-all(bf16[16,40,128]{2,1,0:T(8,128)(2,1)S(1)} %match_warp_pack.1), channel_id=1, replica_groups={{10,11,8,9,14,15,12,13,2,3,0,1,6,7,4,5},{26,27,24,25,30,31,28,29,18,19,..., dimensions={0} | all-to-all | bytes 327680 | tf_op jit(solution)/shard_map/all_to_all | solution.py:413
  16.9 0.9 %place_normalise.1 = (f32[128,128]{1,0:T(8,128)}, f32[1,128]{1,0:T(1,128)}) custom-call(bf16[16,40,128]{2,1,0:T(8,128)(2,1)S(1)} %all_to_all.5.got_ref), custom_call_target="tpu_custom_call" | custom-call | tf_op jit(solution)/shard_map/place_normalise/pallas_call | solution.py:416

commit v30 on v25

--- a/solution.py
+++ b/solution.py
@@ -152,10 +152,10 @@
     owned = BLK_DEV * SUB
 
     pairs = (
-        (image_hbm, image_ref),
         (row_hbm, row_ref),
         (col_hbm, col_ref),
         (mix_hbm, mix_ref),
+        (image_hbm, image_ref),
         (frac_hbm, frac_ref),
         (weight_hbm, weight_ref),
         (block_hbm, block_ref),
@@ -183,10 +183,10 @@
     padded[fold + rows :] = jnp.zeros((fold, cols), jnp.float32)
     spread[:SUB] = jnp.zeros((SUB, cols), jnp.float32)
     spread[SUB + rows :] = jnp.zeros((SUB, cols), jnp.float32)
-    for copy in copies[1:4]:
+    for copy in copies[:3]:
         copy.wait()
     combined_taps(row_ref, col_ref, mix_ref, lifted, base)
-    for copy in copies[:1] + copies[4:]:
+    for copy in copies[3:]:
         copy.wait()
     padded[fold : fold + rows] = image_ref[0].astype(jnp.float32)
     across, down = lanczos_rows(frac_ref, cols)
@@ -296,7 +296,7 @@
     lax.fori_loop(0, owners, message, (nothing, nothing), unroll=min(owners, 16))
 
 
-def sky_kernel(capacity, got_ref, coadd_ref, map_ref):
+def sky_kernel(capacity, got_ref, coadd_hbm, map_ref, coadd_ref, copied):
     sources, message_rows, cols = got_ref.shape
     data_rows = capacity * SUB
     owned = coadd_ref.shape[0]
@@ -337,9 +337,20 @@
     weight_sum = sums[:, cols:] + jnp.concatenate(
         [jnp.broadcast_to(over, (SUB, cols)), rest], axis=0
     )
-    coadd_ref[...] = pixel_sum / jnp.maximum(weight_sum, 1.0)
+    copies = []
+    for index in range(2):
+        part = slice(index * owned // 2, (index + 1) * owned // 2)
+        coadd_ref[part, :] = pixel_sum[part] / jnp.maximum(weight_sum[part], 1.0)
+        copies.append(
+            pltpu.make_async_copy(
+                coadd_ref.at[part, :], coadd_hbm.at[part, :], copied.at[index]
+            )
+        )
+        copies[-1].start()
     diagonal = jnp.where(row == iota((owned, cols), 1), weight_sum, 0.0)
     map_ref[...] = jnp.sum(diagonal, axis=0, keepdims=True)
+    for copy in copies:
+        copy.wait()
 
 
 def on_device(
@@ -419,7 +430,11 @@
             jax.ShapeDtypeStruct((1, BLK_DEV * SUB), jnp.float32),
         ),
         in_specs=[vmem],
-        out_specs=(vmem, vmem),
+        out_specs=(anywhere, vmem),
+        scratch_shapes=[
+            pltpu.VMEM((BLK_DEV * SUB, cols), jnp.float32),
+            pltpu.SemaphoreType.DMA((2,)),
+        ],
         compiler_params=pltpu.CompilerParams(vmem_limit_bytes=SMALL_VMEM),
         name="place_normalise",
     )(received)

time: 17.8 us -> 18.4 us (1.034)
  Pallas kernels: 4.49 us -> 4.94 us
    pallas_call x1, Pallas kernels: 0.88 us -> 1.39 us  [on_device(): pl.pallas_call(functools.partial(sky_kernel, capacity), out_shape=(jax.Sh...]
where the time goes in v30:
time: 18.4 us; the launch traced here: 18.1 us
  blocking collectives  11.9 us (65%)
  Pallas kernels  4.94 us (27%)
  between operations  1.29 us (7%)
    all_to_all x1, blocking collectives, on_device(): lax.all_to_all(messages, 'sky', split_axis=0, concat_axis=0, axis_index_g...  11.9 us
    pallas_call x1, Pallas kernels, on_device(): pl.pallas_call(functools.partial(window_kernel, capacity), out_shape=pltp...  3.55 us
    pallas_call x1, Pallas kernels, on_device(): pl.pallas_call(functools.partial(sky_kernel, capacity), out_shape=(jax.Sh...  1.39 us

profile of v30, /device:TPU:1, one launch (start us, length us, event | category | flops | bytes accessed | tf_op | source)
XLA Modules:
  0.0 18.1 jit_solution(16585401281303463396)
XLA Ops:
  1.3 3.6 %match_warp_pack.1 = bf16[16,40,128]{2,1,0:T(8,128)(2,1)S(1)} custom-call(bf16[1,512,128]{2,1,0:T(8,128)(2,1)} %image_hbm.1, bf16[31,40]{1,0:T(8,128)(2,1)} %bitcast.5, bf16[31,40]{1,0:T(8,128)(2,1)} %bitcast.6, f32[3,1,40]{2,1,0:T(1,128)} %bitcast.7, bf16[1,4]{1,0:T(2,128)(2,1)} %bitcast.8, f32[1,2]{1,0:T(1,128)} %frac_hbm.1, s32[64]{0:T(128)} %block_hbm.1, ...), custom_call_target="tpu_custom_call" | custom-call | tf_op jit(solution)/shard_map/match_warp_pack/pallas_call | solution.py:377
  4.8 11.9 %all_to_all.5.got_ref = bf16[16,40,128]{2,1,0:T(8,128)(2,1)S(1)} all-to-all(bf16[16,40,128]{2,1,0:T(8,128)(2,1)S(1)} %match_warp_pack.1), channel_id=1, replica_groups={{10,11,8,9,14,15,12,13,2,3,0,1,6,7,4,5},{26,27,24,25,30,31,28,29,18,19,..., dimensions={0} | all-to-all | bytes 327680 | tf_op jit(solution)/shard_map/all_to_all | solution.py:423
  16.7 1.4 %place_normalise.1 = (f32[128,128]{1,0:T(8,128)}, f32[1,128]{1,0:T(1,128)}) custom-call(bf16[16,40,128]{2,1,0:T(8,128)(2,1)S(1)} %all_to_all.5.got_ref), custom_call_target="tpu_custom_call" | custom-call | tf_op jit(solution)/shard_map/place_normalise/pallas_call | solution.py:426

commit v31 on v25

--- a/solution.py
+++ b/solution.py
@@ -152,10 +152,10 @@
     owned = BLK_DEV * SUB
 
     pairs = (
-        (image_hbm, image_ref),
         (row_hbm, row_ref),
         (col_hbm, col_ref),
         (mix_hbm, mix_ref),
+        (image_hbm, image_ref),
         (frac_hbm, frac_ref),
         (weight_hbm, weight_ref),
         (block_hbm, block_ref),
@@ -183,10 +183,10 @@
     padded[fold + rows :] = jnp.zeros((fold, cols), jnp.float32)
     spread[:SUB] = jnp.zeros((SUB, cols), jnp.float32)
     spread[SUB + rows :] = jnp.zeros((SUB, cols), jnp.float32)
-    for copy in copies[1:4]:
+    for copy in copies[:3]:
         copy.wait()
     combined_taps(row_ref, col_ref, mix_ref, lifted, base)
-    for copy in copies[:1] + copies[4:]:
+    for copy in copies[3:]:
         copy.wait()
     padded[fold : fold + rows] = image_ref[0].astype(jnp.float32)
     across, down = lanczos_rows(frac_ref, cols)

time: 17.8 us -> 17.8 us (level)
  no operation moved by 1% of the time
where the time goes in v31:
time: 17.8 us; the launch traced here: 17.6 us
  blocking collectives  11.9 us (67%)
  Pallas kernels  4.43 us (25%)
  between operations  1.29 us (7%)
    all_to_all x1, blocking collectives, on_device(): lax.all_to_all(messages, 'sky', split_axis=0, concat_axis=0, axis_index_g...  11.9 us
    pallas_call x1, Pallas kernels, on_device(): pl.pallas_call(functools.partial(window_kernel, capacity), out_shape=pltp...  3.55 us
    pallas_call x1, Pallas kernels, on_device(): pl.pallas_call(functools.partial(sky_kernel, capacity), out_shape=(jax.Sh...  0.88 us

profile of v31, /device:TPU:1, one launch (start us, length us, event | category | flops | bytes accessed | tf_op | source)
XLA Modules:
  0.0 17.6 jit_solution(14178593008068834849)
XLA Ops:
  1.3 3.6 %match_warp_pack.1 = bf16[16,40,128]{2,1,0:T(8,128)(2,1)S(1)} custom-call(bf16[1,512,128]{2,1,0:T(8,128)(2,1)} %image_hbm.1, bf16[31,40]{1,0:T(8,128)(2,1)} %bitcast.5, bf16[31,40]{1,0:T(8,128)(2,1)} %bitcast.6, f32[3,1,40]{2,1,0:T(1,128)} %bitcast.7, bf16[1,4]{1,0:T(2,128)(2,1)} %bitcast.8, f32[1,2]{1,0:T(1,128)} %frac_hbm.1, s32[64]{0:T(128)} %block_hbm.1, ...), custom_call_target="tpu_custom_call" | custom-call | tf_op jit(solution)/shard_map/match_warp_pack/pallas_call | solution.py:366
  4.8 11.9 %all_to_all.5.got_ref = bf16[16,40,128]{2,1,0:T(8,128)(2,1)S(1)} all-to-all(bf16[16,40,128]{2,1,0:T(8,128)(2,1)S(1)} %match_warp_pack.1), channel_id=1, replica_groups={{10,11,8,9,14,15,12,13,2,3,0,1,6,7,4,5},{26,27,24,25,30,31,28,29,18,19,..., dimensions={0} | all-to-all | bytes 327680 | tf_op jit(solution)/shard_map/all_to_all | solution.py:412
  16.7 0.9 %place_normalise.1 = (f32[128,128]{1,0:T(8,128)}, f32[1,128]{1,0:T(1,128)}) custom-call(bf16[16,40,128]{2,1,0:T(8,128)(2,1)S(1)} %all_to_all.5.got_ref), custom_call_target="tpu_custom_call" | custom-call | tf_op jit(solution)/shard_map/place_normalise/pallas_call | solution.py:415

commit v32 on v31

--- a/solution.py
+++ b/solution.py
@@ -107,7 +107,7 @@
 
 
 def group_edges(fold):
-    return [0, fold // 8, fold // 2, fold]
+    return [0, fold // 4, fold]
 
 
 def window_kernel(

time: 17.8 us -> 17.8 us (level)
  no operation moved by 1% of the time
where the time goes in v32:
time: 17.8 us; the launch traced here: 17.6 us
  blocking collectives  11.9 us (67%)
  Pallas kernels  4.42 us (25%)
  between operations  1.29 us (7%)
    all_to_all x1, blocking collectives, on_device(): lax.all_to_all(messages, 'sky', split_axis=0, concat_axis=0, axis_index_g...  11.9 us
    pallas_call x1, Pallas kernels, on_device(): pl.pallas_call(functools.partial(window_kernel, capacity), out_shape=pltp...  3.54 us
    pallas_call x1, Pallas kernels, on_device(): pl.pallas_call(functools.partial(sky_kernel, capacity), out_shape=(jax.Sh...  0.88 us

profile of v32, /device:TPU:1, one launch (start us, length us, event | category | flops | bytes accessed | tf_op | source)
XLA Modules:
  0.0 17.6 jit_solution(13901891563391699850)
XLA Ops:
  1.3 3.5 %match_warp_pack.1 = bf16[16,40,128]{2,1,0:T(8,128)(2,1)S(1)} custom-call(bf16[1,512,128]{2,1,0:T(8,128)(2,1)} %image_hbm.1, bf16[31,40]{1,0:T(8,128)(2,1)} %bitcast.5, bf16[31,40]{1,0:T(8,128)(2,1)} %bitcast.6, f32[3,1,40]{2,1,0:T(1,128)} %bitcast.7, bf16[1,4]{1,0:T(2,128)(2,1)} %bitcast.8, f32[1,2]{1,0:T(1,128)} %frac_hbm.1, s32[64]{0:T(128)} %block_hbm.1, ...), custom_call_target="tpu_custom_call" | custom-call | tf_op jit(solution)/shard_map/match_warp_pack/pallas_call | solution.py:366
  4.8 11.9 %all_to_all.5.got_ref = bf16[16,40,128]{2,1,0:T(8,128)(2,1)S(1)} all-to-all(bf16[16,40,128]{2,1,0:T(8,128)(2,1)S(1)} %match_warp_pack.1), channel_id=1, replica_groups={{10,11,8,9,14,15,12,13,2,3,0,1,6,7,4,5},{26,27,24,25,30,31,28,29,18,19,..., dimensions={0} | all-to-all | bytes 327680 | tf_op jit(solution)/shard_map/all_to_all | solution.py:412
  16.7 0.9 %place_normalise.1 = (f32[128,128]{1,0:T(8,128)}, f32[1,128]{1,0:T(1,128)}) custom-call(bf16[16,40,128]{2,1,0:T(8,128)(2,1)S(1)} %all_to_all.5.got_ref), custom_call_target="tpu_custom_call" | custom-call | tf_op jit(solution)/shard_map/place_normalise/pallas_call | solution.py:415
